TPU v7x, 32 devices: a whole 2x2x4 slice. The times are simulated.
32 devices in a mesh: depth: 4 (over x, core), height: 8 (over z, y).
Axes of the slice: x: 2, y: 2, z: 4, core: 2. Of those that a mesh axis runs over, the one named last changes fastest.
Arguments:
- fixed_image: float32 [32, 32, 128], P('depth', 'height'), as said below
- moving_image: float32 [32, 32, 128], P('depth', 'height'), as said below
- conv_one: float32 [64, 1, 3, 3, 3], replicated, may hold values from -1.25 to 1.25
- gain_one: float32 [64], replicated, may hold values from 0.1 to 1.9
- shift_one: float32 [64], replicated, may hold values from -3 to 3
- conv_two: bfloat16 [27, 4096], replicated, may hold values from -0.15625 to 0.15625
- gain_two: float32 [64], replicated, may hold values from 0.1 to 1.9
- shift_two: float32 [64], replicated, may hold values from -3 to 3
- sharpness: float32 [1], replicated, may hold values from 1 to 4
Outputs:
- displacement: float32 [3, 32, 32, 128], P(None, 'depth', 'height')
Inputs may be any that keep to these rules, and one draw needn't show every extreme that they name: `fixed_image`: intensities of a scan; the two scans show the same anatomy. `moving_image`: intensities of a scan; the two scans show the same anatomy.
All inputs are finite; a program needn't handle non-finite values.
Results may differ from a plain program's by a relative error of at most 0.0049.
Values may be sent and summed in bfloat16 or wider, within the bound.
No kernel may reach another device: no remote copies, remote signals or barrier semaphores. Data moves between devices by JAX's collectives and lax.ppermute only.
A program may use at most 64 MiB of HBM per device.

v0:
```python
import functools

import jax
import jax.numpy as jnp
import numpy as np
from jax import lax
from jax.experimental import pallas as pl
from jax.experimental.pallas import tpu as pltpu
from jax.sharding import PartitionSpec as P

RADIUS = 3
TILE = 8
F32 = jnp.float32
BF16 = jnp.bfloat16
FAR = -1e30
LOG2E = 1.4426950408889634
NUM = (((1,), (0,)), ((), ()))
AXES = ("depth", "height")


def leaky(v):
    return jnp.maximum(v, 0.01 * v)


def pair_table():
    axis_types = {}
    for k in range(3):
        for l in range(3):
            if k == l:
                axis_types[k, l] = {1: 0, 2: 1, 0: 2}[k]
            else:
                axis_types[k, l] = {1: 3, -1: 4, 2: 5, -2: 6}[l - k]
    table = np.zeros((729, 256), np.float32)
    taps = [(a, b, c) for a in range(3) for b in range(3) for c in range(3)]
    for i, k in enumerate(taps):
        for j, l in enumerate(taps):
            p, q = (k, l) if l[0] >= k[0] else (l, k)
            inner = axis_types[p[1], q[1]] * 7 + axis_types[p[2], q[2]]
            if p[0] != q[0]:
                table[i * 27 + j, (2 + q[0] - p[0]) * 49 + inner] += 1
            else:
                table[i * 27 + j, inner] += 1
                if p[0] == 2:
                    table[i * 27 + j, 49 + inner] -= 1
                if p[0] == 0:
                    table[i * 27 + j, 98 + inner] -= 1
    return table


def front_kernel(nd, nh, slab, strip, own_ref, other_ref, taps_ref, pairs_ref, two_ref, par_ref, place_ref,
                 mov_ref, fix_ref, sums_ref, img, bank_hi, bank_lo, gram, pieces, toep, plane_hi, plane_lo, feat_m, feat_f):
    zn, yn = nd * slab, nh * strip
    z0, y0, core = place_ref[0], place_ref[1], place_ref[4]
    count = float(zn * yn * 128)
    lane8 = lax.broadcasted_iota(jnp.int32, (8, 128), 1)
    sub8 = lax.broadcasted_iota(jnp.int32, (8, 128), 0)

    img[...] = jnp.zeros(img.shape, F32)
    for slot, src in enumerate((own_ref, other_ref)):
        scan = core if slot == 0 else 1 - core

        def gather(i, _):
            d, p = i // (nh // 2), i % (nh // 2)
            one = d * nh + 2 * p
            at = pl.multiple_of(8 + 8 * p, 8)
            for z in range(slab):
                both = jnp.concatenate([src[one, strip * z:strip * (z + 1)], src[one + 1, strip * z:strip * (z + 1)]], axis=0)
                img[scan, 5 + slab * d + z, pl.ds(at, 8), :] = both
            return _

        lax.fori_loop(0, nd * nh // 2, gather, 0)

    base = taps_ref[...]
    spot = lax.broadcasted_iota(jnp.int32, base.shape, 1)
    base_hi = base.astype(BF16).astype(F32)
    base = jnp.where((spot >= 144) & (spot < 288), (base - base_hi).astype(BF16).astype(F32), base_hi)
    for yo in range(12):
        toep[64 * yo:64 * yo + 64, :] = (pltpu.roll(base, yo, 1) if yo else base).astype(BF16)

    row_y = lax.broadcasted_iota(jnp.int32, (yn, 128), 0)
    step_rows = 256
    par_t = [jnp.broadcast_to(par_ref[i:i + 1, :], (128, 128)).T for i in range(2)]
    gain, shift = par_t[0][0:64], par_t[1][0:64]

    def statistics(scan):
        def build(z, _):
            at = pl.multiple_of(z * yn, yn)
            for ty in range(7):
                move = (0, 0, 0, 1, -1, 2, -2)[ty]
                v = img[scan, 5 + z, 8 + move:8 + move + yn, :]
                if ty == 1:
                    v = jnp.where(row_y == 0, 0.0, v)
                if ty == 2:
                    v = jnp.where(row_y == yn - 1, 0.0, v)
                hi = v.astype(BF16)
                bank_hi[pl.ds(at, yn), 128 * ty:128 * ty + 128] = hi
                bank_lo[pl.ds(at, yn), 128 * ty:128 * ty + 128] = (v - hi.astype(F32)).astype(BF16)
            return _

        lax.fori_loop(0, zn, build, 0)
        zero = jnp.zeros((2 * yn, 896), BF16)
        bank_hi[zn * yn:(zn + 2) * yn, :] = zero
        bank_lo[zn * yn:(zn + 2) * yn, :] = zero

        def product(at, length, far):
            a_hi = bank_hi[pl.ds(at, length), 0:128]
            a_lo = bank_lo[pl.ds(at, length), 0:128]
            b_hi = bank_hi[pl.ds(at + far, length), :]
            b_lo = bank_lo[pl.ds(at + far, length), :]
            left = jnp.concatenate([a_hi, a_hi, a_lo], axis=0)
            right = jnp.concatenate([b_hi, b_lo, b_hi], axis=0)
            return lax.dot_general(left, right, (((0,), (0,)), ((), ())), preferred_element_type=F32)

        gram[...] = jnp.zeros(gram.shape, F32)

        def chunk(i, _):
            at = pl.multiple_of(i * step_rows, step_rows)
            for far in range(3):
                gram[(0, 3, 4)[far]] += product(at, step_rows, far * yn)
            return _

        lax.fori_loop(0, zn * yn // step_rows, chunk, 0)
        gram[1] = product(0, yn, 0)
        gram[2] = product((zn - 1) * yn, yn, 0)

        def diagonals(tz, _):
            for ty in range(7):
                blk = gram[tz, :, 128 * ty:128 * ty + 128]
                halves = []
                for odd in range(2):
                    acc = jnp.zeros((8, 128), F32)
                    for m in range(8):
                        i = 2 * m + odd
                        acc = jnp.where((lane8 + 4 - 8 * odd) // 16 == m, blk[8 * i:8 * i + 8], acc)
                    halves.append(acc)
                for tx in range(7):
                    move = (0, 0, 0, 1, -1, 2, -2)[tx]
                    total = jnp.zeros((8, 128), F32)
                    for odd in range(2):
                        hit = (lane8 - sub8 - move - 8 * odd + 16) % 16 == 0
                        total = total + jnp.where(hit, halves[odd], 0.0)
                    if tx == 1:
                        total = jnp.where(lane8 == 0, 0.0, total)
                    if tx == 2:
                        total = jnp.where(lane8 == 127, 0.0, total)
                    pieces[pl.ds(pl.multiple_of(tz * 392 + (ty * 7 + tx) * 8, 8), 8), :] = total
            return _

        lax.fori_loop(0, 5, diagonals, 0)

        def add(z, total):
            return total + img[scan, 5 + z, 8:8 + yn, :]

        whole = lax.fori_loop(0, zn, add, jnp.zeros((yn, 128), F32))
        first, last = img[scan, 5, 8:8 + yn, :], img[scan, 4 + zn, 8:8 + yn, :]
        for kz in range(3):
            plane = (whole - last, whole, whole - first)[kz]
            for ky in range(3):
                v = plane
                if ky == 0:
                    v = jnp.where(row_y == yn - 1, 0.0, v)
                if ky == 2:
                    v = jnp.where(row_y == 0, 0.0, v)
                v = jnp.sum(v.reshape(yn // 8, 8, 128), axis=0)
                for kx in range(3):
                    w = v
                    if kx == 0:
                        w = jnp.where(lane8 == 127, 0.0, w)
                    if kx == 2:
                        w = jnp.where(lane8 == 0, 0.0, w)
                    at = 2048 + (kz * 9 + ky * 3 + kx) * 8
                    pieces[at:at + 8, :] = w
        pieces[1960:2048, :] = jnp.zeros((88, 128), F32)
        pieces[2264:2304, :] = jnp.zeros((40, 128), F32)
        rows = pieces[pl.ds(0, 288, stride=8), :]
        for s in range(1, 8):
            rows = rows + pieces[pl.ds(s, 288, stride=8), :]
        second = lax.dot_general(pairs_ref[:, 0:256], rows[0:256], NUM, precision=lax.Precision.HIGHEST, preferred_element_type=F32)
        mean = lax.dot_general(pairs_ref[:, 256:288], rows[256:288], NUM, precision=lax.Precision.HIGHEST, preferred_element_type=F32)
        mean = jnp.sum(mean, axis=1, keepdims=True) / count
        second = jnp.sum(second, axis=1, keepdims=True) / count
        scale = lax.rsqrt(second - mean * mean + 1e-05) * gain
        return scale, shift - mean * scale

    lane = lax.broadcasted_iota(jnp.int32, (16, 128), 1)
    lane64 = lax.broadcasted_iota(jnp.int32, (64, 128), 1)
    half = (y0 // strip) % 2

    def encode(scan, planes, rows, near, feat, out):
        scale, offset = statistics(scan)
        low = pl.multiple_of((y0 // 8) * 8, 8)

        def load(i, _):
            v = img[scan, z0 + 5 - near - 1 + i, pl.ds(low, 24), :]
            v = pltpu.roll(v, 24 - (8 - near - 1) - 4 * half, 0)[0:16]
            before = jnp.where(lane == 0, 0.0, pltpu.roll(v, 1, 1))
            after = jnp.where(lane == 127, 0.0, pltpu.roll(v, 127, 1))
            v = jnp.concatenate([before, v, after], axis=0)
            hi = v.astype(BF16)
            plane_hi[i] = hi
            plane_lo[i] = (v - hi.astype(F32)).astype(BF16)
            return _

        lax.fori_loop(0, planes + 2, load, 0)

        def first(i, _):
            sides = []
            for u in range(2):
                hi = plane_hi[pl.ds(2 * i + u, 3)].reshape(144, 128)
                lo = plane_lo[pl.ds(2 * i + u, 3)].reshape(144, 128)
                sides.append(jnp.concatenate([hi, hi, lo, jnp.zeros((80, 128), BF16)], axis=0))
            raw = jnp.dot(toep[0:64 * rows, :], jnp.concatenate(sides, axis=1), preferred_element_type=F32)
            for u in range(2):
                z = z0 - near + 2 * i + u
                for yo in range(rows):
                    y = y0 - near + yo
                    v = leaky(raw[64 * yo:64 * yo + 64, 128 * u:128 * u + 128] * scale + offset)
                    v = jnp.where((z >= 0) & (z < zn) & (y >= 0) & (y < yn), v, 0.0)
                    feat[2 * i + u, :, 128 * yo:128 * yo + 128] = v.astype(BF16)
            return _

        lax.fori_loop(0, planes // 2, first, 0)
        wide = rows - 2
        rim = near - 1

        def second(z, state):
            total, square = state
            taps = [feat[z + a, :, 128 * b:128 * (b + wide)] for a in range(3) for b in range(3)]
            raw = jnp.dot(two_ref[...], jnp.concatenate(taps, axis=0), preferred_element_type=F32)
            mine = jnp.where((z >= rim) & (z < rim + slab), 1.0, 0.0)
            for y in range(wide):
                cut = slice(128 * y, 128 * y + 128)
                before = jnp.where(lane64 == 0, 0.0, pltpu.roll(raw[0:64, cut], 1, 1))
                after = jnp.where(lane64 == 127, 0.0, pltpu.roll(raw[128:192, cut], 127, 1))
                v = before + raw[64:128, cut] + after
                out[z, :, cut] = v
                if rim <= y < rim + strip:
                    total = total + v * mine
                    square = square + v * v * mine
            return total, square

        return lax.fori_loop(0, planes - 2, second, (jnp.zeros((64, 128), F32), jnp.zeros((64, 128), F32)))

    f_sum, f_square = encode(0, slab + 2, strip + 2, 1, feat_f, fix_ref)
    m_sum, m_square = encode(1, slab + 8, strip + 8, 4, feat_m, mov_ref)
    sums_ref[0:1, :] = jnp.sum(jnp.concatenate([f_sum, m_sum], axis=0).T, axis=0, keepdims=True)
    sums_ref[1:2, :] = jnp.sum(jnp.concatenate([f_square, m_square], axis=0).T, axis=0, keepdims=True)


def front(own, other, taps, pairs, two, par, place, nd, nh, slab, strip):
    zn, yn = nd * slab, nh * strip
    vm = pl.BlockSpec(memory_space=pltpu.VMEM)
    sm = pl.BlockSpec(memory_space=pltpu.SMEM)
    return pl.pallas_call(
        functools.partial(front_kernel, nd, nh, slab, strip),
        out_shape=(
            jax.ShapeDtypeStruct((slab + 6, 64, (strip + 6) * 128), F32),
            jax.ShapeDtypeStruct((slab, 64, strip * 128), F32),
            jax.ShapeDtypeStruct((2, 128), F32),
        ),
        in_specs=[vm] * 6 + [sm],
        out_specs=(vm, vm, vm),
        scratch_shapes=[
            pltpu.VMEM((2, zn + 10, yn + 24, 128), F32),
            pltpu.VMEM(((zn + 2) * yn, 896), BF16),
            pltpu.VMEM(((zn + 2) * yn, 896), BF16),
            pltpu.VMEM((5, 128, 896), F32),
            pltpu.VMEM((2304, 128), F32),
            pltpu.VMEM((768, 512), BF16),
            pltpu.VMEM((slab + 10, 48, 128), BF16),
            pltpu.VMEM((slab + 10, 48, 128), BF16),
            pltpu.VMEM((slab + 8, 64, (strip + 8) * 128), BF16),
            pltpu.VMEM((slab + 2, 64, (strip + 2) * 128), BF16),
        ],
        compiler_params=pltpu.CompilerParams(vmem_limit_bytes=56 * 1024 * 1024),
        name="front",
    )(own, other, taps, pairs, two, par, place)


def parameters(conv_one, gain_one, shift_one, conv_two, gain_two, shift_two):
    w = conv_one.reshape(64, 3, 3, 3)
    base = jnp.pad(jnp.transpose(w, (0, 1, 3, 2)), ((0, 0), (0, 0), (0, 0), (0, 13))).reshape(64, 144)
    base = jnp.concatenate([base, base, base, jnp.zeros((64, 80), F32)], axis=1)
    flat = conv_one.reshape(64, 27)
    products = (flat[:, :, None] * flat[:, None, :]).reshape(64, 729)
    quad = jnp.dot(products, pair_table(), precision=lax.Precision.HIGHEST)
    pairs = jnp.concatenate([quad, flat, jnp.zeros((64, 5), F32)], axis=1)
    two = conv_two.reshape(3, 3, 3, 64, 64).transpose(2, 4, 0, 1, 3).reshape(192, 576)
    par = jnp.stack([jnp.concatenate([v, v]) for v in (gain_one, shift_one, gain_two, shift_two)])
    return base, pairs, two, par


def block_swap(rows):
    rows = list(rows)
    lane = lax.broadcasted_iota(jnp.int32, rows[0].shape, 1)
    for bit in range(4):
        step = 1 << bit
        low = (lane // (TILE * step)) % 2 == 0
        for q in range(16):
            if q & step:
                continue
            a, c = rows[q], rows[q + step]
            rows[q] = jnp.where(low, a, pltpu.roll(c, TILE * step, 1))
            rows[q + step] = jnp.where(low, pltpu.roll(a, 128 - TILE * step, 1), c)
    return rows


def match_kernel(slab, strip, mov_ref, fix_ref, sums_ref, par_ref, place_ref, sharp_ref, out_ref, even, odd, fixed, score, found):
    ch = fix_ref.shape[1]
    tall, wide = slab + 2 * RADIUS, strip + 2 * RADIUS
    groups = slab // 4
    span = 4 + 2 * RADIUS
    z0, y0 = place_ref[0], place_ref[1]
    zn, yn = place_ref[2], place_ref[3]

    sums = jnp.sum(sums_ref[...], axis=0) / (zn * yn * 128).astype(F32)
    mean, square = sums[0:1], sums[1:2]
    scale = lax.rsqrt(square - mean * mean + 1e-05) * par_ref[2:3]
    offset = par_ref[3:4] - mean * scale
    scale = jnp.broadcast_to(scale, (128, 128)).T
    offset = jnp.broadcast_to(offset, (128, 128)).T

    def feature(raw, scan):
        v = raw * scale[64 * scan:64 * scan + 64] + offset[64 * scan:64 * scan + 64]
        return leaky(v).astype(BF16).astype(F32)

    row = lax.broadcasted_iota(jnp.int32, (128, 128), 0)
    col = lax.broadcasted_iota(jnp.int32, (128, 128), 1)
    onehot_x = jnp.where(col == 64 + row % 16, 1.0, 0.0)
    sub = lax.broadcasted_iota(jnp.int32, (64, 128), 0)

    def plane(z, _):
        for y in range(wide):
            f = feature(mov_ref[z, :, y * 128:(y + 1) * 128], 1)
            zz, yy = z0 + z - RADIUS, y0 + y - RADIUS
            inside = (zz >= 0) & (zz < zn) & (yy >= 0) & (yy < yn)
            f = jnp.where(inside, f, 0.0)
            norm = jnp.sum(f * f, axis=0, keepdims=True)
            hi = norm.astype(BF16).astype(F32)
            mid = (norm - hi).astype(BF16).astype(F32)
            low = norm - hi - mid
            extra = jnp.where(sub == 48, hi, jnp.where(sub == 49, mid, jnp.where(sub == 50, low, 0.0)))
            t = jnp.concatenate([f, extra], axis=0).T
            ones = jnp.where((col == 64 + 16 + y) | (col == 64 + 32 + z), 1.0, onehot_x)
            even[z, y] = (jnp.where(row >= 4, pltpu.roll(t, 4, 0), 0.0) + ones).astype(BF16)
            odd[z, y] = (jnp.where(row < 124, pltpu.roll(t, 124, 0), 0.0) + ones).astype(BF16)
        return _

    lax.fori_loop(0, tall, plane, 0)

    k = lax.broadcasted_iota(jnp.int32, (64, 128 * groups), 0)
    lane = lax.broadcasted_iota(jnp.int32, (64, 128 * groups), 1)
    fx, fy, fz = lane % 8, (lane // 8) % 4, lane // 32
    span_x = jnp.abs(k - fx - 4)
    span_y = jnp.abs(k - 16 - fy - 3)
    span_z = jnp.abs(k - 32 - fz - 3)
    apart = jnp.where(k < 16, span_x, jnp.where(k < 32, span_y, jnp.where(k < 48, span_z, 0)))
    tail = jnp.where(apart > RADIUS, FAR, 0.0)
    tail = jnp.where((k >= 48) & (k < 51), -0.5, tail).astype(BF16)
    for j in range(16):
        fixed[j, 64:128, :] = tail
    for g in range(groups):
        for part in range(ch // 16):
            rows = []
            for q in range(16):
                raw = fix_ref[4 * g + q // 4, part * 16:(part + 1) * 16, (q % 4) * 128:(q % 4 + 1) * 128]
                at = slice(part * 16, part * 16 + 16)
                rows.append(leaky(raw * scale[at] + offset[at]).astype(BF16).astype(F32))
            for j, v in enumerate(block_swap(rows)):
                fixed[j, part * 16:(part + 1) * 16, g * 128:(g + 1) * 128] = v.astype(BF16)

    factor = sharp_ref[0] * (2.0 * LOG2E / ch)
    count = wide * 16
    lane1 = lax.broadcasted_iota(jnp.int32, (1, 128), 1)
    x_in, y_in, z_in = lane1 % 8, (lane1 // 8) % 4, lane1 // 32
    pos = lax.broadcasted_iota(jnp.int32, (16, 128), 0).astype(F32)

    def tiles(m, _):
        for parity, held in enumerate((even, odd)):
            j = 2 * m + parity
            weights = fixed[j]
            peak = [jnp.full((8, 128), -3e38, F32) for _g in range(groups)]
            for z in range(tall):
                items = held[z, :, pl.ds(pl.multiple_of(16 * m, 16), 16), :].reshape(count, 128)
                users = [g for g in range(groups) if 4 * g <= z < 4 * g + span]
                s = jnp.dot(items, weights[:, users[0] * 128:(users[-1] + 1) * 128], preferred_element_type=F32)
                for i, g in enumerate(users):
                    part = s[:, i * 128:(i + 1) * 128]
                    score[g, z - 4 * g] = part
                    peak[g] = jnp.maximum(peak[g], jnp.max(part.reshape(count // 8, 8, 128), axis=0))
            for g in range(groups):
                top = jnp.max(peak[g], axis=0, keepdims=True) * factor
                run = jnp.zeros((count, 128), F32)
                acc = jnp.zeros((count, 128), F32)
                for z in range(span - 1, -1, -1):
                    run = run + jnp.exp2(score[g, z] * factor - top)
                    if z:
                        acc = acc + run
                acc_z = jnp.sum(acc, axis=0, keepdims=True)
                by_y = run.reshape(wide, 16, 128)
                by_x = jnp.sum(by_y, axis=0)
                total = jnp.sum(by_x, axis=0, keepdims=True)
                acc_x = jnp.sum(by_x * pos, axis=0, keepdims=True)
                acc_y = jnp.zeros((8, 128), F32)
                part_run = jnp.zeros((8, 128), F32)
                for y in range(wide - 1, 0, -1):
                    part_run = part_run + by_y[y, 0:8] + by_y[y, 8:16]
                    acc_y = acc_y + part_run
                acc_y = jnp.sum(acc_y, axis=0, keepdims=True)
                inv = 1.0 / total
                dz = acc_z * inv - (z_in + RADIUS).astype(F32)
                dy = acc_y * inv - (y_in + RADIUS).astype(F32)
                dx = acc_x * inv - (x_in + 4).astype(F32)
                found[g, j] = jnp.concatenate([dz, dy, dx, jnp.zeros((5, 128), F32)], axis=0)
        return _

    lax.fori_loop(0, 8, tiles, 0)
    for g in range(groups):
        for q, v in enumerate(block_swap([found[g, j] for j in range(16)])):
            for comp in range(3):
                out_ref[comp, 4 * g + q // 4, pl.ds(q % 4, 1), :] = v[comp:comp + 1]


def match(moving, fixed, sums, par, place, sharpness, slab, strip):
    tall, wide = slab + 2 * RADIUS, strip + 2 * RADIUS
    groups = slab // 4
    vm = pl.BlockSpec(memory_space=pltpu.VMEM)
    sm = pl.BlockSpec(memory_space=pltpu.SMEM)
    return pl.pallas_call(
        functools.partial(match_kernel, slab, strip),
        out_shape=jax.ShapeDtypeStruct((3, slab, strip, 128), F32),
        in_specs=[vm, vm, vm, vm, sm, sm],
        out_specs=vm,
        scratch_shapes=[
            pltpu.VMEM((tall, wide, 128, 128), BF16),
            pltpu.VMEM((tall, wide, 128, 128), BF16),
            pltpu.VMEM((16, 128, 128 * groups), BF16),
            pltpu.VMEM((groups, 4 + 2 * RADIUS, wide * 16, 128), F32),
            pltpu.VMEM((groups, 16, 8, 128), F32),
        ],
        compiler_params=pltpu.CompilerParams(vmem_limit_bytes=48 * 1024 * 1024),
        name="match",
    )(moving, fixed, sums, par, place, sharpness)


def exchange(fixed_image, moving_image):
    depth, height = lax.axis_size("depth"), lax.axis_size("height")
    slab, strip, width = fixed_image.shape
    both = jnp.stack([fixed_image, moving_image]).reshape(2, slab * strip, width)
    sent = jnp.broadcast_to(both[None, :, None], (depth // 2, 2, height) + both.shape[1:])
    own = lax.all_to_all(sent.reshape((depth * height,) + both.shape[1:]), AXES, 0, 0)
    other = lax.ppermute(own, "depth", [(i, i ^ 1) for i in range(depth)])
    return own, other


def local(fixed_image, moving_image, conv_one, gain_one, shift_one, conv_two, gain_two, shift_two, sharpness):
    depth, height = lax.axis_size("depth"), lax.axis_size("height")
    slab, strip, _ = fixed_image.shape
    own, other = exchange(fixed_image, moving_image)
    base, pairs, two, par = parameters(conv_one, gain_one, shift_one, conv_two, gain_two, shift_two)
    row, column = lax.axis_index("depth"), lax.axis_index("height")
    place = jnp.stack([row * slab, column * strip, slab * depth, strip * height, row % 2]).astype(jnp.int32)
    moving, fixed, sums = front(own, other, base, pairs, two, par, place, depth, height, slab, strip)
    sent = jnp.broadcast_to(sums[None], (depth * height,) + sums.shape)
    sums = lax.all_to_all(sent, AXES, 0, 0)
    return match(moving, fixed, sums, par, place, sharpness, slab, strip)


def solution(mesh):
    image = P("depth", "height", None)
    return jax.shard_map(
        local,
        mesh=mesh,
        in_specs=(image, image) + (P(),) * 7,
        out_specs=P(None, "depth", "height", None),
        check_vma=False,
    )
```

profile of v0, /device:TPU:0, one launch (start us, length us, event | category | flops | bytes accessed | tf_op | source)
XLA Modules:
  0.0 95.1 jit_solution(15980016215419904340)
XLA Ops:
  0.0 0.0 copy-start.5
  0.0 0.0 copy-start.7
  0.0 0.0 copy-start.8
  0.0 0.0 copy-start.9
  0.0 0.0 copy-start.10
  0.0 0.8 maximum_bitcast_fusion
  0.8 0.9 broadcast_in_dim.20
  1.7 7.3 %all-to-all-start = ((f32[32,32,128]{2,1,0:T(8,128)}), f32[32,32,128]{2,1,0:T(8,128)S(1)}, u32[]{:S(2)}, u32[]{:S(2)}) async-start(f32[32,32,128]{2,1,0:T(8,128)} %bitcast.3), calls=%async_computation | async-start | bytes 1048576 | tf_op jit(solution)/shard_map/all_to_all | solution.py:451
  9.0 0.7 copy.25
  9.7 0.8 reduce
  10.5 0.1 copy.18
  10.7 1.4 %reshape.30 = bf16[3,3,3,64,64]{4,3,2,1,0:T(8,128)(2,1)S(1)} reshape(bf16[27,4096]{1,0:T(8,128)(2,1)} %param.15) | data formatting | bytes 442368 | tf_op jit(solution)/shard_map/reshape | solution.py:288
  12.1 0.8 copy.19
  12.9 1.1 %reshape.31.two_ref = bf16[192,576]{1,0:T(8,128)(2,1)} reshape(bf16[3,64,3,3,64]{4,3,2,1,0:T(4,128)(2,1)S(1)} %bitcast.30) | data formatting | bytes 442368 | tf_op jit(solution)/shard_map/reshape | solution.py:288
  14.0 0.1 copy.15
  14.1 0.1 pad.23.clone
  14.2 0.1 pad.27.clone
  14.3 0.0 copy-done.7
  14.3 0.0 copy-done.8
  14.3 0.1 maximum_bitcast_fusion.1
  14.4 0.0 copy-done.9
  14.4 0.0 copy-done.10
  14.4 0.1 maximum_bitcast_fusion.3
  14.5 0.6 pad_maximum_fusion.par_ref
  15.0 0.0 copy-done.5
  15.0 0.8 fusion
  15.9 9.5 %all-to-all-done.own_ref = f32[32,32,128]{2,1,0:T(8,128)S(1)} async-done(((f32[32,32,128]{2,1,0:T(8,128)}), f32[32,32,128]{2,1,0:T(8,128)S(1)}, u32[]{:S(2)}, u32[]{:S(2)}) %all-to-all-start) | async-done | bytes 524320 | tf_op jit(solution)/shard_map/all_to_all | solution.py:451
  25.3 0.0 copy-start.4
  25.3 0.0 collective-permute-start
  25.4 0.7 pad_add_fusion.place_ref
  26.1 0.6 maximum_maximum_fusion.1.pairs_ref
  26.7 0.8 maximum_maximum_fusion.taps_ref
  27.5 0.0 collective-permute-done.other_ref
  27.5 0.0 copy-done.4
  27.5 0.0 copy-start.6
  27.5 0.8 copy-done.6
  28.3 34.3 %front.1 = (f32[14,64,1280]{2,1,0:T(8,128)}, f32[8,64,512]{2,1,0:T(8,128)}, f32[2,128]{1,0:T(2,128)}) custom-call(f32[32,32,128]{2,1,0:T(8,128)} %copy-done.4, f32[32,32,128]{2,1,0:T(8,128)} %copy-done.6, f32[64,512]{1,0:T(8,128)} %maximum_maximum_fusion.taps_ref, f32[64,288]{1,0:T(8,128)} %maximum_maximum_fusion.1.pairs_ref, ...), custom_call_target="tpu_custom_call" | custom-call | tf_op jit(solution)/shard_map/front/pallas_call | solution.py:254
  62.6 1.3 %broadcast_in_dim.23 = f32[32,2,128]{2,1,0:T(2,128)} broadcast(f32[2,128]{1,0:T(2,128)} %get-tuple-element.10), dimensions={1,2} | broadcast | bytes 33792 | tf_op jit(solution)/shard_map/broadcast_in_dim | solution.py:464
  63.9 2.6 %all-to-all-start.1 = ((f32[32,2,128]{2,1,0:T(2,128)}), f32[32,2,128]{2,1,0:T(2,128)S(1)}, u32[]{:S(2)}, u32[]{:S(2)}) async-start(f32[32,2,128]{2,1,0:T(2,128)} %broadcast_in_dim.23), calls=%async_computation.1 | async-start | bytes 65536 | tf_op jit(solution)/shard_map/all_to_all | solution.py:465
  67.1 6.5 %all-to-all-done.1.sums_ref = f32[32,2,128]{2,1,0:T(2,128)S(1)} async-done(((f32[32,2,128]{2,1,0:T(2,128)}), f32[32,2,128]{2,1,0:T(2,128)S(1)}, u32[]{:S(2)}, u32[]{:S(2)}) %all-to-all-start.1) | async-done | bytes 32800 | tf_op jit(solution)/shard_map/all_to_all | solution.py:465
  73.6 0.0 copy-start
  73.6 2.3 %copy-done = f32[14,64,1280]{2,1,0:T(8,128)S(1)} copy-done((f32[14,64,1280]{2,1,0:T(8,128)S(1)}, f32[14,64,1280]{2,1,0:T(8,128)}, u32[]{:S(2)}) %copy-start) | copy-done | bytes 4587544
  75.9 0.0 copy-start.1
  75.9 1.2 %copy-done.1 = f32[8,64,512]{2,1,0:T(8,128)S(1)} copy-done((f32[8,64,512]{2,1,0:T(8,128)S(1)}, f32[8,64,512]{2,1,0:T(8,128)}, u32[]{:S(2)}) %copy-start.1) | copy-done | bytes 1048600
  77.2 0.0 copy-start.2
  77.2 0.7 copy-done.2
  77.8 0.0 copy-start.3
  77.8 0.7 copy-done.3
  78.5 16.7 %match.1 = f32[3,8,4,128]{3,2,1,0:T(4,128)} custom-call(f32[14,64,1280]{2,1,0:T(8,128)S(1)} %copy-done, f32[8,64,512]{2,1,0:T(8,128)S(1)} %copy-done.1, f32[32,2,128]{2,1,0:T(2,128)S(1)} %all-to-all-done.1.sums_ref, f32[4,128]{1,0:T(4,128)S(1)} %copy-done.2, s32[5]{0:T(128)S(1)} %copy-done.3, f32[1]{0:T(128)S(6)} %copy.26.sharp_ref), custom_call_target="tpu_custom_call" | custom-call | tf_op jit(solution)/shard_map/match/pallas_call | solution.py:429
  (7 shorter events, 0.1 us)
Async XLA Ops:
  0.0 15.0 %copy-start.5 = (f32[729,256]{1,0:T(8,128)S(1)}, f32[729,256]{1,0:T(8,128)}, u32[]{:S(2)}) copy-start(f32[729,256]{1,0:T(8,128)} %constant.34.clone) | copy-start | bytes 2239492
  0.0 14.3 %copy-start.7 = (f32[64]{0:T(128)S(1)}, f32[64]{0:T(128)}, u32[]{:S(2)}) copy-start(f32[64]{0:T(128)} %param.13) | copy-start | bytes 772
  0.0 14.3 %copy-start.8 = (f32[64]{0:T(128)S(1)}, f32[64]{0:T(128)}, u32[]{:S(2)}) copy-start(f32[64]{0:T(128)} %param.14) | copy-start | bytes 772
  0.0 14.4 %copy-start.9 = (f32[64]{0:T(128)S(1)}, f32[64]{0:T(128)}, u32[]{:S(2)}) copy-start(f32[64]{0:T(128)} %param.16) | copy-start | bytes 772
  0.0 14.4 %copy-start.10 = (f32[64]{0:T(128)S(1)}, f32[64]{0:T(128)}, u32[]{:S(2)}) copy-start(f32[64]{0:T(128)} %param.17) | copy-start | bytes 772
  1.7 23.7 %all-to-all-start = ((f32[32,32,128]{2,1,0:T(8,128)}), f32[32,32,128]{2,1,0:T(8,128)S(1)}, u32[]{:S(2)}, u32[]{:S(2)}) async-start(f32[32,32,128]{2,1,0:T(8,128)} %bitcast.3), calls=%async_computation | async-start | bytes 1048576 | tf_op jit(solution)/shard_map/all_to_all | solution.py:451
  25.3 2.2 %copy-start.4 = (f32[32,32,128]{2,1,0:T(8,128)}, f32[32,32,128]{2,1,0:T(8,128)S(1)}, u32[]{:S(2)}) copy-start(f32[32,32,128]{2,1,0:T(8,128)S(1)} %all-to-all-done.own_ref) | copy-start | bytes 1572868
  25.3 2.2 %collective-permute-start = (f32[32,32,128]{2,1,0:T(8,128)S(1)}, f32[32,32,128]{2,1,0:T(8,128)S(1)}, u32[]{:S(2)}, u32[]{:S(2)}) collective-permute-start(f32[32,32,128]{2,1,0:T(8,128)S(1)} %all-to-all-done.own_ref), channel_id=1, source_target_pairs={{0,8},{8,0},{16,24},{24,16},{1,9},{9,1},{17,25},{25,17},{2,10},{10... | collective-permute-start | bytes 1572872 | tf_op jit(solution)/shard_map/ppermute | solution.py:452
  27.5 0.8 copy-start.6
  63.9 9.8 %all-to-all-start.1 = ((f32[32,2,128]{2,1,0:T(2,128)}), f32[32,2,128]{2,1,0:T(2,128)S(1)}, u32[]{:S(2)}, u32[]{:S(2)}) async-start(f32[32,2,128]{2,1,0:T(2,128)} %broadcast_in_dim.23), calls=%async_computation.1 | async-start | bytes 65536 | tf_op jit(solution)/shard_map/all_to_all | solution.py:465
  73.6 2.3 %copy-start = (f32[14,64,1280]{2,1,0:T(8,128)S(1)}, f32[14,64,1280]{2,1,0:T(8,128)}, u32[]{:S(2)}) copy-start(f32[14,64,1280]{2,1,0:T(8,128)} %get-tuple-element.8.mov_ref) | copy-start | bytes 13762564
  75.9 1.2 %copy-start.1 = (f32[8,64,512]{2,1,0:T(8,128)S(1)}, f32[8,64,512]{2,1,0:T(8,128)}, u32[]{:S(2)}) copy-start(f32[8,64,512]{2,1,0:T(8,128)} %get-tuple-element.9.fix_ref) | copy-start | bytes 3145732
  77.2 0.7 copy-start.2
  77.8 0.7 copy-start.3
where the time goes:
time: 95.7 us; the launch traced here: 95.1 us
  Pallas kernels  50.9 us (53%)
  waiting for transfers between devices  16 us (17%)
  local copies, waits for them, and re-layouts  12.2 us (13%)
  starting transfers between devices  9.88 us (10%)
  other arithmetic  4.49 us (5%)
    pallas_call x1, Pallas kernels, front(): pl.pallas_call(functools.partial(front_kernel, nd, nh, slab, strip), out_...  34.3 us
    pallas_call x1, Pallas kernels, match(): pl.pallas_call(functools.partial(match_kernel, slab, strip), out_shape=ja...  16.7 us
    all_to_all x1, waiting for transfers between devices, exchange(): lax.all_to_all(sent.reshape((depth * height,) + both.shape[1:]), AXES, 0, 0)  9.48 us
    all_to_all x1, starting transfers between devices, exchange(): lax.all_to_all(sent.reshape((depth * height,) + both.shape[1:]), AXES, 0, 0)  7.31 us
    all_to_all x1, waiting for transfers between devices, local(): sums = lax.all_to_all(sent, AXES, 0, 0)  6.54 us
    unnamed x22, local copies, waits for them, and re-layouts  5.67 us
    reshape x3, local copies, waits for them, and re-layouts, parameters(): conv_two.reshape(3, 3, 3, 64, 64).transpose(2, 4, 0, 1, 3).reshape(192, 576)  3.33 us
    all_to_all x1, starting transfers between devices, local(): sums = lax.all_to_all(sent, AXES, 0, 0)  2.57 us
  transfers between devices with their start and end apart: 3, of which 2 were waited for; matrix products, arithmetic and copies ran while one was open for 9% of the time, Pallas kernels for 0%

commit v1 on v0

v1 whole, which is shorter than its diff:
```python
import functools

import jax
import jax.numpy as jnp
import numpy as np
from jax import lax
from jax.experimental import pallas as pl
from jax.experimental.pallas import tpu as pltpu
from jax.sharding import PartitionSpec as P

RADIUS = 3
TILE = 8
F32 = jnp.float32
BF16 = jnp.bfloat16
FAR = -1e30
LOG2E = 1.4426950408889634
NUM = (((1,), (0,)), ((), ()))
AXES = ("depth", "height")


def leaky(v):
    return jnp.maximum(v, 0.01 * v)


def lag_list(far):
    return [(y, x) for y in range(-2, 3) for x in range(-2, 3) if (far, y, x) >= (0, 0, 0)]


def lag_index():
    keys = [("a", "a", far, y, x, "a") for far in range(3) for y, x in lag_list(far)]
    keys += [(e, "a", 0, y, x, "a") for e in "fl" for y, x in lag_list(0)]
    keys += [("a", e, far, 0, x, "a") for e in "fl" for far in range(3) for y, x in lag_list(far) if y == 0]
    keys += [(d, e, 0, 0, x, "a") for d in "fl" for e in "fl" for y, x in lag_list(0) if y == 0]
    keys += [k[:5] + (e,) for e in "fl" for k in list(keys) if k[4] == 0]
    return {k: i for i, k in enumerate(keys)}


LAGS = lag_index()


def pair_table():
    table = np.zeros((729, 256), np.float32)
    taps = [(a, b, c) for a in range(3) for b in range(3) for c in range(3)]
    for i, k in enumerate(taps):
        for j, l in enumerate(taps):
            p, q = (k, l) if l >= k else (l, k)
            lag = tuple(v - u for u, v in zip(p, q))
            kinds = [[("a", 1)] + ([("f" if u == 2 else "l", -1)] if u == v != 1 else []) for u, v in zip(p, q)]
            for d, sd in kinds[0]:
                for h, sh in kinds[1]:
                    for w, sw in kinds[2]:
                        table[i * 27 + j, LAGS[(d, h) + lag + (w,)]] += sd * sh * sw
    return table


def moments_kernel(nd, nh, slab, strip, own_ref, pairs_ref, par_ref, out_ref, img, slid, pieces):
    zn, yn = nd * slab, nh * strip
    count = float(zn * yn * 128)
    lane8 = lax.broadcasted_iota(jnp.int32, (8, 128), 1)
    sub8 = lax.broadcasted_iota(jnp.int32, (8, 128), 0)
    row_y = lax.broadcasted_iota(jnp.int32, (yn, 128), 0)
    side = lax.broadcasted_iota(jnp.int32, (yn, 128), 1)
    gain, shift = [jnp.broadcast_to(par_ref[i:i + 1, :], (128, 128)).T[0:64] for i in range(2)]

    img[0:2] = jnp.zeros((2, yn + 16, 128), F32)
    img[:, 0:8, :] = jnp.zeros((zn + 2, 8, 128), F32)
    img[:, 8 + yn:16 + yn, :] = jnp.zeros((zn + 2, 8, 128), F32)
    slid[:, :, 0:8, :] = jnp.zeros((4, zn, 8, 128), F32)
    slid[:, :, 8 + yn:16 + yn, :] = jnp.zeros((4, zn, 8, 128), F32)

    def gather(d, _):
        for p in range(nh // 2):
            pair = own_ref[pl.ds(d * nh + 2 * p, 2)]
            for z in range(slab):
                both = jnp.concatenate([pair[0, strip * z:strip * (z + 1)], pair[1, strip * z:strip * (z + 1)]], axis=0)
                img[2 + slab * d + z, 8 + 8 * p:16 + 8 * p, :] = both
        return _

    lax.fori_loop(0, nd, gather, 0)

    def slide(i, _):
        at = 4 * i
        for u in range(4):
            v = img[2 + at + u, 8:8 + yn]
            for n, move in enumerate((-2, -1, 1, 2)):
                kept = (side + move >= 0) & (side + move < 128)
                slid[n, at + u, 8:8 + yn] = jnp.where(kept, pltpu.roll(v, (128 - move) % 128, 1), 0.0)
        return _

    lax.fori_loop(0, zn // 4, slide, 0)

    def other(z, y, x):
        if x == 0:
            return img[2 + z, y:y + 8, :]
        return slid[x + 2 if x < 0 else x + 1, z, y:y + 8, :]

    def put(key, v):
        at = 8 * LAGS[key]
        pieces[at:at + 8, :] = v
        if key[4] == 0:
            for e, end in (("f", 0), ("l", 127)):
                at = 8 * LAGS[key[:5] + (e,)]
                pieces[at:at + 8, :] = jnp.where(lane8 == end, v, 0.0)

    def products(z, y, lags, state, fars):
        state = [list(v) for v in state]
        for i in range(yn // 8):
            held = {far: img[2 + z - far, 8 + 8 * i:16 + 8 * i, :] for far in fars}
            moved = {x: other(z, 8 + 8 * i + y, x) for x in range(-2, 3)}
            part = 0 if y or 0 < i < yn // 8 - 1 else 1 if i == 0 else 2
            for n, (far, x) in enumerate(lags):
                if far in fars:
                    state[part][n] = state[part][n] + held[far] * moved[x]
        return tuple(tuple(v) for v in state)

    def record(d, y, lags, state, fars):
        for n, (far, x) in enumerate(lags):
            if far not in fars:
                continue
            if y == 0:
                put((d, "a", far, y, x, "a"), state[0][n] + state[1][n] + state[2][n])
                put((d, "f", far, y, x, "a"), jnp.where(sub8 == 0, state[1][n], 0.0))
                put((d, "l", far, y, x, "a"), jnp.where(sub8 == 7, state[2][n], 0.0))
            else:
                put((d, "a", far, y, x, "a"), state[0][n])

    nothing = jnp.zeros((8, 128), F32)
    pieces[8 * len(LAGS):2048, :] = jnp.zeros((2048 - 8 * len(LAGS), 128), F32)
    for y in range(-2, 3):
        lags = [(far, x) for far in range(3) for x in range(-2, 3) if (far, y, x) >= (0, 0, 0)]
        empty = ((nothing,) * len(lags),) * (1 if y else 3)
        state = lax.fori_loop(0, zn, lambda z, state: products(z, y, lags, state, (0, 1, 2)), empty)
        record("a", y, lags, state, (0, 1, 2))
        if y >= 0:
            for d, z in (("f", 0), ("l", zn - 1)):
                record(d, y, lags, products(z, y, lags, empty, (0,)), (0,))

    def add(z, total):
        return total + img[2 + z, 8:8 + yn, :]

    whole = lax.fori_loop(0, zn, add, jnp.zeros((yn, 128), F32))
    first, last = img[2, 8:8 + yn, :], img[1 + zn, 8:8 + yn, :]
    for kz in range(3):
        plane = (whole - last, whole, whole - first)[kz]
        for ky in range(3):
            v = plane
            if ky == 0:
                v = jnp.where(row_y == yn - 1, 0.0, v)
            if ky == 2:
                v = jnp.where(row_y == 0, 0.0, v)
            v = jnp.sum(v.reshape(yn // 8, 8, 128), axis=0)
            for kx in range(3):
                w = v
                if kx == 0:
                    w = jnp.where(lane8 == 127, 0.0, w)
                if kx == 2:
                    w = jnp.where(lane8 == 0, 0.0, w)
                at = 2048 + (kz * 9 + ky * 3 + kx) * 8
                pieces[at:at + 8, :] = w
    pieces[2264:2304, :] = jnp.zeros((40, 128), F32)
    rows = pieces[pl.ds(0, 288, stride=8), :]
    for s in range(1, 8):
        rows = rows + pieces[pl.ds(s, 288, stride=8), :]
    second = lax.dot_general(pairs_ref[:, 0:256], rows[0:256], NUM, precision=lax.Precision.HIGHEST, preferred_element_type=F32)
    mean = lax.dot_general(pairs_ref[:, 256:288], rows[256:288], NUM, precision=lax.Precision.HIGHEST, preferred_element_type=F32)
    mean = jnp.sum(mean, axis=1, keepdims=True) / count
    second = jnp.sum(second, axis=1, keepdims=True) / count
    scale = lax.rsqrt(second - mean * mean + 1e-05) * gain
    out_ref[0:64, :] = jnp.broadcast_to(scale, (64, 128))
    out_ref[64:128, :] = jnp.broadcast_to(shift - mean * scale, (64, 128))


def moments(own, pairs, par, nd, nh, slab, strip):
    zn, yn = nd * slab, nh * strip
    vm = pl.BlockSpec(memory_space=pltpu.VMEM)
    return pl.pallas_call(
        functools.partial(moments_kernel, nd, nh, slab, strip),
        out_shape=jax.ShapeDtypeStruct((128, 128), F32),
        in_specs=[vm] * 3,
        out_specs=vm,
        scratch_shapes=[
            pltpu.VMEM((zn + 2, yn + 16, 128), F32),
            pltpu.VMEM((4, zn, yn + 16, 128), F32),
            pltpu.VMEM((2304, 128), F32),
        ],
        compiler_params=pltpu.CompilerParams(vmem_limit_bytes=60 * 1024 * 1024),
        cost_estimate=pl.CostEstimate(flops=10 ** 9, bytes_accessed=10 ** 6, transcendentals=0),
        name="moments",
    )(own, pairs, par)


def convolved(weights, feat, z, first, wide, lane64):
    taps = [feat[z + a, :, 128 * (f + b):128 * (f + b + n)] for a in range(3) for b in range(3) for f, n in [(first, wide)]]
    return joined(weights, jnp.concatenate(taps, axis=0), wide, lane64)


def joined(weights, taps, wide, lane64):
    raw = jnp.dot(weights, taps, preferred_element_type=F32)
    rows = []
    for y in range(wide):
        cut = slice(128 * y, 128 * y + 128)
        before = jnp.where(lane64 == 0, 0.0, pltpu.roll(raw[0:64, cut], 1, 1))
        after = jnp.where(lane64 == 127, 0.0, pltpu.roll(raw[128:192, cut], 127, 1))
        rows.append(before + raw[64:128, cut] + after)
    return rows


def encode_kernel(nd, nh, slab, strip, own_ref, other_ref, mine_ref, theirs_ref, taps_ref, two_ref, place_ref,
                  feat_ref, mov_ref, fix_ref, sums_ref, win, toep, plane_hi, plane_lo, feat_m, feat_f, sem):
    zn, yn = nd * slab, nh * strip
    z0, y0, core = place_ref[0], place_ref[1], place_ref[4]
    row, column = place_ref[5], place_ref[6]

    base = taps_ref[...]
    spot = lax.broadcasted_iota(jnp.int32, base.shape, 1)
    base_hi = base.astype(BF16).astype(F32)
    base = jnp.where((spot >= 144) & (spot < 288), (base - base_hi).astype(BF16).astype(F32), base_hi)
    for yo in range(strip + 8):
        toep[64 * yo:64 * yo + 64, :] = (pltpu.roll(base, yo, 1) if yo else base).astype(BF16)

    lane = lax.broadcasted_iota(jnp.int32, (16, 128), 1)
    lane64 = lax.broadcasted_iota(jnp.int32, (64, 128), 1)

    def encode(scan, planes, rows, near, feat):
        mine = core == scan
        for i in range(-1, 2):
            for j in range(-2, 3):
                d, h = row + i, column + j
                inside = (d >= 0) & (d < nd) & (h >= 0) & (h < nh)
                at = jnp.where(inside, d * nh + h, 0)
                block = jnp.where(mine, own_ref[at], other_ref[at])
                block = jnp.where(inside, block, 0.0)
                for z in range(slab):
                    win[slab * (i + 1) + z, strip * (j + 2):strip * (j + 3), :] = block[strip * z:strip * (z + 1)]
        for i in range(planes + 2):
            low = 8 - near - 1
            v = win[slab - near - 1 + i, low:low + 16, :]
            before = jnp.where(lane == 0, 0.0, pltpu.roll(v, 1, 1))
            after = jnp.where(lane == 127, 0.0, pltpu.roll(v, 127, 1))
            v = jnp.concatenate([before, v, after], axis=0)
            hi = v.astype(BF16)
            plane_hi[i] = hi
            plane_lo[i] = (v - hi.astype(F32)).astype(BF16)
        scale = jnp.where(mine, mine_ref[0:64], theirs_ref[0:64])
        offset = jnp.where(mine, mine_ref[64:128], theirs_ref[64:128])

        def first(i, _):
            sides = []
            for u in range(2):
                hi = plane_hi[pl.ds(2 * i + u, 3)].reshape(144, 128)
                lo = plane_lo[pl.ds(2 * i + u, 3)].reshape(144, 128)
                sides.append(jnp.concatenate([hi, hi, lo, jnp.zeros((80, 128), BF16)], axis=0))
            raw = jnp.dot(toep[0:64 * rows, :], jnp.concatenate(sides, axis=1), preferred_element_type=F32)
            for u in range(2):
                z = z0 - near + 2 * i + u
                for yo in range(rows):
                    y = y0 - near + yo
                    v = leaky(raw[64 * yo:64 * yo + 64, 128 * u:128 * u + 128] * scale + offset)
                    v = jnp.where((z >= 0) & (z < zn) & (y >= 0) & (y < yn), v, 0.0)
                    feat[2 * i + u, :, 128 * yo:128 * yo + 128] = v.astype(BF16)
            return _

        lax.fori_loop(0, planes // 2, first, 0)

    def second(feat, rim, out):
        def plane(z, state):
            total, square = state
            for y, v in enumerate(convolved(two_ref[...], feat, rim + z, rim, strip, lane64)):
                out[z, :, 128 * y:128 * y + 128] = v
                total = total + v
                square = square + v * v
            return total, square

        return lax.fori_loop(0, slab, plane, (jnp.zeros((64, 128), F32), jnp.zeros((64, 128), F32)))

    encode(1, slab + 8, strip + 8, 4, feat_m)
    send = pltpu.make_async_copy(feat_m, feat_ref, sem)
    send.start()
    m_sum, m_square = second(feat_m, 3, mov_ref)
    encode(0, slab + 2, strip + 2, 1, feat_f)
    f_sum, f_square = second(feat_f, 0, fix_ref)
    total = jnp.sum(jnp.concatenate([f_sum, m_sum], axis=0).T, axis=0, keepdims=True)
    square = jnp.sum(jnp.concatenate([f_square, m_square], axis=0).T, axis=0, keepdims=True)
    both = jnp.concatenate([total, square], axis=0)
    sums_ref[...] = jnp.broadcast_to(both[None], sums_ref.shape)
    send.wait()


def encode(own, other, mine, theirs, taps, two, place, nd, nh, slab, strip):
    vm = pl.BlockSpec(memory_space=pltpu.VMEM)
    sm = pl.BlockSpec(memory_space=pltpu.SMEM)
    feat = (slab + 8, 64, (strip + 8) * 128)
    return pl.pallas_call(
        functools.partial(encode_kernel, nd, nh, slab, strip),
        out_shape=(
            jax.ShapeDtypeStruct(feat, BF16),
            jax.ShapeDtypeStruct((slab, 64, strip * 128), F32),
            jax.ShapeDtypeStruct((slab, 64, strip * 128), F32),
            jax.ShapeDtypeStruct((nd * nh, 2, 128), F32),
        ),
        in_specs=[vm] * 6 + [sm],
        out_specs=(pl.BlockSpec(memory_space=pl.ANY), vm, vm, vm),
        scratch_shapes=[
            pltpu.VMEM((3 * slab, 24, 128), F32),
            pltpu.VMEM((64 * (strip + 8), 512), BF16),
            pltpu.VMEM((slab + 10, 48, 128), BF16),
            pltpu.VMEM((slab + 10, 48, 128), BF16),
            pltpu.VMEM(feat, BF16),
            pltpu.VMEM((slab + 2, 64, (strip + 2) * 128), BF16),
            pltpu.SemaphoreType.DMA(()),
        ],
        compiler_params=pltpu.CompilerParams(vmem_limit_bytes=60 * 1024 * 1024),
        name="encode",
    )(own, other, mine, theirs, taps, two, place)


def rim_kernel(slab, strip, feat_ref, two_ref, out_ref, feat, out, in_sem, out_sem):
    lane64 = lax.broadcasted_iota(jnp.int32, (64, 128), 1)
    wide = strip + 6
    loads = [pltpu.make_async_copy(feat_ref.at[z], feat.at[z], in_sem.at[z]) for z in range(slab + 8)]
    for load in loads:
        load.start()

    def whole(z):
        for y, v in enumerate(convolved(two_ref[...], feat, z, 0, wide, lane64)):
            out[z, :, 128 * y:128 * y + 128] = v

    def store(z):
        return pltpu.make_async_copy(out.at[z], out_ref.at[z], out_sem.at[z])

    for load in loads[:3]:
        load.wait()
    for z in range(RADIUS):
        if z:
            loads[z + 2].wait()
        whole(z)
        store(z).start()

    def middle(z, _):
        pltpu.make_async_copy(feat_ref.at[z + 2], feat.at[z + 2], in_sem.at[z + 2]).wait()
        taps = []
        for a in range(3):
            for b in range(3):
                left = feat[z + a, :, 128 * b:128 * (b + 3)]
                right = feat[z + a, :, 128 * (strip + 3 + b):128 * (strip + 6 + b)]
                taps.append(jnp.concatenate([left, right], axis=1))
        for y, v in enumerate(joined(two_ref[...], jnp.concatenate(taps, axis=0), 6, lane64)):
            to = y if y < 3 else y + strip
            out[z, :, 128 * to:128 * to + 128] = v
        store(z).start()
        return _

    lax.fori_loop(RADIUS, RADIUS + slab, middle, 0)
    for z in range(RADIUS + slab, slab + 6):
        loads[z + 2].wait()
        whole(z)
        store(z).start()
    for z in range(slab + 6):
        store(z).wait()


def rim(feat, two, slab, strip):
    hbm = pl.BlockSpec(memory_space=pl.ANY)
    vm = pl.BlockSpec(memory_space=pltpu.VMEM)
    shape = (slab + 6, 64, (strip + 6) * 128)
    return pl.pallas_call(
        functools.partial(rim_kernel, slab, strip),
        out_shape=jax.ShapeDtypeStruct(shape, F32),
        in_specs=[hbm, vm],
        out_specs=hbm,
        scratch_shapes=[
            pltpu.VMEM(feat.shape, BF16),
            pltpu.VMEM(shape, F32),
            pltpu.SemaphoreType.DMA((slab + 8,)),
            pltpu.SemaphoreType.DMA((slab + 6,)),
        ],
        compiler_params=pltpu.CompilerParams(vmem_limit_bytes=60 * 1024 * 1024),
        cost_estimate=pl.CostEstimate(flops=6 * 10 ** 9, bytes_accessed=10 ** 7, transcendentals=0),
        name="rim",
    )(feat, two)


def parameters(conv_one, gain_one, shift_one, conv_two, gain_two, shift_two):
    w = conv_one.reshape(64, 3, 3, 3)
    base = jnp.pad(jnp.transpose(w, (0, 1, 3, 2)), ((0, 0), (0, 0), (0, 0), (0, 13))).reshape(64, 144)
    base = jnp.concatenate([base, base, base, jnp.zeros((64, 80), F32)], axis=1)
    flat = conv_one.reshape(64, 27)
    products = (flat[:, :, None] * flat[:, None, :]).reshape(64, 729)
    quad = jnp.dot(products, pair_table(), precision=lax.Precision.HIGHEST)
    pairs = jnp.concatenate([quad, flat, jnp.zeros((64, 5), F32)], axis=1)
    two = conv_two.reshape(3, 3, 3, 64, 64).transpose(2, 4, 0, 1, 3).reshape(192, 576)
    par = jnp.stack([jnp.concatenate([v, v]) for v in (gain_one, shift_one, gain_two, shift_two)])
    return base, pairs, two, par


def block_swap(rows):
    rows = list(rows)
    lane = lax.broadcasted_iota(jnp.int32, rows[0].shape, 1)
    for bit in range(4):
        step = 1 << bit
        low = (lane // (TILE * step)) % 2 == 0
        for q in range(16):
            if q & step:
                continue
            a, c = rows[q], rows[q + step]
            rows[q] = jnp.where(low, a, pltpu.roll(c, TILE * step, 1))
            rows[q + step] = jnp.where(low, pltpu.roll(a, 128 - TILE * step, 1), c)
    return rows


def match_kernel(slab, strip, rim_hbm, mov_hbm, fix_hbm, sums_ref, par_ref, place_ref, sharp_ref, out_ref,
                 rim_ref, mov_ref, fix_ref, even, odd, fixed, score, found, rim_sem, mov_sem, fix_sem):
    ch = fix_ref.shape[1]
    loads = [pltpu.make_async_copy(rim_hbm.at[z], rim_ref.at[z], rim_sem.at[z]) for z in range(slab + 2 * RADIUS)]
    load_mov = pltpu.make_async_copy(mov_hbm, mov_ref, mov_sem)
    load_fix = pltpu.make_async_copy(fix_hbm, fix_ref, fix_sem)
    for load in loads[:RADIUS] + [load_mov] + loads[RADIUS:] + [load_fix]:
        load.start()
    tall, wide = slab + 2 * RADIUS, strip + 2 * RADIUS
    groups = slab // 4
    span = 4 + 2 * RADIUS
    z0, y0 = place_ref[0], place_ref[1]
    zn, yn = place_ref[2], place_ref[3]

    sums = jnp.sum(sums_ref[...], axis=0) / (zn * yn * 128).astype(F32)
    mean, square = sums[0:1], sums[1:2]
    scale = lax.rsqrt(square - mean * mean + 1e-05) * par_ref[2:3]
    offset = par_ref[3:4] - mean * scale
    scale = jnp.broadcast_to(scale, (128, 128)).T
    offset = jnp.broadcast_to(offset, (128, 128)).T

    def feature(raw, scan):
        v = raw * scale[64 * scan:64 * scan + 64] + offset[64 * scan:64 * scan + 64]
        return leaky(v).astype(BF16).astype(F32)

    row = lax.broadcasted_iota(jnp.int32, (128, 128), 0)
    col = lax.broadcasted_iota(jnp.int32, (128, 128), 1)
    onehot_x = jnp.where(col == 64 + row % 16, 1.0, 0.0)
    sub = lax.broadcasted_iota(jnp.int32, (64, 128), 0)

    def plane(z, middle):
        pltpu.make_async_copy(rim_hbm.at[z], rim_ref.at[z], rim_sem.at[z]).wait()
        for y in range(wide):
            if middle and RADIUS <= y < RADIUS + strip:
                raw = mov_ref[z - RADIUS, :, (y - RADIUS) * 128:(y - RADIUS + 1) * 128]
            else:
                raw = rim_ref[z, :, y * 128:(y + 1) * 128]
            f = feature(raw, 1)
            zz, yy = z0 + z - RADIUS, y0 + y - RADIUS
            inside = (zz >= 0) & (zz < zn) & (yy >= 0) & (yy < yn)
            f = jnp.where(inside, f, 0.0)
            norm = jnp.sum(f * f, axis=0, keepdims=True)
            hi = norm.astype(BF16).astype(F32)
            mid = (norm - hi).astype(BF16).astype(F32)
            low = norm - hi - mid
            extra = jnp.where(sub == 48, hi, jnp.where(sub == 49, mid, jnp.where(sub == 50, low, 0.0)))
            t = jnp.concatenate([f, extra], axis=0).T
            ones = jnp.where((col == 64 + 16 + y) | (col == 64 + 32 + z), 1.0, onehot_x)
            even[z, y] = (jnp.where(row >= 4, pltpu.roll(t, 4, 0), 0.0) + ones).astype(BF16)
            odd[z, y] = (jnp.where(row < 124, pltpu.roll(t, 124, 0), 0.0) + ones).astype(BF16)

    def planes(low, high, middle):
        def step(z, _):
            plane(z, middle)
            return _
        lax.fori_loop(low, high, step, 0)

    planes(0, RADIUS, False)
    load_mov.wait()
    planes(RADIUS, RADIUS + slab, True)
    planes(RADIUS + slab, tall, False)
    load_fix.wait()

    k = lax.broadcasted_iota(jnp.int32, (64, 128 * groups), 0)
    lane = lax.broadcasted_iota(jnp.int32, (64, 128 * groups), 1)
    fx, fy, fz = lane % 8, (lane // 8) % 4, lane // 32
    span_x = jnp.abs(k - fx - 4)
    span_y = jnp.abs(k - 16 - fy - 3)
    span_z = jnp.abs(k - 32 - fz - 3)
    apart = jnp.where(k < 16, span_x, jnp.where(k < 32, span_y, jnp.where(k < 48, span_z, 0)))
    tail = jnp.where(apart > RADIUS, FAR, 0.0)
    tail = jnp.where((k >= 48) & (k < 51), -0.5, tail).astype(BF16)
    for j in range(16):
        fixed[j, 64:128, :] = tail
    for g in range(groups):
        for part in range(ch // 16):
            rows = []
            for q in range(16):
                raw = fix_ref[4 * g + q // 4, part * 16:(part + 1) * 16, (q % 4) * 128:(q % 4 + 1) * 128]
                at = slice(part * 16, part * 16 + 16)
                rows.append(leaky(raw * scale[at] + offset[at]).astype(BF16).astype(F32))
            for j, v in enumerate(block_swap(rows)):
                fixed[j, part * 16:(part + 1) * 16, g * 128:(g + 1) * 128] = v.astype(BF16)

    factor = sharp_ref[0] * (2.0 * LOG2E / ch)
    count = wide * 16
    lane1 = lax.broadcasted_iota(jnp.int32, (1, 128), 1)
    x_in, y_in, z_in = lane1 % 8, (lane1 // 8) % 4, lane1 // 32
    pos = lax.broadcasted_iota(jnp.int32, (16, 128), 0).astype(F32)

    def tiles(m, _):
        for parity, held in enumerate((even, odd)):
            j = 2 * m + parity
            weights = fixed[j]
            peak = [jnp.full((8, 128), -3e38, F32) for _g in range(groups)]
            for z in range(tall):
                items = held[z, :, pl.ds(pl.multiple_of(16 * m, 16), 16), :].reshape(count, 128)
                users = [g for g in range(groups) if 4 * g <= z < 4 * g + span]
                s = jnp.dot(items, weights[:, users[0] * 128:(users[-1] + 1) * 128], preferred_element_type=F32)
                for i, g in enumerate(users):
                    part = s[:, i * 128:(i + 1) * 128]
                    score[g, z - 4 * g] = part
                    peak[g] = jnp.maximum(peak[g], jnp.max(part.reshape(count // 8, 8, 128), axis=0))
            for g in range(groups):
                top = jnp.max(peak[g], axis=0, keepdims=True) * factor
                run = jnp.zeros((count, 128), F32)
                acc = jnp.zeros((count, 128), F32)
                for z in range(span - 1, -1, -1):
                    run = run + jnp.exp2(score[g, z] * factor - top)
                    if z:
                        acc = acc + run
                acc_z = jnp.sum(acc, axis=0, keepdims=True)
                by_y = run.reshape(wide, 16, 128)
                by_x = jnp.sum(by_y, axis=0)
                total = jnp.sum(by_x, axis=0, keepdims=True)
                acc_x = jnp.sum(by_x * pos, axis=0, keepdims=True)
                acc_y = jnp.zeros((8, 128), F32)
                part_run = jnp.zeros((8, 128), F32)
                for y in range(wide - 1, 0, -1):
                    part_run = part_run + by_y[y, 0:8] + by_y[y, 8:16]
                    acc_y = acc_y + part_run
                acc_y = jnp.sum(acc_y, axis=0, keepdims=True)
                inv = 1.0 / total
                dz = acc_z * inv - (z_in + RADIUS).astype(F32)
                dy = acc_y * inv - (y_in + RADIUS).astype(F32)
                dx = acc_x * inv - (x_in + 4).astype(F32)
                found[g, j] = jnp.concatenate([dz, dy, dx, jnp.zeros((5, 128), F32)], axis=0)
        return _

    lax.fori_loop(0, 8, tiles, 0)
    for g in range(groups):
        for q, v in enumerate(block_swap([found[g, j] for j in range(16)])):
            for comp in range(3):
                out_ref[comp, 4 * g + q // 4, pl.ds(q % 4, 1), :] = v[comp:comp + 1]


def match(around, moving, fixed, sums, par, place, sharpness, slab, strip):
    tall, wide = slab + 2 * RADIUS, strip + 2 * RADIUS
    groups = slab // 4
    vm = pl.BlockSpec(memory_space=pltpu.VMEM)
    sm = pl.BlockSpec(memory_space=pltpu.SMEM)
    hbm = pl.BlockSpec(memory_space=pl.ANY)
    return pl.pallas_call(
        functools.partial(match_kernel, slab, strip),
        out_shape=jax.ShapeDtypeStruct((3, slab, strip, 128), F32),
        in_specs=[hbm, hbm, hbm, vm, vm, sm, sm],
        out_specs=vm,
        scratch_shapes=[
            pltpu.VMEM(around.shape, F32),
            pltpu.VMEM(moving.shape, F32),
            pltpu.VMEM(fixed.shape, F32),
            pltpu.VMEM((tall, wide, 128, 128), BF16),
            pltpu.VMEM((tall, wide, 128, 128), BF16),
            pltpu.VMEM((16, 128, 128 * groups), BF16),
            pltpu.VMEM((groups, 4 + 2 * RADIUS, wide * 16, 128), F32),
            pltpu.VMEM((groups, 16, 8, 128), F32),
            pltpu.SemaphoreType.DMA((tall,)),
            pltpu.SemaphoreType.DMA(()),
            pltpu.SemaphoreType.DMA(()),
        ],
        compiler_params=pltpu.CompilerParams(vmem_limit_bytes=60 * 1024 * 1024),
        name="match",
    )(around, moving, fixed, sums, par, place, sharpness)


def gathered(fixed_image, moving_image):
    depth, height = lax.axis_size("depth"), lax.axis_size("height")
    slab, strip, width = fixed_image.shape
    both = jnp.stack([fixed_image, moving_image]).reshape(2, slab * strip, width)
    power = jnp.clip(jnp.floor(jnp.log2(jnp.max(jnp.abs(both), axis=(1, 2), keepdims=True))) - 13.0, -113.0, 113.0)
    scaled = (both * jnp.exp2(-power)).astype(jnp.float16)
    power = jnp.broadcast_to(power, (2, 8, width)).astype(jnp.float16)
    sent = jnp.concatenate([scaled, power], axis=1)
    sent = jnp.broadcast_to(sent[None, :, None], (depth // 2, 2, height) + sent.shape[1:])
    return lax.all_to_all(sent.reshape((depth * height,) + sent.shape[3:]), AXES, 0, 0)


def restored(blocks):
    power = jnp.exp2(blocks[:, -8:-7].astype(F32))
    return blocks[:, :-8].astype(F32) * power


def local(fixed_image, moving_image, conv_one, gain_one, shift_one, conv_two, gain_two, shift_two, sharpness):
    depth, height = lax.axis_size("depth"), lax.axis_size("height")
    slab, strip, _ = fixed_image.shape
    swap = [(i, i ^ 1) for i in range(depth)]
    blocks = gathered(fixed_image, moving_image)
    base, pairs, two, par = parameters(conv_one, gain_one, shift_one, conv_two, gain_two, shift_two)
    row, column = lax.axis_index("depth"), lax.axis_index("height")
    place = jnp.stack([row * slab, column * strip, slab * depth, strip * height, row % 2, row, column]).astype(jnp.int32)
    other = restored(lax.ppermute(blocks, "depth", swap))
    own = restored(blocks)
    mine = moments(own, pairs, par, depth, height, slab, strip)
    theirs = lax.ppermute(mine, "depth", swap)
    feat, moving, fixed, sums = encode(own, other, mine, theirs, base, two, place, depth, height, slab, strip)
    sums = lax.all_to_all(sums, AXES, 0, 0)
    around = rim(feat, two, slab, strip)
    return match(around, moving, fixed, sums, par, place, sharpness, slab, strip)


def solution(mesh):
    image = P("depth", "height", None)
    return jax.shard_map(
        local,
        mesh=mesh,
        in_specs=(image, image) + (P(),) * 7,
        out_specs=P(None, "depth", "height", None),
        check_vma=False,
    )
```

time: 95.7 us -> 80.9 us (0.85)
  waiting for transfers between devices: 16 us -> 2.8 us
  local copies, waits for them, and re-layouts: 12.2 us -> 7.12 us
  other arithmetic: 4.49 us -> 6.45 us
  starting transfers between devices: 9.88 us -> 11.4 us
    all_to_all x2, waiting for transfers between devices: 16 us -> 2.57 us  [the longest x1 2.57 us: gathered(): lax.all_to_all(sent.reshape((depth * height,) + sent.shape[3:]), AXES, 0, 0)]
    unnamed x22 -> x14, local copies, waits for them, and re-layouts: 5.67 us -> 1.23 us
    pallas_call x1 -> x3, Pallas kernels: 34.3 us -> 32 us  [the longest x1 14.3 us: encode(): pl.pallas_call(functools.partial(encode_kernel, nd, nh, slab, strip), out...]
    pallas_call x1, Pallas kernels: 16.7 us -> 18.6 us  [match(): pl.pallas_call(functools.partial(match_kernel, slab, strip), out_shape=ja...]
    mul x0 -> x2, other arithmetic: none -> 1.71 us  [restored(): return blocks[:, :-8].astype(F32) * power]
    broadcast_in_dim x2, local copies, waits for them, and re-layouts: 2.14 us -> 0.85 us  [the longest x1 0.77 us: gathered(): jnp.broadcast_to(sent[None, :, None], (depth // 2, 2, height) + sent.shap...]
  transfers between devices with their start and end apart: 3 -> 4, of which waited for: 2 -> 2; matrix products, arithmetic and copies ran while one was open for 9% -> 13% of each run, Pallas kernels for 0% -> 22%
where the time goes in v1:
time: 80.9 us; the launch traced here: 80.1 us
  Pallas kernels  50.6 us (63%)
  starting transfers between devices  11.4 us (14%)
  local copies, waits for them, and re-layouts  7.12 us (9%)
  other arithmetic  6.45 us (8%)
  waiting for transfers between devices  2.8 us (3%)
  between operations  1 us (1%)
  matrix products  0.82 us (1%)
    pallas_call x1, Pallas kernels, match(): pl.pallas_call(functools.partial(match_kernel, slab, strip), out_shape=ja...  18.6 us
    pallas_call x1, Pallas kernels, encode(): pl.pallas_call(functools.partial(encode_kernel, nd, nh, slab, strip), out...  14.3 us
    pallas_call x1, Pallas kernels, rim(): pl.pallas_call(functools.partial(rim_kernel, slab, strip), out_shape=jax....  11 us
    all_to_all x1, starting transfers between devices, gathered(): lax.all_to_all(sent.reshape((depth * height,) + sent.shape[3:]), AXES, 0, 0)  7.31 us
    pallas_call x1, Pallas kernels, moments(): pl.pallas_call(functools.partial(moments_kernel, nd, nh, slab, strip), ou...  6.72 us
    all_to_all x1, starting transfers between devices, local(): sums = lax.all_to_all(sums, AXES, 0, 0)  3.5 us
    reshape x3, local copies, waits for them, and re-layouts, parameters(): conv_two.reshape(3, 3, 3, 64, 64).transpose(2, 4, 0, 1, 3).reshape(192, 576)  3.35 us
    all_to_all x1, waiting for transfers between devices, gathered(): lax.all_to_all(sent.reshape((depth * height,) + sent.shape[3:]), AXES, 0, 0)  2.57 us
  transfers between devices with their start and end apart: 4, of which 2 were waited for; matrix products, arithmetic and copies ran while one was open for 13% of the time, Pallas kernels for 22%

profile of v1, /device:TPU:0, one launch (start us, length us, event | category | flops | bytes accessed | tf_op | source)
XLA Modules:
  0.0 80.1 jit_solution(9713656283899149861)
XLA Ops:
  0.0 0.0 copy-start
  0.0 0.0 copy-start.3
  0.0 0.0 copy-start.4
  0.0 0.0 copy-start.5
  0.0 0.0 copy-start.6
  0.0 0.9 %abs_reduce_fusion = f32[2]{0:T(128)S(1)} fusion(f32[1,32,128]{2,1,0:T(8,128)} %bitcast.35, f32[1,32,128]{2,1,0:T(8,128)} %bitcast.37), kind=kLoop, calls=%fused_computation.7 | loop fusion | flops 24574 | bytes 32776 | tf_op jit(solution)/shard_map/reduce_max | solution.py:580
  0.9 0.8 %multiply_convert_fusion = f16[2,32,128]{2,1,0:T(8,128)(2,1)S(1)} fusion(f32[1,32,128]{2,1,0:T(8,128)} %bitcast.36, f32[1,32,128]{2,1,0:T(8,128)} %bitcast.38, f32[2]{0:T(128)S(1)} %get-tuple-element.13), kind=kLoop, calls=%fused_computation.6 | loop fusion | flops 24576 | bytes 49160 | tf_op jit(solution)/shard_map/convert_element_type | solution.py:581
  1.8 0.1 broadcast_in_dim.8
  1.8 0.8 broadcast_in_dim.9
  2.6 7.3 %all-to-all-start = ((f16[32,40,128]{2,1,0:T(8,128)(2,1)}), f16[32,40,128]{2,1,0:T(8,128)(2,1)S(1)}, u32[]{:S(2)}, u32[]{:S(2)}) async-start(f16[32,40,128]{2,1,0:T(8,128)(2,1)} %bitcast.2), calls=%async_computation | async-start | bytes 655360 | tf_op jit(solution)/shard_map/all_to_all | solution.py:585
  9.9 0.8 reduce
  10.8 0.1 copy.14
  10.9 0.7 copy.25
  11.6 1.4 %reshape.51 = bf16[3,3,3,64,64]{4,3,2,1,0:T(8,128)(2,1)S(1)} reshape(bf16[27,4096]{1,0:T(8,128)(2,1)} %param.15) | data formatting | bytes 442368 | tf_op jit(solution)/shard_map/reshape | solution.py:391
  13.0 0.8 %copy.19 = bf16[3,3,3,64,64]{3,1,0,4,2:T(4,128)(2,1)S(1)} copy(bf16[3,3,3,64,64]{4,3,2,1,0:T(8,128)(2,1)S(1)} %reshape.51) | data formatting | bytes 442368 | tf_op jit(solution)/shard_map/reshape | solution.py:391
  13.9 1.1 %reshape.52.two_ref = bf16[192,576]{1,0:T(8,128)(2,1)} reshape(bf16[3,64,3,3,64]{4,3,2,1,0:T(4,128)(2,1)S(1)} %bitcast.32) | data formatting | bytes 442368 | tf_op jit(solution)/shard_map/reshape | solution.py:391
  15.0 0.1 copy.16
  15.1 0.1 pad.23.clone
  15.2 0.1 pad.8.clone
  15.9 0.0 copy-done.3
  15.9 0.0 copy-done.4
  15.9 0.1 maximum_bitcast_fusion
  16.0 0.0 copy-done
  16.0 0.8 %fusion.5 = f32[64,256]{1,0:T(8,128)S(1)} fusion(f32[64,729]{0,1:T(8,128)S(1)} %mul.65, f32[729,256]{1,0:T(8,128)S(1)} %copy-done), kind=kOutput, calls=%fused_computation.24 | convolution fusion | flops 143327232 | bytes 998656 | tf_op jit(solution)/shard_map/dot_general | solution.py:389
  16.8 0.6 stack.55.place_ref
  17.4 0.0 copy-done.5
  17.4 0.0 copy-done.6
  17.4 0.1 maximum_bitcast_fusion.2
  17.5 0.6 pad_maximum_fusion.2.par_ref
  18.1 0.6 maximum_maximum_fusion.1.pairs_ref
  18.8 0.7 maximum_maximum_fusion.taps_ref
  19.5 2.6 %all-to-all-done = f16[32,40,128]{2,1,0:T(8,128)(2,1)S(1)} async-done(((f16[32,40,128]{2,1,0:T(8,128)(2,1)}), f16[32,40,128]{2,1,0:T(8,128)(2,1)S(1)}, u32[]{:S(2)}, u32[]{:S(2)}) %all-to-all-start) | async-done | bytes 327712 | tf_op jit(solution)/shard_map/all_to_all | solution.py:585
  22.1 0.1 collective-permute-start
  22.2 0.9 %convert_multiply_fusion.1.own_ref = f32[32,32,128]{2,1,0:T(8,128)} fusion(f16[32,40,128]{2,1,0:T(8,128)(2,1)S(1)} %all-to-all-done, f32[32,128]{1,0:T(8,128)S(1)} %bitcast.39), kind=kLoop, calls=%fused_computation.1 | loop fusion | flops 262144 | bytes 802816 | tf_op jit(solution)/shard_map/mul | solution.py:590
  23.0 6.7 %moments.1.mine_ref = f32[128,128]{1,0:T(8,128)} custom-call(f32[32,32,128]{2,1,0:T(8,128)} %convert_multiply_fusion.1.own_ref, f32[64,288]{1,0:T(8,128)} %maximum_maximum_fusion.1.pairs_ref, f32[4,128]{1,0:T(4,128)} %pad_maximum_fusion.2.par_ref), custom_call_target="tpu_custom_call" | custom-call | flops 1000000000 | bytes 1000000 | tf_op jit(solution)/shard_map/moments/pallas_call | solution.py:176
  29.8 0.5 collective-permute-start.1
  30.3 0.0 collective-permute-done
  30.3 0.8 %convert_multiply_fusion.other_ref = f32[32,32,128]{2,1,0:T(8,128)} fusion(f16[32,40,128]{2,1,0:T(8,128)(2,1)S(1)} %collective-permute-done, f32[32,128]{1,0:T(8,128)S(1)} %bitcast.40), kind=kLoop, calls=%fused_computation | loop fusion | flops 262144 | bytes 802816 | tf_op jit(solution)/shard_map/mul | solution.py:590
  31.1 0.2 collective-permute-done.1.theirs_ref
  31.4 0.0 copy-start.2
  31.4 0.6 copy-done.2
  32.0 14.3 %encode.1 = (bf16[16,64,1536]{2,1,0:T(8,128)(2,1)}, f32[8,64,512]{2,1,0:T(8,128)}, f32[8,64,512]{2,1,0:T(8,128)}, f32[32,2,128]{2,1,0:T(2,128)}) custom-call(f32[32,32,128]{2,1,0:T(8,128)} %convert_multiply_fusion.1.own_ref, f32[32,32,128]{2,1,0:T(8,128)} %convert_multiply_fusion.other_ref, f32[128,128]{1,0:T(8,128)} %moments.1.mine_ref, ...), custom_call_target="tpu_custom_call" | custom-call | tf_op jit(solution)/shard_map/encode/pallas_call | solution.py:293
  46.3 3.5 %all-to-all-start.1 = ((f32[32,2,128]{2,1,0:T(2,128)}), f32[32,2,128]{2,1,0:T(2,128)S(1)}, u32[]{:S(2)}, u32[]{:S(2)}) async-start(f32[32,2,128]{2,1,0:T(2,128)} %get-tuple-element.12), calls=%async_computation.1 | async-start | bytes 65536 | tf_op jit(solution)/shard_map/all_to_all | solution.py:606
  49.8 11.0 %rim.1.rim_hbm = f32[14,64,1280]{2,1,0:T(8,128)} custom-call(bf16[16,64,1536]{2,1,0:T(8,128)(2,1)} %get-tuple-element.9.feat_ref, bf16[192,576]{1,0:T(8,128)(2,1)} %reshape.52.two_ref), custom_call_target="tpu_custom_call" | custom-call | flops 6000000000 | bytes 10000000 | tf_op jit(solution)/shard_map/rim/pallas_call | solution.py:366
  60.8 0.0 all-to-all-done.1.sums_ref
  60.8 0.0 copy-start.1
  60.8 0.6 copy-done.1
  61.4 18.6 %match.1 = f32[3,8,4,128]{3,2,1,0:T(4,128)} custom-call(f32[14,64,1280]{2,1,0:T(8,128)} %rim.1.rim_hbm, f32[8,64,512]{2,1,0:T(8,128)} %get-tuple-element.10.mov_hbm, f32[8,64,512]{2,1,0:T(8,128)} %get-tuple-element.11.fix_hbm, f32[32,2,128]{2,1,0:T(2,128)} %copy-done.1, f32[4,128]{1,0:T(4,128)} %pad_maximum_fusion.2.par_ref, s32[7]{0:T(128)} %stack.55.place_ref, ...), custom_call_target="tpu_custom_call" | custom-call | tf_op jit(solution)/shard_map/match/pallas_call | solution.py:553
  (11 shorter events, 0.2 us)
Async XLA Ops:
  0.0 16.0 %copy-start = (f32[729,256]{1,0:T(8,128)S(1)}, f32[729,256]{1,0:T(8,128)}, u32[]{:S(2)}) copy-start(f32[729,256]{1,0:T(8,128)} %constant.48.clone) | copy-start | bytes 2239492
  0.0 15.9 %copy-start.3 = (f32[64]{0:T(128)S(1)}, f32[64]{0:T(128)}, u32[]{:S(2)}) copy-start(f32[64]{0:T(128)} %param.13) | copy-start | bytes 772
  0.0 15.9 %copy-start.4 = (f32[64]{0:T(128)S(1)}, f32[64]{0:T(128)}, u32[]{:S(2)}) copy-start(f32[64]{0:T(128)} %param.14) | copy-start | bytes 772
  0.0 17.4 %copy-start.5 = (f32[64]{0:T(128)S(1)}, f32[64]{0:T(128)}, u32[]{:S(2)}) copy-start(f32[64]{0:T(128)} %param.16) | copy-start | bytes 772
  0.0 17.4 %copy-start.6 = (f32[64]{0:T(128)S(1)}, f32[64]{0:T(128)}, u32[]{:S(2)}) copy-start(f32[64]{0:T(128)} %param.17) | copy-start | bytes 772
  2.6 19.5 %all-to-all-start = ((f16[32,40,128]{2,1,0:T(8,128)(2,1)}), f16[32,40,128]{2,1,0:T(8,128)(2,1)S(1)}, u32[]{:S(2)}, u32[]{:S(2)}) async-start(f16[32,40,128]{2,1,0:T(8,128)(2,1)} %bitcast.2), calls=%async_computation | async-start | bytes 655360 | tf_op jit(solution)/shard_map/all_to_all | solution.py:585
  22.1 8.2 %collective-permute-start = (f16[32,40,128]{2,1,0:T(8,128)(2,1)S(1)}, f16[32,40,128]{2,1,0:T(8,128)(2,1)S(1)}, u32[]{:S(2)}, u32[]{:S(2)}) collective-permute-start(f16[32,40,128]{2,1,0:T(8,128)(2,1)S(1)} %all-to-all-done), channel_id=1, source_target_pairs={{0,8},{8,0},{16,24},{24,16},{1,9},{9,1},{17,25},{25,17},{2,10},{10... | collective-permute-start | bytes 983048 | tf_op jit(solution)/shard_map/ppermute | solution.py:601
  29.8 1.6 %collective-permute-start.1 = (f32[128,128]{1,0:T(8,128)}, f32[128,128]{1,0:T(8,128)S(1)}, u32[]{:S(2)}, u32[]{:S(2)}) collective-permute-start(f32[128,128]{1,0:T(8,128)} %moments.1.mine_ref), channel_id=1, source_target_pairs={{0,8},{8,0},{16,24},{24,16},{1,9},{9,1},{17,25},{25,17},{2,10},{10... | collective-permute-start | bytes 196616 | tf_op jit(solution)/shard_map/ppermute | solution.py:604
  31.4 0.6 copy-start.2
  46.3 14.5 %all-to-all-start.1 = ((f32[32,2,128]{2,1,0:T(2,128)}), f32[32,2,128]{2,1,0:T(2,128)S(1)}, u32[]{:S(2)}, u32[]{:S(2)}) async-start(f32[32,2,128]{2,1,0:T(2,128)} %get-tuple-element.12), calls=%async_computation.1 | async-start | bytes 65536 | tf_op jit(solution)/shard_map/all_to_all | solution.py:606
  60.8 0.6 copy-start.1

commit v2 on v1

--- a/solution.py
+++ b/solution.py
@@ -183,7 +183,7 @@
             pltpu.VMEM((4, zn, yn + 16, 128), F32),
             pltpu.VMEM((2304, 128), F32),
         ],
-        compiler_params=pltpu.CompilerParams(vmem_limit_bytes=60 * 1024 * 1024),
+        compiler_params=pltpu.CompilerParams(vmem_limit_bytes=40 * 1024 * 1024),
         cost_estimate=pl.CostEstimate(flops=10 ** 9, bytes_accessed=10 ** 6, transcendentals=0),
         name="moments",
     )(own, pairs, par)
@@ -205,179 +205,204 @@
     return rows
 
 
-def encode_kernel(nd, nh, slab, strip, own_ref, other_ref, mine_ref, theirs_ref, taps_ref, two_ref, place_ref,
-                  feat_ref, mov_ref, fix_ref, sums_ref, win, toep, plane_hi, plane_lo, feat_m, feat_f, sem):
-    zn, yn = nd * slab, nh * strip
-    z0, y0, core = place_ref[0], place_ref[1], place_ref[4]
-    row, column = place_ref[5], place_ref[6]
-
+def banded(taps_ref, toep, rows):
     base = taps_ref[...]
     spot = lax.broadcasted_iota(jnp.int32, base.shape, 1)
     base_hi = base.astype(BF16).astype(F32)
     base = jnp.where((spot >= 144) & (spot < 288), (base - base_hi).astype(BF16).astype(F32), base_hi)
-    for yo in range(strip + 8):
+    for yo in range(rows):
         toep[64 * yo:64 * yo + 64, :] = (pltpu.roll(base, yo, 1) if yo else base).astype(BF16)
 
+
+def first_layer(scans, slab, strip, near, group, nd, nh, own_ref, other_ref, mine_ref, theirs_ref, place_ref, win, toep, plane_hi, plane_lo, feat):
+    planes, rows = slab + 2 * near, strip + 2 * near
+    zn, yn = nd * slab, nh * strip
+    z0, y0, core = place_ref[0], place_ref[1], place_ref[4]
+    row, column = place_ref[5], place_ref[6]
     lane = lax.broadcasted_iota(jnp.int32, (16, 128), 1)
-    lane64 = lax.broadcasted_iota(jnp.int32, (64, 128), 1)
-
-    def encode(scan, planes, rows, near, feat):
+    reach = -(-(near + 1) // strip)
+    for s, scan in enumerate(scans):
         mine = core == scan
         for i in range(-1, 2):
-            for j in range(-2, 3):
+            for j in range(-reach, reach + 1):
                 d, h = row + i, column + j
                 inside = (d >= 0) & (d < nd) & (h >= 0) & (h < nh)
                 at = jnp.where(inside, d * nh + h, 0)
                 block = jnp.where(mine, own_ref[at], other_ref[at])
                 block = jnp.where(inside, block, 0.0)
                 for z in range(slab):
-                    win[slab * (i + 1) + z, strip * (j + 2):strip * (j + 3), :] = block[strip * z:strip * (z + 1)]
+                    win[s, slab * (i + 1) + z, strip * (j + 2):strip * (j + 3), :] = block[strip * z:strip * (z + 1)]
         for i in range(planes + 2):
-            low = 8 - near - 1
-            v = win[slab - near - 1 + i, low:low + 16, :]
+            low = 2 * strip - near - 1
+            v = win[s, slab - near - 1 + i, low:low + 16, :]
             before = jnp.where(lane == 0, 0.0, pltpu.roll(v, 1, 1))
             after = jnp.where(lane == 127, 0.0, pltpu.roll(v, 127, 1))
             v = jnp.concatenate([before, v, after], axis=0)
             hi = v.astype(BF16)
-            plane_hi[i] = hi
-            plane_lo[i] = (v - hi.astype(F32)).astype(BF16)
-        scale = jnp.where(mine, mine_ref[0:64], theirs_ref[0:64])
-        offset = jnp.where(mine, mine_ref[64:128], theirs_ref[64:128])
-
-        def first(i, _):
-            sides = []
-            for u in range(2):
-                hi = plane_hi[pl.ds(2 * i + u, 3)].reshape(144, 128)
-                lo = plane_lo[pl.ds(2 * i + u, 3)].reshape(144, 128)
+            plane_hi[s, i] = hi
+            plane_lo[s, i] = (v - hi.astype(F32)).astype(BF16)
+    scales = [jnp.where(core == scan, mine_ref[0:64], theirs_ref[0:64]) for scan in scans]
+    offsets = [jnp.where(core == scan, mine_ref[64:128], theirs_ref[64:128]) for scan in scans]
+
+    def first(i, _):
+        sides = []
+        for s in range(len(scans)):
+            for u in range(group):
+                hi = plane_hi[s, pl.ds(group * i + u, 3)].reshape(144, 128)
+                lo = plane_lo[s, pl.ds(group * i + u, 3)].reshape(144, 128)
                 sides.append(jnp.concatenate([hi, hi, lo, jnp.zeros((80, 128), BF16)], axis=0))
-            raw = jnp.dot(toep[0:64 * rows, :], jnp.concatenate(sides, axis=1), preferred_element_type=F32)
-            for u in range(2):
-                z = z0 - near + 2 * i + u
+        raw = jnp.dot(toep[0:64 * rows, :], jnp.concatenate(sides, axis=1), preferred_element_type=F32)
+        for s in range(len(scans)):
+            for u in range(group):
+                z = z0 - near + group * i + u
+                cut = slice(128 * (s * group + u), 128 * (s * group + u) + 128)
                 for yo in range(rows):
                     y = y0 - near + yo
-                    v = leaky(raw[64 * yo:64 * yo + 64, 128 * u:128 * u + 128] * scale + offset)
+                    v = leaky(raw[64 * yo:64 * yo + 64, cut] * scales[s] + offsets[s])
                     v = jnp.where((z >= 0) & (z < zn) & (y >= 0) & (y < yn), v, 0.0)
-                    feat[2 * i + u, :, 128 * yo:128 * yo + 128] = v.astype(BF16)
-            return _
-
-        lax.fori_loop(0, planes // 2, first, 0)
-
-    def second(feat, rim, out):
-        def plane(z, state):
-            total, square = state
-            for y, v in enumerate(convolved(two_ref[...], feat, rim + z, rim, strip, lane64)):
-                out[z, :, 128 * y:128 * y + 128] = v
-                total = total + v
-                square = square + v * v
-            return total, square
-
-        return lax.fori_loop(0, slab, plane, (jnp.zeros((64, 128), F32), jnp.zeros((64, 128), F32)))
-
-    encode(1, slab + 8, strip + 8, 4, feat_m)
-    send = pltpu.make_async_copy(feat_m, feat_ref, sem)
-    send.start()
-    m_sum, m_square = second(feat_m, 3, mov_ref)
-    encode(0, slab + 2, strip + 2, 1, feat_f)
-    f_sum, f_square = second(feat_f, 0, fix_ref)
-    total = jnp.sum(jnp.concatenate([f_sum, m_sum], axis=0).T, axis=0, keepdims=True)
-    square = jnp.sum(jnp.concatenate([f_square, m_square], axis=0).T, axis=0, keepdims=True)
+                    to = 128 * (s * rows + yo)
+                    feat[group * i + u, :, to:to + 128] = v.astype(BF16)
+        return _
+
+    lax.fori_loop(0, planes // group, first, 0)
+
+
+def encode_kernel(nd, nh, slab, strip, own_ref, other_ref, mine_ref, theirs_ref, taps_ref, two_ref, place_ref,
+                  mov_hbm, fix_hbm, sums_ref, win, toep, plane_hi, plane_lo, feat, mov_ref, fix_ref, mov_sem, fix_sem):
+    rows = strip + 2
+    banded(taps_ref, toep, rows)
+    first_layer((0, 1), slab, strip, 1, 2, nd, nh, own_ref, other_ref, mine_ref, theirs_ref, place_ref, win, toep, plane_hi, plane_lo, feat)
+    lane64 = lax.broadcasted_iota(jnp.int32, (64, 128), 1)
+    zero = jnp.zeros((64, 128), F32)
+
+    def stores(z):
+        return (
+            pltpu.make_async_copy(mov_ref.at[z], mov_hbm.at[z], mov_sem.at[z]),
+            pltpu.make_async_copy(fix_ref.at[z], fix_hbm.at[z], fix_sem.at[z]),
+        )
+
+    def plane(z, state):
+        state = list(state)
+        taps = []
+        for a in range(3):
+            for b in range(3):
+                cuts = [feat[z + a, :, 128 * (s * rows + b):128 * (s * rows + b + strip)] for s in range(2)]
+                taps.append(jnp.concatenate(cuts, axis=1))
+        for i, v in enumerate(joined(two_ref[...], jnp.concatenate(taps, axis=0), 2 * strip, lane64)):
+            s, y = i // strip, i % strip
+            (fix_ref, mov_ref)[s][z, :, 128 * y:128 * y + 128] = v
+            state[s] = state[s] + v
+            state[2 + s] = state[2 + s] + v * v
+        for store in stores(z):
+            store.start()
+        return tuple(state)
+
+    sums = lax.fori_loop(0, slab, plane, (zero,) * 4)
+    total = jnp.sum(jnp.concatenate(sums[0:2], axis=0).T, axis=0, keepdims=True)
+    square = jnp.sum(jnp.concatenate(sums[2:4], axis=0).T, axis=0, keepdims=True)
     both = jnp.concatenate([total, square], axis=0)
     sums_ref[...] = jnp.broadcast_to(both[None], sums_ref.shape)
-    send.wait()
+    for z in range(slab):
+        for store in stores(z):
+            store.wait()
 
 
 def encode(own, other, mine, theirs, taps, two, place, nd, nh, slab, strip):
     vm = pl.BlockSpec(memory_space=pltpu.VMEM)
     sm = pl.BlockSpec(memory_space=pltpu.SMEM)
-    feat = (slab + 8, 64, (strip + 8) * 128)
+    hbm = pl.BlockSpec(memory_space=pl.ANY)
     return pl.pallas_call(
         functools.partial(encode_kernel, nd, nh, slab, strip),
         out_shape=(
-            jax.ShapeDtypeStruct(feat, BF16),
             jax.ShapeDtypeStruct((slab, 64, strip * 128), F32),
             jax.ShapeDtypeStruct((slab, 64, strip * 128), F32),
             jax.ShapeDtypeStruct((nd * nh, 2, 128), F32),
         ),
         in_specs=[vm] * 6 + [sm],
-        out_specs=(pl.BlockSpec(memory_space=pl.ANY), vm, vm, vm),
+        out_specs=(hbm, hbm, vm),
         scratch_shapes=[
-            pltpu.VMEM((3 * slab, 24, 128), F32),
-            pltpu.VMEM((64 * (strip + 8), 512), BF16),
-            pltpu.VMEM((slab + 10, 48, 128), BF16),
-            pltpu.VMEM((slab + 10, 48, 128), BF16),
-            pltpu.VMEM(feat, BF16),
-            pltpu.VMEM((slab + 2, 64, (strip + 2) * 128), BF16),
-            pltpu.SemaphoreType.DMA(()),
+            pltpu.VMEM((2, 3 * slab, 24, 128), F32),
+            pltpu.VMEM((64 * (strip + 2), 512), BF16),
+            pltpu.VMEM((2, slab + 4, 48, 128), BF16),
+            pltpu.VMEM((2, slab + 4, 48, 128), BF16),
+            pltpu.VMEM((slab + 2, 64, 2 * (strip + 2) * 128), BF16),
+            pltpu.VMEM((slab, 64, strip * 128), F32),
+            pltpu.VMEM((slab, 64, strip * 128), F32),
+            pltpu.SemaphoreType.DMA((slab,)),
+            pltpu.SemaphoreType.DMA((slab,)),
         ],
         compiler_params=pltpu.CompilerParams(vmem_limit_bytes=60 * 1024 * 1024),
         name="encode",
     )(own, other, mine, theirs, taps, two, place)
 
 
-def rim_kernel(slab, strip, feat_ref, two_ref, out_ref, feat, out, in_sem, out_sem):
+def rim_kernel(nd, nh, slab, strip, own_ref, other_ref, mine_ref, theirs_ref, taps_ref, two_ref, place_ref,
+               edge_ref, side_ref, win, toep, plane_hi, plane_lo, feat, edge, side, edge_sem, side_sem):
     lane64 = lax.broadcasted_iota(jnp.int32, (64, 128), 1)
     wide = strip + 6
-    loads = [pltpu.make_async_copy(feat_ref.at[z], feat.at[z], in_sem.at[z]) for z in range(slab + 8)]
-    for load in loads:
-        load.start()
-
-    def whole(z):
+    banded(taps_ref, toep, strip + 8)
+    first_layer((1,), slab, strip, 4, 4, nd, nh, own_ref, other_ref, mine_ref, theirs_ref, place_ref, win, toep, plane_hi, plane_lo, feat)
+
+    def store_edge(i):
+        return pltpu.make_async_copy(edge.at[i], edge_ref.at[i], edge_sem.at[i])
+
+    def store_side(i):
+        return pltpu.make_async_copy(side.at[i], side_ref.at[i], side_sem.at[i])
+
+    def whole(i, _):
+        z = jnp.where(i < RADIUS, i, i + slab)
         for y, v in enumerate(convolved(two_ref[...], feat, z, 0, wide, lane64)):
-            out[z, :, 128 * y:128 * y + 128] = v
-
-    def store(z):
-        return pltpu.make_async_copy(out.at[z], out_ref.at[z], out_sem.at[z])
-
-    for load in loads[:3]:
-        load.wait()
-    for z in range(RADIUS):
-        if z:
-            loads[z + 2].wait()
-        whole(z)
-        store(z).start()
-
-    def middle(z, _):
-        pltpu.make_async_copy(feat_ref.at[z + 2], feat.at[z + 2], in_sem.at[z + 2]).wait()
+            edge[i, :, 128 * y:128 * y + 128] = v
+        store_edge(i).start()
+        return _
+
+    def middle(i, _):
+        z = RADIUS + 2 * i
         taps = []
         for a in range(3):
             for b in range(3):
-                left = feat[z + a, :, 128 * b:128 * (b + 3)]
-                right = feat[z + a, :, 128 * (strip + 3 + b):128 * (strip + 6 + b)]
-                taps.append(jnp.concatenate([left, right], axis=1))
-        for y, v in enumerate(joined(two_ref[...], jnp.concatenate(taps, axis=0), 6, lane64)):
-            to = y if y < 3 else y + strip
-            out[z, :, 128 * to:128 * to + 128] = v
-        store(z).start()
+                cuts = [feat[z + u + a, :, 128 * (c + b):128 * (c + b + 3)] for u in range(2) for c in (0, strip + 3)]
+                taps.append(jnp.concatenate(cuts, axis=1))
+        for y, v in enumerate(joined(two_ref[...], jnp.concatenate(taps, axis=0), 12, lane64)):
+            side[2 * i + y // 6, :, 128 * (y % 6):128 * (y % 6) + 128] = v
+        store_side(2 * i).start()
+        store_side(2 * i + 1).start()
         return _
 
-    lax.fori_loop(RADIUS, RADIUS + slab, middle, 0)
-    for z in range(RADIUS + slab, slab + 6):
-        loads[z + 2].wait()
-        whole(z)
-        store(z).start()
-    for z in range(slab + 6):
-        store(z).wait()
-
-
-def rim(feat, two, slab, strip):
+    lax.fori_loop(0, 2 * RADIUS, whole, 0)
+    lax.fori_loop(0, slab // 2, middle, 0)
+    for i in range(2 * RADIUS):
+        store_edge(i).wait()
+    for i in range(slab):
+        store_side(i).wait()
+
+
+def rim(own, other, mine, theirs, taps, two, place, nd, nh, slab, strip):
     hbm = pl.BlockSpec(memory_space=pl.ANY)
     vm = pl.BlockSpec(memory_space=pltpu.VMEM)
-    shape = (slab + 6, 64, (strip + 6) * 128)
+    sm = pl.BlockSpec(memory_space=pltpu.SMEM)
+    edge = (6, 64, (strip + 6) * 128)
+    side = (slab, 64, 6 * 128)
     return pl.pallas_call(
-        functools.partial(rim_kernel, slab, strip),
-        out_shape=jax.ShapeDtypeStruct(shape, F32),
-        in_specs=[hbm, vm],
-        out_specs=hbm,
+        functools.partial(rim_kernel, nd, nh, slab, strip),
+        out_shape=(jax.ShapeDtypeStruct(edge, F32), jax.ShapeDtypeStruct(side, F32)),
+        in_specs=[vm] * 6 + [sm],
+        out_specs=(hbm, hbm),
         scratch_shapes=[
-            pltpu.VMEM(feat.shape, BF16),
-            pltpu.VMEM(shape, F32),
-            pltpu.SemaphoreType.DMA((slab + 8,)),
-            pltpu.SemaphoreType.DMA((slab + 6,)),
+            pltpu.VMEM((1, 3 * slab, 24, 128), F32),
+            pltpu.VMEM((64 * (strip + 8), 512), BF16),
+            pltpu.VMEM((1, slab + 10, 48, 128), BF16),
+            pltpu.VMEM((1, slab + 10, 48, 128), BF16),
+            pltpu.VMEM((slab + 8, 64, (strip + 8) * 128), BF16),
+            pltpu.VMEM(edge, F32),
+            pltpu.VMEM(side, F32),
+            pltpu.SemaphoreType.DMA((6,)),
+            pltpu.SemaphoreType.DMA((slab,)),
         ],
         compiler_params=pltpu.CompilerParams(vmem_limit_bytes=60 * 1024 * 1024),
         cost_estimate=pl.CostEstimate(flops=6 * 10 ** 9, bytes_accessed=10 ** 7, transcendentals=0),
         name="rim",
-    )(feat, two)
+    )(own, other, mine, theirs, taps, two, place)
 
 
 def parameters(conv_one, gain_one, shift_one, conv_two, gain_two, shift_two):
@@ -408,14 +433,23 @@
     return rows
 
 
-def match_kernel(slab, strip, rim_hbm, mov_hbm, fix_hbm, sums_ref, par_ref, place_ref, sharp_ref, out_ref,
-                 rim_ref, mov_ref, fix_ref, even, odd, fixed, score, found, rim_sem, mov_sem, fix_sem):
+def match_kernel(slab, strip, edge_hbm, side_hbm, mov_hbm, fix_hbm, sums_ref, par_ref, place_ref, sharp_ref, out_ref,
+                 edge_ref, side_ref, mov_ref, fix_ref, turned, even, odd, fixed, score, peak, found,
+                 edge_sem, side_sem, mov_sem, fix_sem):
     ch = fix_ref.shape[1]
-    loads = [pltpu.make_async_copy(rim_hbm.at[z], rim_ref.at[z], rim_sem.at[z]) for z in range(slab + 2 * RADIUS)]
-    load_mov = pltpu.make_async_copy(mov_hbm, mov_ref, mov_sem)
     load_fix = pltpu.make_async_copy(fix_hbm, fix_ref, fix_sem)
-    for load in loads[:RADIUS] + [load_mov] + loads[RADIUS:] + [load_fix]:
-        load.start()
+
+    def load_edge(i):
+        return pltpu.make_async_copy(edge_hbm.at[i], edge_ref.at[i], edge_sem.at[i])
+
+    def load_side(i):
+        return pltpu.make_async_copy(side_hbm.at[i], side_ref.at[i], side_sem.at[i])
+
+    def load_mov(i):
+        return pltpu.make_async_copy(mov_hbm.at[i], mov_ref.at[i], mov_sem.at[i])
+
+    for i in range(RADIUS):
+        load_edge(i).start()
     tall, wide = slab + 2 * RADIUS, strip + 2 * RADIUS
     groups = slab // 4
     span = 4 + 2 * RADIUS
@@ -433,42 +467,77 @@
         v = raw * scale[64 * scan:64 * scan + 64] + offset[64 * scan:64 * scan + 64]
         return leaky(v).astype(BF16).astype(F32)
 
-    row = lax.broadcasted_iota(jnp.int32, (128, 128), 0)
-    col = lax.broadcasted_iota(jnp.int32, (128, 128), 1)
-    onehot_x = jnp.where(col == 64 + row % 16, 1.0, 0.0)
-    sub = lax.broadcasted_iota(jnp.int32, (64, 128), 0)
+    row16 = lax.broadcasted_iota(jnp.int32, (16, 128), 0)
+    col16 = lax.broadcasted_iota(jnp.int32, (16, 128), 1)
+    onehot_x = jnp.where(col16 == 64 + row16, 1.0, 0.0)
+    sub8 = lax.broadcasted_iota(jnp.int32, (8, 128), 0)
+    blank = jnp.zeros((8, 128), F32)
+    for i in range(2):
+        turned[i, 0:8] = blank
+        turned[i, 128:136] = blank
 
     def plane(z, middle):
-        pltpu.make_async_copy(rim_hbm.at[z], rim_ref.at[z], rim_sem.at[z]).wait()
+        if middle:
+            load_side(z - RADIUS).wait()
+            load_mov(z - RADIUS).wait()
+        else:
+            at = jnp.where(z < RADIUS, z, z - slab)
+            load_edge(at).wait()
+        zz = z0 + z - RADIUS
         for y in range(wide):
-            if middle and RADIUS <= y < RADIUS + strip:
+            if not middle:
+                raw = edge_ref[at, :, y * 128:(y + 1) * 128]
+            elif RADIUS <= y < RADIUS + strip:
                 raw = mov_ref[z - RADIUS, :, (y - RADIUS) * 128:(y - RADIUS + 1) * 128]
             else:
-                raw = rim_ref[z, :, y * 128:(y + 1) * 128]
+                c = y if y < RADIUS else y - strip
+                raw = side_ref[z - RADIUS, :, c * 128:(c + 1) * 128]
             f = feature(raw, 1)
-            zz, yy = z0 + z - RADIUS, y0 + y - RADIUS
-            inside = (zz >= 0) & (zz < zn) & (yy >= 0) & (yy < yn)
-            f = jnp.where(inside, f, 0.0)
+            yy = y0 + y - RADIUS
+            f = jnp.where((zz >= 0) & (zz < zn) & (yy >= 0) & (yy < yn), f, 0.0)
             norm = jnp.sum(f * f, axis=0, keepdims=True)
             hi = norm.astype(BF16).astype(F32)
             mid = (norm - hi).astype(BF16).astype(F32)
             low = norm - hi - mid
-            extra = jnp.where(sub == 48, hi, jnp.where(sub == 49, mid, jnp.where(sub == 50, low, 0.0)))
-            t = jnp.concatenate([f, extra], axis=0).T
-            ones = jnp.where((col == 64 + 16 + y) | (col == 64 + 32 + z), 1.0, onehot_x)
-            even[z, y] = (jnp.where(row >= 4, pltpu.roll(t, 4, 0), 0.0) + ones).astype(BF16)
-            odd[z, y] = (jnp.where(row < 124, pltpu.roll(t, 124, 0), 0.0) + ones).astype(BF16)
-
-    def planes(low, high, middle):
-        def step(z, _):
-            plane(z, middle)
-            return _
-        lax.fori_loop(low, high, step, 0)
-
-    planes(0, RADIUS, False)
-    load_mov.wait()
-    planes(RADIUS, RADIUS + slab, True)
-    planes(RADIUS + slab, tall, False)
+            extra = jnp.where(sub8 == 0, hi, jnp.where(sub8 == 1, mid, jnp.where(sub8 == 2, low, 0.0)))
+            t = jnp.concatenate([f] + [blank] * 6 + [extra, blank], axis=0).T
+            turned[y % 2, 4:132] = t
+            ones = jnp.where((col16 == 64 + 16 + y) | (col16 == 64 + 32 + z) | ((col16 >= 115) & (col16 < 118)), 1.0, onehot_x).astype(BF16)[None]
+            even[z, y] = (turned[y % 2, 0:128].astype(BF16).reshape(8, 16, 128) + ones).reshape(128, 128)
+            odd[z, y] = (turned[y % 2, 8:136].astype(BF16).reshape(8, 16, 128) + ones).reshape(128, 128)
+
+    def before(z, _):
+        load_side(z).start()
+        load_mov(z).start()
+        plane(z, False)
+        return _
+
+    def among(z, _):
+        i = z - RADIUS
+
+        @pl.when(i < slab - RADIUS)
+        def more():
+            load_side(i + RADIUS).start()
+            load_mov(i + RADIUS).start()
+
+        @pl.when(i >= slab - RADIUS)
+        def last():
+            load_edge(i - slab + 2 * RADIUS).start()
+
+        @pl.when(i == slab - 1)
+        def end():
+            load_fix.start()
+
+        plane(z, True)
+        return _
+
+    def after(z, _):
+        plane(z, False)
+        return _
+
+    lax.fori_loop(0, RADIUS, before, 0)
+    lax.fori_loop(RADIUS, RADIUS + slab, among, 0)
+    lax.fori_loop(RADIUS + slab, tall, after, 0)
     load_fix.wait()
 
     k = lax.broadcasted_iota(jnp.int32, (64, 128 * groups), 0)
@@ -479,10 +548,12 @@
     span_z = jnp.abs(k - 32 - fz - 3)
     apart = jnp.where(k < 16, span_x, jnp.where(k < 32, span_y, jnp.where(k < 48, span_z, 0)))
     tail = jnp.where(apart > RADIUS, FAR, 0.0)
-    tail = jnp.where((k >= 48) & (k < 51), -0.5, tail).astype(BF16)
+    tail = tail.astype(BF16)
     for j in range(16):
-        fixed[j, 64:128, :] = tail
+        fixed[j, 64:112, :] = tail[0:48]
+    row16f = lax.broadcasted_iota(jnp.int32, (16, 128), 0)
     for g in range(groups):
+        norms = [jnp.zeros((16, 128), F32)] * 16
         for part in range(ch // 16):
             rows = []
             for q in range(16):
@@ -491,6 +562,13 @@
                 rows.append(leaky(raw * scale[at] + offset[at]).astype(BF16).astype(F32))
             for j, v in enumerate(block_swap(rows)):
                 fixed[j, part * 16:(part + 1) * 16, g * 128:(g + 1) * 128] = v.astype(BF16)
+                norms[j] = norms[j] + v * v
+        for j in range(16):
+            norm = -0.5 * jnp.sum(norms[j], axis=0, keepdims=True)
+            hi = norm.astype(BF16).astype(F32)
+            mid = (norm - hi).astype(BF16).astype(F32)
+            end = jnp.where(row16f < 3, -0.5, jnp.where(row16f == 3, hi, jnp.where(row16f == 4, mid, jnp.where(row16f == 5, norm - hi - mid, 0.0))))
+            fixed[j, 112:128, g * 128:(g + 1) * 128] = end.astype(BF16)
 
     factor = sharp_ref[0] * (2.0 * LOG2E / ch)
     count = wide * 16
@@ -498,53 +576,94 @@
     x_in, y_in, z_in = lane1 % 8, (lane1 // 8) % 4, lane1 // 32
     pos = lax.broadcasted_iota(jnp.int32, (16, 128), 0).astype(F32)
 
-    def tiles(m, _):
-        for parity, held in enumerate((even, odd)):
-            j = 2 * m + parity
-            weights = fixed[j]
-            peak = [jnp.full((8, 128), -3e38, F32) for _g in range(groups)]
-            for z in range(tall):
-                items = held[z, :, pl.ds(pl.multiple_of(16 * m, 16), 16), :].reshape(count, 128)
-                users = [g for g in range(groups) if 4 * g <= z < 4 * g + span]
-                s = jnp.dot(items, weights[:, users[0] * 128:(users[-1] + 1) * 128], preferred_element_type=F32)
-                for i, g in enumerate(users):
-                    part = s[:, i * 128:(i + 1) * 128]
-                    score[g, z - 4 * g] = part
-                    peak[g] = jnp.maximum(peak[g], jnp.max(part.reshape(count // 8, 8, 128), axis=0))
-            for g in range(groups):
-                top = jnp.max(peak[g], axis=0, keepdims=True) * factor
-                run = jnp.zeros((count, 128), F32)
-                acc = jnp.zeros((count, 128), F32)
+    marks = sorted({0, tall} | {4 * g for g in range(groups)} | {4 * g + span for g in range(groups)})
+
+    def scores(m, parity):
+        held = (even, odd)[parity]
+        weights = fixed[2 * m + parity]
+        best = [jnp.full((8, 128), -3e38, F32) for _g in range(groups)]
+        for low, high in zip(marks[:-1], marks[1:]):
+            items = held[low:high, :, pl.ds(pl.multiple_of(16 * m, 16), 16), :].reshape((high - low) * count, 128)
+            users = [g for g in range(groups) if 4 * g <= low < 4 * g + span]
+            s = jnp.dot(items, weights[:, users[0] * 128:(users[-1] + 1) * 128], preferred_element_type=F32)
+            for i, g in enumerate(users):
+                part = s[:, i * 128:(i + 1) * 128]
+                score[parity, g, low - 4 * g:high - 4 * g] = part.reshape(high - low, count, 128)
+                best[g] = jnp.maximum(best[g], jnp.max(part.reshape(-1, 8, 128), axis=0))
+        for g in range(groups):
+            peak[parity, g] = best[g]
+
+    def sums_of(weight):
+        zero = jnp.zeros((16, 128), F32)
+        state = [[zero] * 4 for _g in range(groups)]
+        for y in range(wide - 1, -1, -1):
+            for g, at in enumerate(weight(y)):
+                by_x, acc_z, part, acc_y = state[g]
+                run, acc = zero, zero
                 for z in range(span - 1, -1, -1):
-                    run = run + jnp.exp2(score[g, z] * factor - top)
+                    run = run + at(z)
                     if z:
                         acc = acc + run
-                acc_z = jnp.sum(acc, axis=0, keepdims=True)
-                by_y = run.reshape(wide, 16, 128)
-                by_x = jnp.sum(by_y, axis=0)
-                total = jnp.sum(by_x, axis=0, keepdims=True)
-                acc_x = jnp.sum(by_x * pos, axis=0, keepdims=True)
-                acc_y = jnp.zeros((8, 128), F32)
-                part_run = jnp.zeros((8, 128), F32)
-                for y in range(wide - 1, 0, -1):
-                    part_run = part_run + by_y[y, 0:8] + by_y[y, 8:16]
-                    acc_y = acc_y + part_run
-                acc_y = jnp.sum(acc_y, axis=0, keepdims=True)
-                inv = 1.0 / total
-                dz = acc_z * inv - (z_in + RADIUS).astype(F32)
-                dy = acc_y * inv - (y_in + RADIUS).astype(F32)
-                dx = acc_x * inv - (x_in + 4).astype(F32)
-                found[g, j] = jnp.concatenate([dz, dy, dx, jnp.zeros((5, 128), F32)], axis=0)
-        return _
-
-    lax.fori_loop(0, 8, tiles, 0)
+                if y:
+                    part = part + run
+                    acc_y = acc_y + part
+                state[g] = [by_x + run, acc_z + acc, part, acc_y]
+        return [[jnp.sum(v, axis=0, keepdims=True) for v in (by_x, acc_z, acc_y, by_x * pos)] for by_x, acc_z, _p, acc_y in state]
+
+    def settle(g, j, total, acc_z, acc_y, acc_x):
+        inv = 1.0 / total
+        dz = acc_z * inv - (z_in + RADIUS).astype(F32)
+        dy = acc_y * inv - (y_in + RADIUS).astype(F32)
+        dx = acc_x * inv - (x_in + 4).astype(F32)
+        found[g, j] = jnp.concatenate([dz, dy, dx, total, jnp.zeros((4, 128), F32)], axis=0)
+
+    def tiles(m, least):
+        for parity, held in enumerate((even, odd)):
+            weights = fixed[2 * m + parity]
+
+            def weight(y):
+                items = held[:, y, pl.ds(pl.multiple_of(16 * m, 16), 16), :].reshape(tall * 16, 128)
+                s = jnp.dot(items, weights, preferred_element_type=F32)
+
+                def of(g):
+                    first = 64 * g
+                    return lambda z: jnp.exp2(s[first + 16 * z:first + 16 * z + 16, 128 * g:128 * g + 128] * factor)
+
+                return [of(g) for g in range(groups)]
+
+            for g, sums in enumerate(sums_of(weight)):
+                settle(g, 2 * m + parity, *sums)
+                least = jnp.minimum(least, sums[0])
+        return least
+
+    least = lax.fori_loop(0, 8, tiles, jnp.full((1, 128), 1.0, F32))
+
+    @pl.when(jnp.logical_not(jnp.min(least) > 1e-18))
+    def again():
+        def tiles_again(m, _):
+            for parity in range(2):
+                scores(m, parity)
+                tops = [jnp.max(peak[parity, g], axis=0, keepdims=True) * factor for g in range(groups)]
+
+                def weight(y):
+                    def of(g):
+                        return lambda z: jnp.exp2(score[parity, g, z, 16 * y:16 * y + 16] * factor - tops[g])
+
+                    return [of(g) for g in range(groups)]
+
+                for g, sums in enumerate(sums_of(weight)):
+                    settle(g, 2 * m + parity, *sums)
+            return _
+
+        lax.fori_loop(0, 8, tiles_again, 0)
+
     for g in range(groups):
         for q, v in enumerate(block_swap([found[g, j] for j in range(16)])):
             for comp in range(3):
                 out_ref[comp, 4 * g + q // 4, pl.ds(q % 4, 1), :] = v[comp:comp + 1]
 
 
-def match(around, moving, fixed, sums, par, place, sharpness, slab, strip):
+def match(edge, side, moving, fixed, sums, par, place, sharpness, slab, strip):
     tall, wide = slab + 2 * RADIUS, strip + 2 * RADIUS
     groups = slab // 4
     vm = pl.BlockSpec(memory_space=pltpu.VMEM)
@@ -553,24 +672,28 @@
     return pl.pallas_call(
         functools.partial(match_kernel, slab, strip),
         out_shape=jax.ShapeDtypeStruct((3, slab, strip, 128), F32),
-        in_specs=[hbm, hbm, hbm, vm, vm, sm, sm],
+        in_specs=[hbm] * 4 + [vm, vm, sm, sm],
         out_specs=vm,
         scratch_shapes=[
-            pltpu.VMEM(around.shape, F32),
+            pltpu.VMEM(edge.shape, F32),
+            pltpu.VMEM(side.shape, F32),
             pltpu.VMEM(moving.shape, F32),
             pltpu.VMEM(fixed.shape, F32),
+            pltpu.VMEM((2, 136, 128), F32),
             pltpu.VMEM((tall, wide, 128, 128), BF16),
             pltpu.VMEM((tall, wide, 128, 128), BF16),
             pltpu.VMEM((16, 128, 128 * groups), BF16),
-            pltpu.VMEM((groups, 4 + 2 * RADIUS, wide * 16, 128), F32),
+            pltpu.VMEM((2, groups, 4 + 2 * RADIUS, wide * 16, 128), F32),
+            pltpu.VMEM((2, groups, 8, 128), F32),
             pltpu.VMEM((groups, 16, 8, 128), F32),
-            pltpu.SemaphoreType.DMA((tall,)),
-            pltpu.SemaphoreType.DMA(()),
+            pltpu.SemaphoreType.DMA((2 * RADIUS,)),
+            pltpu.SemaphoreType.DMA((slab,)),
+            pltpu.SemaphoreType.DMA((slab,)),
             pltpu.SemaphoreType.DMA(()),
         ],
         compiler_params=pltpu.CompilerParams(vmem_limit_bytes=60 * 1024 * 1024),
         name="match",
-    )(around, moving, fixed, sums, par, place, sharpness)
+    )(edge, side, moving, fixed, sums, par, place, sharpness)
 
 
 def gathered(fixed_image, moving_image):
@@ -578,9 +701,9 @@
     slab, strip, width = fixed_image.shape
     both = jnp.stack([fixed_image, moving_image]).reshape(2, slab * strip, width)
     power = jnp.clip(jnp.floor(jnp.log2(jnp.max(jnp.abs(both), axis=(1, 2), keepdims=True))) - 13.0, -113.0, 113.0)
-    scaled = (both * jnp.exp2(-power)).astype(jnp.float16)
-    power = jnp.broadcast_to(power, (2, 8, width)).astype(jnp.float16)
-    sent = jnp.concatenate([scaled, power], axis=1)
+    scaled = jnp.pad(both * jnp.exp2(-power), ((0, 0), (0, 8), (0, 0)))
+    spot = lax.broadcasted_iota(jnp.int32, scaled.shape, 1)
+    sent = jnp.where(spot < slab * strip, scaled, power).astype(jnp.float16)
     sent = jnp.broadcast_to(sent[None, :, None], (depth // 2, 2, height) + sent.shape[1:])
     return lax.all_to_all(sent.reshape((depth * height,) + sent.shape[3:]), AXES, 0, 0)
 
@@ -602,10 +725,10 @@
     own = restored(blocks)
     mine = moments(own, pairs, par, depth, height, slab, strip)
     theirs = lax.ppermute(mine, "depth", swap)
-    feat, moving, fixed, sums = encode(own, other, mine, theirs, base, two, place, depth, height, slab, strip)
+    moving, fixed, sums = encode(own, other, mine, theirs, base, two, place, depth, height, slab, strip)
     sums = lax.all_to_all(sums, AXES, 0, 0)
-    around = rim(feat, two, slab, strip)
-    return match(around, moving, fixed, sums, par, place, sharpness, slab, strip)
+    edge, side = rim(own, other, mine, theirs, base, two, place, depth, height, slab, strip)
+    return match(edge, side, moving, fixed, sums, par, place, sharpness, slab, strip)
 
 
 def solution(mesh):

time: 80.9 us -> 71 us (0.88)
  Pallas kernels: 50.6 us -> 42.7 us
  other arithmetic: 6.45 us -> 4.53 us
  waiting for transfers between devices: 2.8 us -> 4.59 us
  local copies, waits for them, and re-layouts: 7.12 us -> 6.17 us
  starting transfers between devices: 11.4 us -> 10.5 us
    pallas_call x1, Pallas kernels: 14.3 us -> 9.77 us  [encode(): pl.pallas_call(functools.partial(encode_kernel, nd, nh, slab, strip), out...]
    pallas_call x1, Pallas kernels: 18.6 us -> 15.9 us  [match(): pl.pallas_call(functools.partial(match_kernel, slab, strip), out_shape=ja...]
    all_to_all x1, waiting for transfers between devices: 2.57 us -> 4.59 us  [gathered(): lax.all_to_all(sent.reshape((depth * height,) + sent.shape[3:]), AXES, 0, 0)]
    pallas_call x1, Pallas kernels: 6.72 us -> 5.01 us  [moments(): pl.pallas_call(functools.partial(moments_kernel, nd, nh, slab, strip), ou...]
    pallas_call x1, Pallas kernels: 11 us -> 12 us  [rim(): pl.pallas_call(functools.partial(rim_kernel, nd, nh, slab, strip), out_sh...]
    reshape x3, local copies, waits for them, and re-layouts: 3.35 us -> 2.37 us  [parameters(): conv_two.reshape(3, 3, 3, 64, 64).transpose(2, 4, 0, 1, 3).reshape(192, 576)]
    all_to_all x1, starting transfers between devices: 3.5 us -> 2.59 us  [local(): sums = lax.all_to_all(sums, AXES, 0, 0)]
    mul x0 -> x1, other arithmetic: none -> 0.82 us  [gathered(): scaled = jnp.pad(both * jnp.exp2(-power), ((0, 0), (0, 8), (0, 0)))]
  transfers between devices with their start and end apart: 4 -> 4, of which waited for: 2 -> 1; matrix products, arithmetic and copies ran while one was open for 13% -> 11% of each run, Pallas kernels for 22% -> 24%
where the time goes in v2:
time: 71 us; the launch traced here: 70.3 us
  Pallas kernels  42.7 us (60%)
  starting transfers between devices  10.5 us (15%)
  local copies, waits for them, and re-layouts  6.17 us (9%)
  waiting for transfers between devices  4.59 us (6%)
  other arithmetic  4.53 us (6%)
  between operations  0.95 us (1%)
  matrix products  0.82 us (1%)
    pallas_call x1, Pallas kernels, match(): pl.pallas_call(functools.partial(match_kernel, slab, strip), out_shape=ja...  15.9 us
    pallas_call x1, Pallas kernels, rim(): pl.pallas_call(functools.partial(rim_kernel, nd, nh, slab, strip), out_sh...  12 us
    pallas_call x1, Pallas kernels, encode(): pl.pallas_call(functools.partial(encode_kernel, nd, nh, slab, strip), out...  9.77 us
    all_to_all x1, starting transfers between devices, gathered(): lax.all_to_all(sent.reshape((depth * height,) + sent.shape[3:]), AXES, 0, 0)  7.3 us
    pallas_call x1, Pallas kernels, moments(): pl.pallas_call(functools.partial(moments_kernel, nd, nh, slab, strip), ou...  5.01 us
    all_to_all x1, waiting for transfers between devices, gathered(): lax.all_to_all(sent.reshape((depth * height,) + sent.shape[3:]), AXES, 0, 0)  4.59 us
    all_to_all x1, starting transfers between devices, local(): sums = lax.all_to_all(sums, AXES, 0, 0)  2.59 us
    reshape x3, local copies, waits for them, and re-layouts, parameters(): conv_two.reshape(3, 3, 3, 64, 64).transpose(2, 4, 0, 1, 3).reshape(192, 576)  2.37 us
  transfers between devices with their start and end apart: 4, of which 1 were waited for; matrix products, arithmetic and copies ran while one was open for 11% of the time, Pallas kernels for 24%

profile of v2, /device:TPU:0, one launch (start us, length us, event | category | flops | bytes accessed | tf_op | source)
XLA Modules:
  0.0 70.3 jit_solution(4140978011421332424)
XLA Ops:
  0.0 0.0 copy-start.4
  0.0 0.9 %abs_reduce_fusion = f32[2]{0:T(128)S(1)} fusion(f32[1,32,128]{2,1,0:T(8,128)} %bitcast.37, f32[1,32,128]{2,1,0:T(8,128)} %bitcast.39), kind=kLoop, calls=%fused_computation.7 | loop fusion | flops 24574 | bytes 32776 | tf_op jit(solution)/shard_map/reduce_max | solution.py:703
  0.9 0.8 %fusion = f32[2,32,128]{2,1,0:T(8,128)S(1)} fusion(f32[1,32,128]{2,1,0:T(8,128)} %bitcast.38, f32[1,32,128]{2,1,0:T(8,128)} %bitcast.40, f32[2]{0:T(128)S(1)} %get-tuple-element.15), kind=kLoop, calls=%fused_computation.8 | loop fusion | flops 16384 | bytes 65544 | tf_op jit(solution)/shard_map/mul | solution.py:704
  1.7 0.1 select_convert_fusion
  1.8 0.8 %broadcast_in_dim.22 = f16[2,2,8,40,128]{4,3,2,1,0:T(8,128)(2,1)} broadcast(f16[2,40,128]{2,1,0:T(8,128)(2,1)S(1)} %select_convert_fusion), dimensions={1,3,4} | broadcast | bytes 348160 | tf_op jit(solution)/shard_map/broadcast_in_dim | solution.py:707
  2.6 7.3 %all-to-all-start = ((f16[32,40,128]{2,1,0:T(8,128)(2,1)}), f16[32,40,128]{2,1,0:T(8,128)(2,1)S(1)}, u32[]{:S(2)}, u32[]{:S(2)}) async-start(f16[32,40,128]{2,1,0:T(8,128)(2,1)} %bitcast.2), calls=%async_computation | async-start | bytes 655360 | tf_op jit(solution)/shard_map/all_to_all | solution.py:708
  9.9 0.8 %reduce = f32[64,3,3,3]{0,3,2,1:T(4,128)S(1)} reduce(f32[64,1,3,3,3]{0,1,4,3,2:T(1,128)} %param.12, f32[]{:T(128)} %constant.56), dimensions={1}, to_apply=%param.12.reduce_sub_computation | reduce | bytes 13828 | tf_op args[2]
  10.7 0.0 copy-start.7
  10.7 0.0 copy-start.8
  10.7 0.0 copy-start.3
  10.8 0.1 copy.14
  10.8 0.8 %copy.25 = f32[64,1,3,3,3]{0,3,4,2,1:T(4,128)S(1)} copy(f32[64,1,3,3,3]{0,1,4,3,2:T(1,128)} %param.12) | data formatting | bytes 13824 | tf_op jit(solution)/shard_map/transpose | solution.py:410
  11.7 0.0 copy-done.4
  11.7 0.0 copy-start.9
  11.7 0.0 copy-start.10
  11.7 0.4 reshape.51
  12.1 0.8 %copy.19 = bf16[3,3,3,64,64]{3,1,0,4,2:T(4,128)(2,1)S(1)} copy(bf16[3,3,3,64,64]{4,3,2,1,0:T(8,128)(2,1)S(1)} %reshape.51) | data formatting | bytes 442368 | tf_op jit(solution)/shard_map/reshape | solution.py:416
  13.0 1.1 %reshape.52.two_ref = bf16[192,576]{1,0:T(8,128)(2,1)} reshape(bf16[3,64,3,3,64]{4,3,2,1,0:T(4,128)(2,1)S(1)} %bitcast.32) | data formatting | bytes 442368 | tf_op jit(solution)/shard_map/reshape | solution.py:416
  14.1 0.1 copy.16
  14.2 0.1 pad.28.clone
  14.3 0.1 pad.13.clone
  15.0 0.0 copy-done.7
  15.0 0.0 copy-done.8
  15.0 0.1 maximum_bitcast_fusion
  15.1 0.0 copy-done.3
  15.1 0.8 %fusion.5 = f32[64,256]{1,0:T(8,128)S(1)} fusion(f32[64,729]{0,1:T(8,128)S(1)} %mul.65, f32[729,256]{1,0:T(8,128)S(1)} %copy-done.3), kind=kOutput, calls=%fused_computation.24 | convolution fusion | flops 143327232 | bytes 998656 | tf_op jit(solution)/shard_map/dot_general | solution.py:414
  15.9 0.6 stack.55.place_ref
  16.5 0.0 copy-done.9
  16.5 0.0 copy-done.10
  16.5 0.1 maximum_bitcast_fusion.2
  16.6 0.0 copy-start.2
  16.7 0.8 %maximum_maximum_fusion.taps_ref = f32[64,512]{1,0:T(8,128)} fusion(f32[64,144]{1,0:T(8,128)S(1)} %copy.16, f32[512]{0:T(512)S(1)} %pad.13.clone), kind=kLoop, calls=%fused_computation.3 | loop fusion | flops 98304 | bytes 169984 | tf_op jit(solution)/shard_map/concatenate | solution.py:411
  17.4 4.6 %all-to-all-done = f16[32,40,128]{2,1,0:T(8,128)(2,1)S(1)} async-done(((f16[32,40,128]{2,1,0:T(8,128)(2,1)}), f16[32,40,128]{2,1,0:T(8,128)(2,1)S(1)}, u32[]{:S(2)}, u32[]{:S(2)}) %all-to-all-start) | async-done | bytes 327712 | tf_op jit(solution)/shard_map/all_to_all | solution.py:708
  22.1 0.1 collective-permute-start
  22.1 0.1 convert_multiply_fusion.1.own_ref
  22.2 0.0 copy-start
  22.2 5.0 %moments.1.mine_ref = f32[128,128]{1,0:T(8,128)S(1)} custom-call(f32[32,32,128]{2,1,0:T(8,128)S(1)} %convert_multiply_fusion.1.own_ref, f32[64,288]{1,0:T(8,128)S(1)} %maximum_maximum_fusion.1.pairs_ref, f32[4,128]{1,0:T(4,128)S(1)} %pad_maximum_fusion.1.par_ref), custom_call_target="tpu_custom_call" | custom-call | flops 1000000000 | bytes 1000000 | tf_op jit(solution)/shard_map/moments/pallas_call | solution.py:176
  27.2 0.0 copy-done.2
  27.2 0.0 copy-start.1
  27.2 0.6 collective-permute-start.1
  27.8 0.0 collective-permute-done
  27.8 0.9 %convert_multiply_fusion.other_ref = f32[32,32,128]{2,1,0:T(8,128)} fusion(f16[32,40,128]{2,1,0:T(8,128)(2,1)S(1)} %collective-permute-done, f32[32,128]{1,0:T(8,128)S(1)} %bitcast.36), kind=kLoop, calls=%fused_computation | loop fusion | flops 262144 | bytes 802816 | tf_op jit(solution)/shard_map/mul | solution.py:713
  28.7 0.0 copy-done
  28.7 0.0 collective-permute-done.1.theirs_ref
  28.7 0.0 copy-done.1
  28.7 0.0 copy-start.6
  28.7 0.6 copy-done.6
  29.3 9.8 %encode.1 = (f32[8,64,512]{2,1,0:T(8,128)}, f32[8,64,512]{2,1,0:T(8,128)}, f32[32,2,128]{2,1,0:T(2,128)}) custom-call(f32[32,32,128]{2,1,0:T(8,128)} %copy-done, f32[32,32,128]{2,1,0:T(8,128)} %convert_multiply_fusion.other_ref, f32[128,128]{1,0:T(8,128)} %copy-done.1, f32[128,128]{1,0:T(8,128)} %copy-done.6, f32[64,512]{1,0:T(8,128)} %maximum_maximum_fusion.taps_ref, ...), custom_call_target="tpu_custom_call" | custom-call | tf_op jit(solution)/shard_map/encode/pallas_call | solution.py:314
  39.1 2.6 %all-to-all-start.1 = ((f32[32,2,128]{2,1,0:T(2,128)}), f32[32,2,128]{2,1,0:T(2,128)S(1)}, u32[]{:S(2)}, u32[]{:S(2)}) async-start(f32[32,2,128]{2,1,0:T(2,128)} %get-tuple-element.14), calls=%async_computation.1 | async-start | bytes 65536 | tf_op jit(solution)/shard_map/all_to_all | solution.py:729
  41.7 12.0 %rim.1 = (f32[6,64,1280]{2,1,0:T(8,128)}, f32[8,64,768]{2,1,0:T(8,128)}) custom-call(f32[32,32,128]{2,1,0:T(8,128)} %copy-done, f32[32,32,128]{2,1,0:T(8,128)} %convert_multiply_fusion.other_ref, f32[128,128]{1,0:T(8,128)} %copy-done.1, f32[128,128]{1,0:T(8,128)} %copy-done.6, f32[64,512]{1,0:T(8,128)} %maximum_maximum_fusion.taps_ref, ...), custom_call_target="tpu_custom_call" | custom-call | flops 6000000000 | bytes 10000000 | tf_op jit(solution)/shard_map/rim/pallas_call | solution.py:386
  53.8 0.0 all-to-all-done.1.sums_ref
  53.8 0.0 copy-start.5
  53.8 0.6 copy-done.5
  54.4 15.9 %match.1 = f32[3,8,4,128]{3,2,1,0:T(4,128)} custom-call(f32[6,64,1280]{2,1,0:T(8,128)} %get-tuple-element.10.edge_hbm, f32[8,64,768]{2,1,0:T(8,128)} %get-tuple-element.11.side_hbm, f32[8,64,512]{2,1,0:T(8,128)} %get-tuple-element.12.mov_hbm, f32[8,64,512]{2,1,0:T(8,128)} %get-tuple-element.13.fix_hbm, f32[32,2,128]{2,1,0:T(2,128)} %copy-done.5, ...), custom_call_target="tpu_custom_call" | custom-call | tf_op jit(solution)/shard_map/match/pallas_call | solution.py:672
  (13 shorter events, 0.2 us)
Async XLA Ops:
  0.0 11.7 %copy-start.4 = (bf16[27,4096]{1,0:T(8,128)(2,1)S(1)}, bf16[27,4096]{1,0:T(8,128)(2,1)}, u32[]{:S(2)}) copy-start(bf16[27,4096]{1,0:T(8,128)(2,1)} %param.15) | copy-start | bytes 663556
  2.6 19.4 %all-to-all-start = ((f16[32,40,128]{2,1,0:T(8,128)(2,1)}), f16[32,40,128]{2,1,0:T(8,128)(2,1)S(1)}, u32[]{:S(2)}, u32[]{:S(2)}) async-start(f16[32,40,128]{2,1,0:T(8,128)(2,1)} %bitcast.2), calls=%async_computation | async-start | bytes 655360 | tf_op jit(solution)/shard_map/all_to_all | solution.py:708
  10.7 4.3 %copy-start.7 = (f32[64]{0:T(128)S(1)}, f32[64]{0:T(128)}, u32[]{:S(2)}) copy-start(f32[64]{0:T(128)} %param.13) | copy-start | bytes 772
  10.7 4.3 %copy-start.8 = (f32[64]{0:T(128)S(1)}, f32[64]{0:T(128)}, u32[]{:S(2)}) copy-start(f32[64]{0:T(128)} %param.14) | copy-start | bytes 772
  10.7 4.4 %copy-start.3 = (f32[729,256]{1,0:T(8,128)S(1)}, f32[729,256]{1,0:T(8,128)}, u32[]{:S(2)}) copy-start(f32[729,256]{1,0:T(8,128)} %constant.49.clone) | copy-start | bytes 2239492
  11.7 4.9 %copy-start.9 = (f32[64]{0:T(128)S(1)}, f32[64]{0:T(128)}, u32[]{:S(2)}) copy-start(f32[64]{0:T(128)} %param.16) | copy-start | bytes 772
  11.7 4.9 %copy-start.10 = (f32[64]{0:T(128)S(1)}, f32[64]{0:T(128)}, u32[]{:S(2)}) copy-start(f32[64]{0:T(128)} %param.17) | copy-start | bytes 772
  16.6 10.6 %copy-start.2 = (f32[4,128]{1,0:T(4,128)}, f32[4,128]{1,0:T(4,128)S(1)}, u32[]{:S(2)}) copy-start(f32[4,128]{1,0:T(4,128)S(1)} %pad_maximum_fusion.1.par_ref) | copy-start | bytes 6148
  22.1 5.8 %collective-permute-start = (f16[32,40,128]{2,1,0:T(8,128)(2,1)S(1)}, f16[32,40,128]{2,1,0:T(8,128)(2,1)S(1)}, u32[]{:S(2)}, u32[]{:S(2)}) collective-permute-start(f16[32,40,128]{2,1,0:T(8,128)(2,1)S(1)} %all-to-all-done), channel_id=1, source_target_pairs={{0,8},{8,0},{16,24},{24,16},{1,9},{9,1},{17,25},{25,17},{2,10},{10... | collective-permute-start | bytes 983048 | tf_op jit(solution)/shard_map/ppermute | solution.py:724
  22.2 6.5 %copy-start = (f32[32,32,128]{2,1,0:T(8,128)}, f32[32,32,128]{2,1,0:T(8,128)S(1)}, u32[]{:S(2)}) copy-start(f32[32,32,128]{2,1,0:T(8,128)S(1)} %convert_multiply_fusion.1.own_ref) | copy-start | bytes 1572868
  27.2 1.5 %copy-start.1 = (f32[128,128]{1,0:T(8,128)}, f32[128,128]{1,0:T(8,128)S(1)}, u32[]{:S(2)}) copy-start(f32[128,128]{1,0:T(8,128)S(1)} %moments.1.mine_ref) | copy-start | bytes 196612
  27.2 1.5 %collective-permute-start.1 = (f32[128,128]{1,0:T(8,128)S(1)}, f32[128,128]{1,0:T(8,128)S(1)}, u32[]{:S(2)}, u32[]{:S(2)}) collective-permute-start(f32[128,128]{1,0:T(8,128)S(1)} %moments.1.mine_ref), channel_id=1, source_target_pairs={{0,8},{8,0},{16,24},{24,16},{1,9},{9,1},{17,25},{25,17},{2,10},{10... | collective-permute-start | bytes 196616 | tf_op jit(solution)/shard_map/ppermute | solution.py:727
  28.7 0.6 copy-start.6
  39.1 14.6 %all-to-all-start.1 = ((f32[32,2,128]{2,1,0:T(2,128)}), f32[32,2,128]{2,1,0:T(2,128)S(1)}, u32[]{:S(2)}, u32[]{:S(2)}) async-start(f32[32,2,128]{2,1,0:T(2,128)} %get-tuple-element.14), calls=%async_computation.1 | async-start | bytes 65536 | tf_op jit(solution)/shard_map/all_to_all | solution.py:729
  53.8 0.6 copy-start.5

commit v3 on v2

--- a/solution.py
+++ b/solution.py
@@ -268,18 +268,15 @@
 
 
 def encode_kernel(nd, nh, slab, strip, own_ref, other_ref, mine_ref, theirs_ref, taps_ref, two_ref, place_ref,
-                  mov_hbm, fix_hbm, sums_ref, win, toep, plane_hi, plane_lo, feat, mov_ref, fix_ref, mov_sem, fix_sem):
+                  raw_hbm, sums_ref, win, toep, plane_hi, plane_lo, feat, raw, sem):
     rows = strip + 2
     banded(taps_ref, toep, rows)
     first_layer((0, 1), slab, strip, 1, 2, nd, nh, own_ref, other_ref, mine_ref, theirs_ref, place_ref, win, toep, plane_hi, plane_lo, feat)
     lane64 = lax.broadcasted_iota(jnp.int32, (64, 128), 1)
     zero = jnp.zeros((64, 128), F32)
 
-    def stores(z):
-        return (
-            pltpu.make_async_copy(mov_ref.at[z], mov_hbm.at[z], mov_sem.at[z]),
-            pltpu.make_async_copy(fix_ref.at[z], fix_hbm.at[z], fix_sem.at[z]),
-        )
+    def store(z):
+        return pltpu.make_async_copy(raw.at[z], raw_hbm.at[z], sem.at[z])
 
     def plane(z, state):
         state = list(state)
@@ -290,11 +287,10 @@
                 taps.append(jnp.concatenate(cuts, axis=1))
         for i, v in enumerate(joined(two_ref[...], jnp.concatenate(taps, axis=0), 2 * strip, lane64)):
             s, y = i // strip, i % strip
-            (fix_ref, mov_ref)[s][z, :, 128 * y:128 * y + 128] = v
+            raw[z, s, :, 128 * y:128 * y + 128] = v
             state[s] = state[s] + v
             state[2 + s] = state[2 + s] + v * v
-        for store in stores(z):
-            store.start()
+        store(z).start()
         return tuple(state)
 
     sums = lax.fori_loop(0, slab, plane, (zero,) * 4)
@@ -303,8 +299,7 @@
     both = jnp.concatenate([total, square], axis=0)
     sums_ref[...] = jnp.broadcast_to(both[None], sums_ref.shape)
     for z in range(slab):
-        for store in stores(z):
-            store.wait()
+        store(z).wait()
 
 
 def encode(own, other, mine, theirs, taps, two, place, nd, nh, slab, strip):
@@ -314,24 +309,21 @@
     return pl.pallas_call(
         functools.partial(encode_kernel, nd, nh, slab, strip),
         out_shape=(
-            jax.ShapeDtypeStruct((slab, 64, strip * 128), F32),
-            jax.ShapeDtypeStruct((slab, 64, strip * 128), F32),
+            jax.ShapeDtypeStruct((slab, 2, 64, strip * 128), F32),
             jax.ShapeDtypeStruct((nd * nh, 2, 128), F32),
         ),
         in_specs=[vm] * 6 + [sm],
-        out_specs=(hbm, hbm, vm),
+        out_specs=(hbm, vm),
         scratch_shapes=[
             pltpu.VMEM((2, 3 * slab, 24, 128), F32),
             pltpu.VMEM((64 * (strip + 2), 512), BF16),
             pltpu.VMEM((2, slab + 4, 48, 128), BF16),
             pltpu.VMEM((2, slab + 4, 48, 128), BF16),
             pltpu.VMEM((slab + 2, 64, 2 * (strip + 2) * 128), BF16),
-            pltpu.VMEM((slab, 64, strip * 128), F32),
-            pltpu.VMEM((slab, 64, strip * 128), F32),
-            pltpu.SemaphoreType.DMA((slab,)),
+            pltpu.VMEM((slab, 2, 64, strip * 128), F32),
             pltpu.SemaphoreType.DMA((slab,)),
         ],
-        compiler_params=pltpu.CompilerParams(vmem_limit_bytes=60 * 1024 * 1024),
+        compiler_params=pltpu.CompilerParams(vmem_limit_bytes=52 * 1024 * 1024),
         name="encode",
     )(own, other, mine, theirs, taps, two, place)
 
@@ -399,7 +391,7 @@
             pltpu.SemaphoreType.DMA((6,)),
             pltpu.SemaphoreType.DMA((slab,)),
         ],
-        compiler_params=pltpu.CompilerParams(vmem_limit_bytes=60 * 1024 * 1024),
+        compiler_params=pltpu.CompilerParams(vmem_limit_bytes=52 * 1024 * 1024),
         cost_estimate=pl.CostEstimate(flops=6 * 10 ** 9, bytes_accessed=10 ** 7, transcendentals=0),
         name="rim",
     )(own, other, mine, theirs, taps, two, place)
@@ -433,23 +425,24 @@
     return rows
 
 
-def match_kernel(slab, strip, edge_hbm, side_hbm, mov_hbm, fix_hbm, sums_ref, par_ref, place_ref, sharp_ref, out_ref,
-                 edge_ref, side_ref, mov_ref, fix_ref, turned, even, odd, fixed, score, peak, found,
-                 edge_sem, side_sem, mov_sem, fix_sem):
-    ch = fix_ref.shape[1]
-    load_fix = pltpu.make_async_copy(fix_hbm, fix_ref, fix_sem)
-
+def match_kernel(slab, strip, edge_hbm, side_hbm, raw_hbm, sums_ref, par_ref, place_ref, sharp_ref, out_ref,
+                 edge_ref, side_ref, raw_ref, turned, even, odd, fixed, score, peak, found,
+                 edge_sem, side_sem, raw_sem):
+    ch = raw_ref.shape[2]
     def load_edge(i):
         return pltpu.make_async_copy(edge_hbm.at[i], edge_ref.at[i], edge_sem.at[i])
 
     def load_side(i):
         return pltpu.make_async_copy(side_hbm.at[i], side_ref.at[i], side_sem.at[i])
 
-    def load_mov(i):
-        return pltpu.make_async_copy(mov_hbm.at[i], mov_ref.at[i], mov_sem.at[i])
-
-    for i in range(RADIUS):
-        load_edge(i).start()
+    def load_raw(i):
+        return pltpu.make_async_copy(raw_hbm.at[i], raw_ref.at[i], raw_sem.at[i])
+
+    ahead = [load_edge(i) for i in range(RADIUS)]
+    ahead += [load(i) for i in range(slab) for load in (load_side, load_raw)]
+    ahead += [load_edge(RADIUS + i) for i in range(RADIUS)]
+    for load in ahead:
+        load.start()
     tall, wide = slab + 2 * RADIUS, strip + 2 * RADIUS
     groups = slab // 4
     span = 4 + 2 * RADIUS
@@ -469,17 +462,16 @@
 
     row16 = lax.broadcasted_iota(jnp.int32, (16, 128), 0)
     col16 = lax.broadcasted_iota(jnp.int32, (16, 128), 1)
-    onehot_x = jnp.where(col16 == 64 + row16, 1.0, 0.0)
+    onehot_x = jnp.where((col16 == 80 + row16) | ((col16 >= 67) & (col16 < 70)), 1.0, 0.0)
     sub8 = lax.broadcasted_iota(jnp.int32, (8, 128), 0)
     blank = jnp.zeros((8, 128), F32)
     for i in range(2):
-        turned[i, 0:8] = blank
-        turned[i, 128:136] = blank
+        turned[i] = jnp.zeros((136, 128), F32)
 
     def plane(z, middle):
         if middle:
             load_side(z - RADIUS).wait()
-            load_mov(z - RADIUS).wait()
+            load_raw(z - RADIUS).wait()
         else:
             at = jnp.where(z < RADIUS, z, z - slab)
             load_edge(at).wait()
@@ -488,7 +480,7 @@
             if not middle:
                 raw = edge_ref[at, :, y * 128:(y + 1) * 128]
             elif RADIUS <= y < RADIUS + strip:
-                raw = mov_ref[z - RADIUS, :, (y - RADIUS) * 128:(y - RADIUS + 1) * 128]
+                raw = raw_ref[z - RADIUS, 1, :, (y - RADIUS) * 128:(y - RADIUS + 1) * 128]
             else:
                 c = y if y < RADIUS else y - strip
                 raw = side_ref[z - RADIUS, :, c * 128:(c + 1) * 128]
@@ -500,34 +492,12 @@
             mid = (norm - hi).astype(BF16).astype(F32)
             low = norm - hi - mid
             extra = jnp.where(sub8 == 0, hi, jnp.where(sub8 == 1, mid, jnp.where(sub8 == 2, low, 0.0)))
-            t = jnp.concatenate([f] + [blank] * 6 + [extra, blank], axis=0).T
-            turned[y % 2, 4:132] = t
-            ones = jnp.where((col16 == 64 + 16 + y) | (col16 == 64 + 32 + z) | ((col16 >= 115) & (col16 < 118)), 1.0, onehot_x).astype(BF16)[None]
+            turned[y % 2, 4:132, 0:72] = jnp.concatenate([f, extra], axis=0).T
+            ones = jnp.where((col16 == 96 + y) | (col16 == 112 + z), 1.0, onehot_x).astype(BF16)[None]
             even[z, y] = (turned[y % 2, 0:128].astype(BF16).reshape(8, 16, 128) + ones).reshape(128, 128)
             odd[z, y] = (turned[y % 2, 8:136].astype(BF16).reshape(8, 16, 128) + ones).reshape(128, 128)
 
-    def before(z, _):
-        load_side(z).start()
-        load_mov(z).start()
-        plane(z, False)
-        return _
-
     def among(z, _):
-        i = z - RADIUS
-
-        @pl.when(i < slab - RADIUS)
-        def more():
-            load_side(i + RADIUS).start()
-            load_mov(i + RADIUS).start()
-
-        @pl.when(i >= slab - RADIUS)
-        def last():
-            load_edge(i - slab + 2 * RADIUS).start()
-
-        @pl.when(i == slab - 1)
-        def end():
-            load_fix.start()
-
         plane(z, True)
         return _
 
@@ -535,10 +505,9 @@
         plane(z, False)
         return _
 
-    lax.fori_loop(0, RADIUS, before, 0)
+    lax.fori_loop(0, RADIUS, after, 0)
     lax.fori_loop(RADIUS, RADIUS + slab, among, 0)
     lax.fori_loop(RADIUS + slab, tall, after, 0)
-    load_fix.wait()
 
     k = lax.broadcasted_iota(jnp.int32, (64, 128 * groups), 0)
     lane = lax.broadcasted_iota(jnp.int32, (64, 128 * groups), 1)
@@ -550,25 +519,25 @@
     tail = jnp.where(apart > RADIUS, FAR, 0.0)
     tail = tail.astype(BF16)
     for j in range(16):
-        fixed[j, 64:112, :] = tail[0:48]
+        fixed[j, 80:128, :] = tail[0:48]
     row16f = lax.broadcasted_iota(jnp.int32, (16, 128), 0)
     for g in range(groups):
         norms = [jnp.zeros((16, 128), F32)] * 16
         for part in range(ch // 16):
             rows = []
             for q in range(16):
-                raw = fix_ref[4 * g + q // 4, part * 16:(part + 1) * 16, (q % 4) * 128:(q % 4 + 1) * 128]
+                raw = raw_ref[4 * g + q // 4, 0, part * 16:(part + 1) * 16, (q % 4) * 128:(q % 4 + 1) * 128]
                 at = slice(part * 16, part * 16 + 16)
-                rows.append(leaky(raw * scale[at] + offset[at]).astype(BF16).astype(F32))
+                rows.append(leaky(raw * scale[at] + offset[at]).astype(BF16))
             for j, v in enumerate(block_swap(rows)):
-                fixed[j, part * 16:(part + 1) * 16, g * 128:(g + 1) * 128] = v.astype(BF16)
-                norms[j] = norms[j] + v * v
+                fixed[j, part * 16:(part + 1) * 16, g * 128:(g + 1) * 128] = v
+                norms[j] = norms[j] + v.astype(F32) * v.astype(F32)
         for j in range(16):
             norm = -0.5 * jnp.sum(norms[j], axis=0, keepdims=True)
             hi = norm.astype(BF16).astype(F32)
             mid = (norm - hi).astype(BF16).astype(F32)
             end = jnp.where(row16f < 3, -0.5, jnp.where(row16f == 3, hi, jnp.where(row16f == 4, mid, jnp.where(row16f == 5, norm - hi - mid, 0.0))))
-            fixed[j, 112:128, g * 128:(g + 1) * 128] = end.astype(BF16)
+            fixed[j, 64:80, g * 128:(g + 1) * 128] = end.astype(BF16)
 
     factor = sharp_ref[0] * (2.0 * LOG2E / ch)
     count = wide * 16
@@ -663,7 +632,7 @@
                 out_ref[comp, 4 * g + q // 4, pl.ds(q % 4, 1), :] = v[comp:comp + 1]
 
 
-def match(edge, side, moving, fixed, sums, par, place, sharpness, slab, strip):
+def match(edge, side, raw, sums, par, place, sharpness, slab, strip):
     tall, wide = slab + 2 * RADIUS, strip + 2 * RADIUS
     groups = slab // 4
     vm = pl.BlockSpec(memory_space=pltpu.VMEM)
@@ -672,13 +641,12 @@
     return pl.pallas_call(
         functools.partial(match_kernel, slab, strip),
         out_shape=jax.ShapeDtypeStruct((3, slab, strip, 128), F32),
-        in_specs=[hbm] * 4 + [vm, vm, sm, sm],
+        in_specs=[hbm] * 3 + [vm, vm, sm, sm],
         out_specs=vm,
         scratch_shapes=[
             pltpu.VMEM(edge.shape, F32),
             pltpu.VMEM(side.shape, F32),
-            pltpu.VMEM(moving.shape, F32),
-            pltpu.VMEM(fixed.shape, F32),
+            pltpu.VMEM(raw.shape, F32),
             pltpu.VMEM((2, 136, 128), F32),
             pltpu.VMEM((tall, wide, 128, 128), BF16),
             pltpu.VMEM((tall, wide, 128, 128), BF16),
@@ -689,11 +657,10 @@
             pltpu.SemaphoreType.DMA((2 * RADIUS,)),
             pltpu.SemaphoreType.DMA((slab,)),
             pltpu.SemaphoreType.DMA((slab,)),
-            pltpu.SemaphoreType.DMA(()),
         ],
         compiler_params=pltpu.CompilerParams(vmem_limit_bytes=60 * 1024 * 1024),
         name="match",
-    )(edge, side, moving, fixed, sums, par, place, sharpness)
+    )(edge, side, raw, sums, par, place, sharpness)
 
 
 def gathered(fixed_image, moving_image):
@@ -725,10 +692,10 @@
     own = restored(blocks)
     mine = moments(own, pairs, par, depth, height, slab, strip)
     theirs = lax.ppermute(mine, "depth", swap)
-    moving, fixed, sums = encode(own, other, mine, theirs, base, two, place, depth, height, slab, strip)
+    raw, sums = encode(own, other, mine, theirs, base, two, place, depth, height, slab, strip)
     sums = lax.all_to_all(sums, AXES, 0, 0)
     edge, side = rim(own, other, mine, theirs, base, two, place, depth, height, slab, strip)
-    return match(edge, side, moving, fixed, sums, par, place, sharpness, slab, strip)
+    return match(edge, side, raw, sums, par, place, sharpness, slab, strip)
 
 
 def solution(mesh):

time: 71 us -> 68.7 us (0.968)
  waiting for transfers between devices: 4.59 us -> 7.24 us
  local copies, waits for them, and re-layouts: 6.17 us -> 4.32 us
  Pallas kernels: 42.7 us -> 41.1 us
  other arithmetic: 4.53 us -> 3.05 us
    all_to_all x1, waiting for transfers between devices: 4.59 us -> 6.44 us  [gathered(): lax.all_to_all(sent.reshape((depth * height,) + sent.shape[3:]), AXES, 0, 0)]
    mul x2, other arithmetic: 0.94 us -> 0.12 us  [restored(): return blocks[:, :-8].astype(F32) * power]
    pallas_call x1, Pallas kernels: 9.77 us -> 8.95 us  [encode(): pl.pallas_call(functools.partial(encode_kernel, nd, nh, slab, strip), out...]
    pallas_call x1, Pallas kernels: 12 us -> 11.2 us  [rim(): pl.pallas_call(functools.partial(rim_kernel, nd, nh, slab, strip), out_sh...]
    ppermute x1, waiting for transfers between devices: 0.01 us -> 0.8 us  [local(): theirs = lax.ppermute(mine, 'depth', swap)]
    reshape x3, local copies, waits for them, and re-layouts: 2.37 us -> 1.65 us  [parameters(): conv_two.reshape(3, 3, 3, 64, 64).transpose(2, 4, 0, 1, 3).reshape(192, 576)]
  transfers between devices with their start and end apart: 4 -> 4, of which waited for: 1 -> 2; matrix products, arithmetic and copies ran while one was open for 11% -> 7% of each run, Pallas kernels for 24% -> 24%
where the time goes in v3:
time: 68.7 us; the launch traced here: 68 us
  Pallas kernels  41.1 us (60%)
  starting transfers between devices  10.5 us (15%)
  waiting for transfers between devices  7.24 us (11%)
  local copies, waits for them, and re-layouts  4.32 us (6%)
  other arithmetic  3.05 us (4%)
  between operations  0.97 us (1%)
  matrix products  0.82 us (1%)
    pallas_call x1, Pallas kernels, match(): pl.pallas_call(functools.partial(match_kernel, slab, strip), out_shape=ja...  15.9 us
    pallas_call x1, Pallas kernels, rim(): pl.pallas_call(functools.partial(rim_kernel, nd, nh, slab, strip), out_sh...  11.2 us
    pallas_call x1, Pallas kernels, encode(): pl.pallas_call(functools.partial(encode_kernel, nd, nh, slab, strip), out...  8.95 us
    all_to_all x1, starting transfers between devices, gathered(): lax.all_to_all(sent.reshape((depth * height,) + sent.shape[3:]), AXES, 0, 0)  7.3 us
    all_to_all x1, waiting for transfers between devices, gathered(): lax.all_to_all(sent.reshape((depth * height,) + sent.shape[3:]), AXES, 0, 0)  6.44 us
    pallas_call x1, Pallas kernels, moments(): pl.pallas_call(functools.partial(moments_kernel, nd, nh, slab, strip), ou...  5.01 us
    all_to_all x1, starting transfers between devices, local(): sums = lax.all_to_all(sums, AXES, 0, 0)  2.59 us
    reshape x3, local copies, waits for them, and re-layouts, parameters(): conv_two.reshape(3, 3, 3, 64, 64).transpose(2, 4, 0, 1, 3).reshape(192, 576)  1.65 us
  transfers between devices with their start and end apart: 4, of which 2 were waited for; matrix products, arithmetic and copies ran while one was open for 7% of the time, Pallas kernels for 24%

profile of v3, /device:TPU:0, one launch (start us, length us, event | category | flops | bytes accessed | tf_op | source)
XLA Modules:
  0.0 68.0 jit_solution(3760177412561065622)
XLA Ops:
  0.0 0.0 copy-start.3
  0.0 0.9 %abs_reduce_fusion = f32[2]{0:T(128)S(1)} fusion(f32[1,32,128]{2,1,0:T(8,128)} %bitcast.37, f32[1,32,128]{2,1,0:T(8,128)} %bitcast.39), kind=kLoop, calls=%fused_computation.7 | loop fusion | flops 24574 | bytes 32776 | tf_op jit(solution)/shard_map/reduce_max | solution.py:670
  0.9 0.8 %fusion = f32[2,32,128]{2,1,0:T(8,128)S(1)} fusion(f32[1,32,128]{2,1,0:T(8,128)} %bitcast.38, f32[1,32,128]{2,1,0:T(8,128)} %bitcast.40, f32[2]{0:T(128)S(1)} %get-tuple-element.13), kind=kLoop, calls=%fused_computation.8 | loop fusion | flops 16384 | bytes 65544 | tf_op jit(solution)/shard_map/mul | solution.py:671
  1.7 0.1 select_convert_fusion
  1.8 0.8 %broadcast_in_dim.22 = f16[2,2,8,40,128]{4,3,2,1,0:T(8,128)(2,1)} broadcast(f16[2,40,128]{2,1,0:T(8,128)(2,1)S(1)} %select_convert_fusion), dimensions={1,3,4} | broadcast | bytes 348160 | tf_op jit(solution)/shard_map/broadcast_in_dim | solution.py:674
  2.6 7.3 %all-to-all-start = ((f16[32,40,128]{2,1,0:T(8,128)(2,1)}), f16[32,40,128]{2,1,0:T(8,128)(2,1)S(1)}, u32[]{:S(2)}, u32[]{:S(2)}) async-start(f16[32,40,128]{2,1,0:T(8,128)(2,1)} %bitcast.2), calls=%async_computation | async-start | bytes 655360 | tf_op jit(solution)/shard_map/all_to_all | solution.py:675
  9.9 0.8 %reduce = f32[64,3,3,3]{0,3,2,1:T(4,128)S(1)} reduce(f32[64,1,3,3,3]{0,1,4,3,2:T(1,128)} %param.12, f32[]{:T(128)} %constant.56), dimensions={1}, to_apply=%param.12.reduce_sub_computation | reduce | bytes 13828 | tf_op args[2]
  10.7 0.0 copy-start.5
  10.7 0.0 copy-start.6
  10.7 0.0 copy-start.2
  10.8 0.1 copy.14
  10.8 0.8 %copy.25 = f32[64,1,3,3,3]{0,3,4,2,1:T(4,128)S(1)} copy(f32[64,1,3,3,3]{0,1,4,3,2:T(1,128)} %param.12) | data formatting | bytes 13824 | tf_op jit(solution)/shard_map/transpose | solution.py:402
  11.7 0.0 copy-done.3
  11.7 0.0 copy-start.7
  11.7 0.0 copy-start.8
  11.7 0.4 reshape.51
  12.1 0.8 %copy.19 = bf16[3,3,3,64,64]{3,1,0,4,2:T(4,128)(2,1)S(1)} copy(bf16[3,3,3,64,64]{4,3,2,1,0:T(8,128)(2,1)S(1)} %reshape.51) | data formatting | bytes 442368 | tf_op jit(solution)/shard_map/reshape | solution.py:408
  13.0 0.4 reshape.52.two_ref
  13.4 0.1 copy.16
  13.5 0.1 pad.28.clone
  13.6 0.1 pad.13.clone
  14.3 0.0 copy-done.5
  14.3 0.0 copy-done.6
  14.3 0.1 maximum_bitcast_fusion
  14.4 0.0 copy-done.2
  14.4 0.8 %fusion.5 = f32[64,256]{1,0:T(8,128)S(1)} fusion(f32[64,729]{0,1:T(8,128)S(1)} %mul.65, f32[729,256]{1,0:T(8,128)S(1)} %copy-done.2), kind=kOutput, calls=%fused_computation.24 | convolution fusion | flops 143327232 | bytes 998656 | tf_op jit(solution)/shard_map/dot_general | solution.py:406
  15.2 0.1 stack.55.place_ref
  15.3 0.0 copy-done.7
  15.3 0.0 copy-done.8
  15.3 0.0 copy-start.1
  15.3 0.1 maximum_bitcast_fusion.2
  15.4 0.0 copy-start
  15.5 0.1 maximum_maximum_fusion.taps_ref
  15.6 6.4 %all-to-all-done = f16[32,40,128]{2,1,0:T(8,128)(2,1)S(1)} async-done(((f16[32,40,128]{2,1,0:T(8,128)(2,1)}), f16[32,40,128]{2,1,0:T(8,128)(2,1)S(1)}, u32[]{:S(2)}, u32[]{:S(2)}) %all-to-all-start) | async-done | bytes 327712 | tf_op jit(solution)/shard_map/all_to_all | solution.py:675
  22.0 0.1 collective-permute-start
  22.1 0.1 convert_multiply_fusion.1.own_ref
  22.2 5.0 %moments.1.mine_ref = f32[128,128]{1,0:T(8,128)S(1)} custom-call(f32[32,32,128]{2,1,0:T(8,128)S(1)} %convert_multiply_fusion.1.own_ref, f32[64,288]{1,0:T(8,128)S(1)} %maximum_maximum_fusion.1.pairs_ref, f32[4,128]{1,0:T(4,128)S(1)} %pad_maximum_fusion.1.par_ref), custom_call_target="tpu_custom_call" | custom-call | flops 1000000000 | bytes 1000000 | tf_op jit(solution)/shard_map/moments/pallas_call | solution.py:176
  27.2 0.0 copy-done
  27.2 0.6 collective-permute-start.1
  27.8 0.0 collective-permute-done
  27.8 0.1 convert_multiply_fusion.other_ref
  27.9 0.8 %collective-permute-done.1.theirs_ref = f32[128,128]{1,0:T(8,128)S(1)} collective-permute-done((f32[128,128]{1,0:T(8,128)S(1)}, f32[128,128]{1,0:T(8,128)S(1)}, u32[]{:S(2)}, u32[]{:S(2)}) %collective-permute-start.1) | collective-permute-done | bytes 65568 | tf_op jit(solution)/shard_map/ppermute | solution.py:694
  28.7 9.0 %encode.1 = (f32[8,2,64,512]{3,2,1,0:T(8,128)}, f32[32,2,128]{2,1,0:T(2,128)}) custom-call(f32[32,32,128]{2,1,0:T(8,128)S(1)} %convert_multiply_fusion.1.own_ref, f32[32,32,128]{2,1,0:T(8,128)S(1)} %convert_multiply_fusion.other_ref, f32[128,128]{1,0:T(8,128)S(1)} %moments.1.mine_ref, f32[128,128]{1,0:T(8,128)S(1)} %collective-permute-done.1.theirs_ref, ...), custom_call_target="tpu_custom_call" | custom-call | tf_op jit(solution)/shard_map/encode/pallas_call | solution.py:309
  37.6 2.6 %all-to-all-start.1 = ((f32[32,2,128]{2,1,0:T(2,128)}), f32[32,2,128]{2,1,0:T(2,128)S(1)}, u32[]{:S(2)}, u32[]{:S(2)}) async-start(f32[32,2,128]{2,1,0:T(2,128)} %get-tuple-element.12), calls=%async_computation.1 | async-start | bytes 65536 | tf_op jit(solution)/shard_map/all_to_all | solution.py:696
  40.2 0.0 copy-done.1
  40.2 11.2 %rim.1 = (f32[6,64,1280]{2,1,0:T(8,128)}, f32[8,64,768]{2,1,0:T(8,128)}) custom-call(f32[32,32,128]{2,1,0:T(8,128)S(1)} %convert_multiply_fusion.1.own_ref, f32[32,32,128]{2,1,0:T(8,128)S(1)} %convert_multiply_fusion.other_ref, f32[128,128]{1,0:T(8,128)S(1)} %moments.1.mine_ref, f32[128,128]{1,0:T(8,128)S(1)} %collective-permute-done.1.theirs_ref, ...), custom_call_target="tpu_custom_call" | custom-call | flops 6000000000 | bytes 10000000 | tf_op jit(solution)/shard_map/rim/pallas_call | solution.py:378
  51.5 0.0 all-to-all-done.1.sums_ref
  51.5 0.0 copy-start.4
  51.5 0.6 copy-done.4
  52.1 15.9 %match.1 = f32[3,8,4,128]{3,2,1,0:T(4,128)} custom-call(f32[6,64,1280]{2,1,0:T(8,128)} %get-tuple-element.9.edge_hbm, f32[8,64,768]{2,1,0:T(8,128)} %get-tuple-element.10.side_hbm, f32[8,2,64,512]{3,2,1,0:T(8,128)} %get-tuple-element.11.raw_hbm, f32[32,2,128]{2,1,0:T(2,128)} %copy-done.4, f32[4,128]{1,0:T(4,128)} %copy-done, s32[7]{0:T(128)} %copy-done.1, ...), custom_call_target="tpu_custom_call" | custom-call | tf_op jit(solution)/shard_map/match/pallas_call | solution.py:641
  (13 shorter events, 0.2 us)
Async XLA Ops:
  0.0 11.7 %copy-start.3 = (bf16[27,4096]{1,0:T(8,128)(2,1)S(1)}, bf16[27,4096]{1,0:T(8,128)(2,1)}, u32[]{:S(2)}) copy-start(bf16[27,4096]{1,0:T(8,128)(2,1)} %param.15) | copy-start | bytes 663556
  2.6 19.4 %all-to-all-start = ((f16[32,40,128]{2,1,0:T(8,128)(2,1)}), f16[32,40,128]{2,1,0:T(8,128)(2,1)S(1)}, u32[]{:S(2)}, u32[]{:S(2)}) async-start(f16[32,40,128]{2,1,0:T(8,128)(2,1)} %bitcast.2), calls=%async_computation | async-start | bytes 655360 | tf_op jit(solution)/shard_map/all_to_all | solution.py:675
  10.7 3.6 %copy-start.5 = (f32[64]{0:T(128)S(1)}, f32[64]{0:T(128)}, u32[]{:S(2)}) copy-start(f32[64]{0:T(128)} %param.13) | copy-start | bytes 772
  10.7 3.6 %copy-start.6 = (f32[64]{0:T(128)S(1)}, f32[64]{0:T(128)}, u32[]{:S(2)}) copy-start(f32[64]{0:T(128)} %param.14) | copy-start | bytes 772
  10.7 3.7 %copy-start.2 = (f32[729,256]{1,0:T(8,128)S(1)}, f32[729,256]{1,0:T(8,128)}, u32[]{:S(2)}) copy-start(f32[729,256]{1,0:T(8,128)} %constant.49.clone) | copy-start | bytes 2239492
  11.7 3.7 %copy-start.7 = (f32[64]{0:T(128)S(1)}, f32[64]{0:T(128)}, u32[]{:S(2)}) copy-start(f32[64]{0:T(128)} %param.16) | copy-start | bytes 772
  11.7 3.6 %copy-start.8 = (f32[64]{0:T(128)S(1)}, f32[64]{0:T(128)}, u32[]{:S(2)}) copy-start(f32[64]{0:T(128)} %param.17) | copy-start | bytes 772
  15.3 24.9 %copy-start.1 = (s32[7]{0:T(128)}, s32[7]{0:T(128)S(1)}, u32[]{:S(2)}) copy-start(s32[7]{0:T(128)S(1)} %stack.55.place_ref) | copy-start | bytes 88
  15.4 11.8 %copy-start = (f32[4,128]{1,0:T(4,128)}, f32[4,128]{1,0:T(4,128)S(1)}, u32[]{:S(2)}) copy-start(f32[4,128]{1,0:T(4,128)S(1)} %pad_maximum_fusion.1.par_ref) | copy-start | bytes 6148
  22.0 5.7 %collective-permute-start = (f16[32,40,128]{2,1,0:T(8,128)(2,1)S(1)}, f16[32,40,128]{2,1,0:T(8,128)(2,1)S(1)}, u32[]{:S(2)}, u32[]{:S(2)}) collective-permute-start(f16[32,40,128]{2,1,0:T(8,128)(2,1)S(1)} %all-to-all-done), channel_id=1, source_target_pairs={{0,8},{8,0},{16,24},{24,16},{1,9},{9,1},{17,25},{25,17},{2,10},{10... | collective-permute-start | bytes 983048 | tf_op jit(solution)/shard_map/ppermute | solution.py:691
  27.2 1.5 %collective-permute-start.1 = (f32[128,128]{1,0:T(8,128)S(1)}, f32[128,128]{1,0:T(8,128)S(1)}, u32[]{:S(2)}, u32[]{:S(2)}) collective-permute-start(f32[128,128]{1,0:T(8,128)S(1)} %moments.1.mine_ref), channel_id=1, source_target_pairs={{0,8},{8,0},{16,24},{24,16},{1,9},{9,1},{17,25},{25,17},{2,10},{10... | collective-permute-start | bytes 196616 | tf_op jit(solution)/shard_map/ppermute | solution.py:694
  37.6 13.8 %all-to-all-start.1 = ((f32[32,2,128]{2,1,0:T(2,128)}), f32[32,2,128]{2,1,0:T(2,128)S(1)}, u32[]{:S(2)}, u32[]{:S(2)}) async-start(f32[32,2,128]{2,1,0:T(2,128)} %get-tuple-element.12), calls=%async_computation.1 | async-start | bytes 65536 | tf_op jit(solution)/shard_map/all_to_all | solution.py:696
  51.5 0.6 copy-start.4

commit v4 on v3

--- a/solution.py
+++ b/solution.py
@@ -189,11 +189,6 @@
     )(own, pairs, par)
 
 
-def convolved(weights, feat, z, first, wide, lane64):
-    taps = [feat[z + a, :, 128 * (f + b):128 * (f + b + n)] for a in range(3) for b in range(3) for f, n in [(first, wide)]]
-    return joined(weights, jnp.concatenate(taps, axis=0), wide, lane64)
-
-
 def joined(weights, taps, wide, lane64):
     raw = jnp.dot(weights, taps, preferred_element_type=F32)
     rows = []
@@ -222,6 +217,7 @@
     lane = lax.broadcasted_iota(jnp.int32, (16, 128), 1)
     reach = -(-(near + 1) // strip)
     for s, scan in enumerate(scans):
+        win[s, :, 16:24, :] = jnp.zeros((3 * slab, 8, 128), F32)
         mine = core == scan
         for i in range(-1, 2):
             for j in range(-reach, reach + 1):
@@ -271,29 +267,30 @@
                   raw_hbm, sums_ref, win, toep, plane_hi, plane_lo, feat, raw, sem):
     rows = strip + 2
     banded(taps_ref, toep, rows)
-    first_layer((0, 1), slab, strip, 1, 2, nd, nh, own_ref, other_ref, mine_ref, theirs_ref, place_ref, win, toep, plane_hi, plane_lo, feat)
+    first_layer((0, 1), slab, strip, 1, 5, nd, nh, own_ref, other_ref, mine_ref, theirs_ref, place_ref, win, toep, plane_hi, plane_lo, feat)
     lane64 = lax.broadcasted_iota(jnp.int32, (64, 128), 1)
     zero = jnp.zeros((64, 128), F32)
 
     def store(z):
         return pltpu.make_async_copy(raw.at[z], raw_hbm.at[z], sem.at[z])
 
-    def plane(z, state):
+    def plane(i, state):
         state = list(state)
         taps = []
         for a in range(3):
             for b in range(3):
-                cuts = [feat[z + a, :, 128 * (s * rows + b):128 * (s * rows + b + strip)] for s in range(2)]
+                cuts = [feat[4 * i + u + a, :, 128 * (s * rows + b):128 * (s * rows + b + strip)] for u in range(4) for s in range(2)]
                 taps.append(jnp.concatenate(cuts, axis=1))
-        for i, v in enumerate(joined(two_ref[...], jnp.concatenate(taps, axis=0), 2 * strip, lane64)):
-            s, y = i // strip, i % strip
-            raw[z, s, :, 128 * y:128 * y + 128] = v
+        for n, v in enumerate(joined(two_ref[...], jnp.concatenate(taps, axis=0), 8 * strip, lane64)):
+            u, s, y = n // (2 * strip), n // strip % 2, n % strip
+            raw[4 * i + u, s, :, 128 * y:128 * y + 128] = v
             state[s] = state[s] + v
             state[2 + s] = state[2 + s] + v * v
-        store(z).start()
+        for u in range(4):
+            store(4 * i + u).start()
         return tuple(state)
 
-    sums = lax.fori_loop(0, slab, plane, (zero,) * 4)
+    sums = lax.fori_loop(0, slab // 4, plane, (zero,) * 4)
     total = jnp.sum(jnp.concatenate(sums[0:2], axis=0).T, axis=0, keepdims=True)
     square = jnp.sum(jnp.concatenate(sums[2:4], axis=0).T, axis=0, keepdims=True)
     both = jnp.concatenate([total, square], axis=0)
@@ -333,7 +330,7 @@
     lane64 = lax.broadcasted_iota(jnp.int32, (64, 128), 1)
     wide = strip + 6
     banded(taps_ref, toep, strip + 8)
-    first_layer((1,), slab, strip, 4, 4, nd, nh, own_ref, other_ref, mine_ref, theirs_ref, place_ref, win, toep, plane_hi, plane_lo, feat)
+    first_layer((1,), slab, strip, 4, 8, nd, nh, own_ref, other_ref, mine_ref, theirs_ref, place_ref, win, toep, plane_hi, plane_lo, feat)
 
     def store_edge(i):
         return pltpu.make_async_copy(edge.at[i], edge_ref.at[i], edge_sem.at[i])
@@ -342,27 +339,33 @@
         return pltpu.make_async_copy(side.at[i], side_ref.at[i], side_sem.at[i])
 
     def whole(i, _):
-        z = jnp.where(i < RADIUS, i, i + slab)
-        for y, v in enumerate(convolved(two_ref[...], feat, z, 0, wide, lane64)):
-            edge[i, :, 128 * y:128 * y + 128] = v
-        store_edge(i).start()
-        return _
-
-    def middle(i, _):
-        z = RADIUS + 2 * i
+        at = [jnp.where(n < RADIUS, n, n + slab) for n in (2 * i, 2 * i + 1)]
         taps = []
         for a in range(3):
             for b in range(3):
-                cuts = [feat[z + u + a, :, 128 * (c + b):128 * (c + b + 3)] for u in range(2) for c in (0, strip + 3)]
+                taps.append(jnp.concatenate([feat[z + a, :, 128 * b:128 * (b + wide)] for z in at], axis=1))
+        for n, v in enumerate(joined(two_ref[...], jnp.concatenate(taps, axis=0), 2 * wide, lane64)):
+            y = n % wide
+            edge[2 * i + n // wide, :, 128 * y:128 * y + 128] = v
+        store_edge(2 * i).start()
+        store_edge(2 * i + 1).start()
+        return _
+
+    def middle(i, _):
+        z = RADIUS + 4 * i
+        taps = []
+        for a in range(3):
+            for b in range(3):
+                cuts = [feat[z + u + a, :, 128 * (c + b):128 * (c + b + 3)] for u in range(4) for c in (0, strip + 3)]
                 taps.append(jnp.concatenate(cuts, axis=1))
-        for y, v in enumerate(joined(two_ref[...], jnp.concatenate(taps, axis=0), 12, lane64)):
-            side[2 * i + y // 6, :, 128 * (y % 6):128 * (y % 6) + 128] = v
-        store_side(2 * i).start()
-        store_side(2 * i + 1).start()
+        for y, v in enumerate(joined(two_ref[...], jnp.concatenate(taps, axis=0), 24, lane64)):
+            side[4 * i + y // 6, :, 128 * (y % 6):128 * (y % 6) + 128] = v
+        for u in range(4):
+            store_side(4 * i + u).start()
         return _
 
-    lax.fori_loop(0, 2 * RADIUS, whole, 0)
-    lax.fori_loop(0, slab // 2, middle, 0)
+    lax.fori_loop(0, RADIUS, whole, 0)
+    lax.fori_loop(0, slab // 4, middle, 0)
     for i in range(2 * RADIUS):
         store_edge(i).wait()
     for i in range(slab):
@@ -492,7 +495,7 @@
             mid = (norm - hi).astype(BF16).astype(F32)
             low = norm - hi - mid
             extra = jnp.where(sub8 == 0, hi, jnp.where(sub8 == 1, mid, jnp.where(sub8 == 2, low, 0.0)))
-            turned[y % 2, 4:132, 0:72] = jnp.concatenate([f, extra], axis=0).T
+            turned[y % 2, 4:132, 0:80] = jnp.concatenate([f, extra, blank], axis=0).astype(BF16).T.astype(F32)
             ones = jnp.where((col16 == 96 + y) | (col16 == 112 + z), 1.0, onehot_x).astype(BF16)[None]
             even[z, y] = (turned[y % 2, 0:128].astype(BF16).reshape(8, 16, 128) + ones).reshape(128, 128)
             odd[z, y] = (turned[y % 2, 8:136].astype(BF16).reshape(8, 16, 128) + ones).reshape(128, 128)

time: 68.7 us -> 64.6 us (0.940)
  Pallas kernels: 41.1 us -> 36.9 us
    pallas_call x1, Pallas kernels: 8.95 us -> 6.95 us  [encode(): pl.pallas_call(functools.partial(encode_kernel, nd, nh, slab, strip), out...]
    pallas_call x1, Pallas kernels: 11.2 us -> 9.59 us  [rim(): pl.pallas_call(functools.partial(rim_kernel, nd, nh, slab, strip), out_sh...]
  transfers between devices with their start and end apart: 4 -> 4, of which waited for: 2 -> 2; matrix products, arithmetic and copies ran while one was open for 7% -> 8% of each run, Pallas kernels for 24% -> 23%
where the time goes in v4:
time: 64.6 us; the launch traced here: 63.8 us
  Pallas kernels  36.9 us (57%)
  starting transfers between devices  10.5 us (16%)
  waiting for transfers between devices  7.24 us (11%)
  local copies, waits for them, and re-layouts  4.32 us (7%)
  other arithmetic  3.05 us (5%)
  between operations  0.97 us (2%)
  matrix products  0.82 us (1%)
    pallas_call x1, Pallas kernels, match(): pl.pallas_call(functools.partial(match_kernel, slab, strip), out_shape=ja...  15.3 us
    pallas_call x1, Pallas kernels, rim(): pl.pallas_call(functools.partial(rim_kernel, nd, nh, slab, strip), out_sh...  9.59 us
    all_to_all x1, starting transfers between devices, gathered(): lax.all_to_all(sent.reshape((depth * height,) + sent.shape[3:]), AXES, 0, 0)  7.3 us
    pallas_call x1, Pallas kernels, encode(): pl.pallas_call(functools.partial(encode_kernel, nd, nh, slab, strip), out...  6.95 us
    all_to_all x1, waiting for transfers between devices, gathered(): lax.all_to_all(sent.reshape((depth * height,) + sent.shape[3:]), AXES, 0, 0)  6.44 us
    pallas_call x1, Pallas kernels, moments(): pl.pallas_call(functools.partial(moments_kernel, nd, nh, slab, strip), ou...  5.01 us
    all_to_all x1, starting transfers between devices, local(): sums = lax.all_to_all(sums, AXES, 0, 0)  2.59 us
    reshape x3, local copies, waits for them, and re-layouts, parameters(): conv_two.reshape(3, 3, 3, 64, 64).transpose(2, 4, 0, 1, 3).reshape(192, 576)  1.65 us
  transfers between devices with their start and end apart: 4, of which 2 were waited for; matrix products, arithmetic and copies ran while one was open for 8% of the time, Pallas kernels for 23%

profile of v4, /device:TPU:0, one launch (start us, length us, event | category | flops | bytes accessed | tf_op | source)
XLA Modules:
  0.0 63.8 jit_solution(10951956345122618086)
XLA Ops:
  0.0 0.0 copy-start.3
  0.0 0.9 %abs_reduce_fusion = f32[2]{0:T(128)S(1)} fusion(f32[1,32,128]{2,1,0:T(8,128)} %bitcast.37, f32[1,32,128]{2,1,0:T(8,128)} %bitcast.39), kind=kLoop, calls=%fused_computation.7 | loop fusion | flops 24574 | bytes 32776 | tf_op jit(solution)/shard_map/reduce_max | solution.py:673
  0.9 0.8 %fusion = f32[2,32,128]{2,1,0:T(8,128)S(1)} fusion(f32[1,32,128]{2,1,0:T(8,128)} %bitcast.38, f32[1,32,128]{2,1,0:T(8,128)} %bitcast.40, f32[2]{0:T(128)S(1)} %get-tuple-element.13), kind=kLoop, calls=%fused_computation.8 | loop fusion | flops 16384 | bytes 65544 | tf_op jit(solution)/shard_map/mul | solution.py:674
  1.7 0.1 select_convert_fusion
  1.8 0.8 %broadcast_in_dim.22 = f16[2,2,8,40,128]{4,3,2,1,0:T(8,128)(2,1)} broadcast(f16[2,40,128]{2,1,0:T(8,128)(2,1)S(1)} %select_convert_fusion), dimensions={1,3,4} | broadcast | bytes 348160 | tf_op jit(solution)/shard_map/broadcast_in_dim | solution.py:677
  2.6 7.3 %all-to-all-start = ((f16[32,40,128]{2,1,0:T(8,128)(2,1)}), f16[32,40,128]{2,1,0:T(8,128)(2,1)S(1)}, u32[]{:S(2)}, u32[]{:S(2)}) async-start(f16[32,40,128]{2,1,0:T(8,128)(2,1)} %bitcast.2), calls=%async_computation | async-start | bytes 655360 | tf_op jit(solution)/shard_map/all_to_all | solution.py:678
  9.9 0.8 %reduce = f32[64,3,3,3]{0,3,2,1:T(4,128)S(1)} reduce(f32[64,1,3,3,3]{0,1,4,3,2:T(1,128)} %param.12, f32[]{:T(128)} %constant.56), dimensions={1}, to_apply=%param.12.reduce_sub_computation | reduce | bytes 13828 | tf_op args[2]
  10.7 0.0 copy-start.5
  10.7 0.0 copy-start.6
  10.7 0.0 copy-start.2
  10.8 0.1 copy.14
  10.8 0.8 %copy.25 = f32[64,1,3,3,3]{0,3,4,2,1:T(4,128)S(1)} copy(f32[64,1,3,3,3]{0,1,4,3,2:T(1,128)} %param.12) | data formatting | bytes 13824 | tf_op jit(solution)/shard_map/transpose | solution.py:405
  11.7 0.0 copy-done.3
  11.7 0.0 copy-start.7
  11.7 0.0 copy-start.8
  11.7 0.4 reshape.51
  12.1 0.8 %copy.19 = bf16[3,3,3,64,64]{3,1,0,4,2:T(4,128)(2,1)S(1)} copy(bf16[3,3,3,64,64]{4,3,2,1,0:T(8,128)(2,1)S(1)} %reshape.51) | data formatting | bytes 442368 | tf_op jit(solution)/shard_map/reshape | solution.py:411
  13.0 0.4 reshape.52.two_ref
  13.4 0.1 copy.16
  13.5 0.1 pad.28.clone
  13.6 0.1 pad.13.clone
  14.3 0.0 copy-done.5
  14.3 0.0 copy-done.6
  14.3 0.1 maximum_bitcast_fusion
  14.4 0.0 copy-done.2
  14.4 0.8 %fusion.5 = f32[64,256]{1,0:T(8,128)S(1)} fusion(f32[64,729]{0,1:T(8,128)S(1)} %mul.65, f32[729,256]{1,0:T(8,128)S(1)} %copy-done.2), kind=kOutput, calls=%fused_computation.24 | convolution fusion | flops 143327232 | bytes 998656 | tf_op jit(solution)/shard_map/dot_general | solution.py:409
  15.2 0.1 stack.55.place_ref
  15.3 0.0 copy-done.7
  15.3 0.0 copy-done.8
  15.3 0.0 copy-start.1
  15.3 0.1 maximum_bitcast_fusion.2
  15.4 0.0 copy-start
  15.5 0.1 maximum_maximum_fusion.taps_ref
  15.6 6.4 %all-to-all-done = f16[32,40,128]{2,1,0:T(8,128)(2,1)S(1)} async-done(((f16[32,40,128]{2,1,0:T(8,128)(2,1)}), f16[32,40,128]{2,1,0:T(8,128)(2,1)S(1)}, u32[]{:S(2)}, u32[]{:S(2)}) %all-to-all-start) | async-done | bytes 327712 | tf_op jit(solution)/shard_map/all_to_all | solution.py:678
  22.0 0.1 collective-permute-start
  22.1 0.1 convert_multiply_fusion.1.own_ref
  22.2 5.0 %moments.1.mine_ref = f32[128,128]{1,0:T(8,128)S(1)} custom-call(f32[32,32,128]{2,1,0:T(8,128)S(1)} %convert_multiply_fusion.1.own_ref, f32[64,288]{1,0:T(8,128)S(1)} %maximum_maximum_fusion.1.pairs_ref, f32[4,128]{1,0:T(4,128)S(1)} %pad_maximum_fusion.1.par_ref), custom_call_target="tpu_custom_call" | custom-call | flops 1000000000 | bytes 1000000 | tf_op jit(solution)/shard_map/moments/pallas_call | solution.py:176
  27.2 0.0 copy-done
  27.2 0.6 collective-permute-start.1
  27.8 0.0 collective-permute-done
  27.8 0.1 convert_multiply_fusion.other_ref
  27.9 0.8 %collective-permute-done.1.theirs_ref = f32[128,128]{1,0:T(8,128)S(1)} collective-permute-done((f32[128,128]{1,0:T(8,128)S(1)}, f32[128,128]{1,0:T(8,128)S(1)}, u32[]{:S(2)}, u32[]{:S(2)}) %collective-permute-start.1) | collective-permute-done | bytes 65568 | tf_op jit(solution)/shard_map/ppermute | solution.py:697
  28.7 7.0 %encode.1 = (f32[8,2,64,512]{3,2,1,0:T(8,128)}, f32[32,2,128]{2,1,0:T(2,128)}) custom-call(f32[32,32,128]{2,1,0:T(8,128)S(1)} %convert_multiply_fusion.1.own_ref, f32[32,32,128]{2,1,0:T(8,128)S(1)} %convert_multiply_fusion.other_ref, f32[128,128]{1,0:T(8,128)S(1)} %moments.1.mine_ref, f32[128,128]{1,0:T(8,128)S(1)} %collective-permute-done.1.theirs_ref, ...), custom_call_target="tpu_custom_call" | custom-call | tf_op jit(solution)/shard_map/encode/pallas_call | solution.py:306
  35.6 2.6 %all-to-all-start.1 = ((f32[32,2,128]{2,1,0:T(2,128)}), f32[32,2,128]{2,1,0:T(2,128)S(1)}, u32[]{:S(2)}, u32[]{:S(2)}) async-start(f32[32,2,128]{2,1,0:T(2,128)} %get-tuple-element.12), calls=%async_computation.1 | async-start | bytes 65536 | tf_op jit(solution)/shard_map/all_to_all | solution.py:699
  38.2 0.0 copy-done.1
  38.3 9.6 %rim.1 = (f32[6,64,1280]{2,1,0:T(8,128)}, f32[8,64,768]{2,1,0:T(8,128)}) custom-call(f32[32,32,128]{2,1,0:T(8,128)S(1)} %convert_multiply_fusion.1.own_ref, f32[32,32,128]{2,1,0:T(8,128)S(1)} %convert_multiply_fusion.other_ref, f32[128,128]{1,0:T(8,128)S(1)} %moments.1.mine_ref, f32[128,128]{1,0:T(8,128)S(1)} %collective-permute-done.1.theirs_ref, ...), custom_call_target="tpu_custom_call" | custom-call | flops 6000000000 | bytes 10000000 | tf_op jit(solution)/shard_map/rim/pallas_call | solution.py:381
  47.9 0.0 all-to-all-done.1.sums_ref
  47.9 0.0 copy-start.4
  47.9 0.6 copy-done.4
  48.5 15.3 %match.1 = f32[3,8,4,128]{3,2,1,0:T(4,128)} custom-call(f32[6,64,1280]{2,1,0:T(8,128)} %get-tuple-element.9.edge_hbm, f32[8,64,768]{2,1,0:T(8,128)} %get-tuple-element.10.side_hbm, f32[8,2,64,512]{3,2,1,0:T(8,128)} %get-tuple-element.11.raw_hbm, f32[32,2,128]{2,1,0:T(2,128)} %copy-done.4, f32[4,128]{1,0:T(4,128)} %copy-done, s32[7]{0:T(128)} %copy-done.1, ...), custom_call_target="tpu_custom_call" | custom-call | tf_op jit(solution)/shard_map/match/pallas_call | solution.py:644
  (13 shorter events, 0.2 us)
Async XLA Ops:
  0.0 11.7 %copy-start.3 = (bf16[27,4096]{1,0:T(8,128)(2,1)S(1)}, bf16[27,4096]{1,0:T(8,128)(2,1)}, u32[]{:S(2)}) copy-start(bf16[27,4096]{1,0:T(8,128)(2,1)} %param.15) | copy-start | bytes 663556
  2.6 19.4 %all-to-all-start = ((f16[32,40,128]{2,1,0:T(8,128)(2,1)}), f16[32,40,128]{2,1,0:T(8,128)(2,1)S(1)}, u32[]{:S(2)}, u32[]{:S(2)}) async-start(f16[32,40,128]{2,1,0:T(8,128)(2,1)} %bitcast.2), calls=%async_computation | async-start | bytes 655360 | tf_op jit(solution)/shard_map/all_to_all | solution.py:678
  10.7 3.6 %copy-start.5 = (f32[64]{0:T(128)S(1)}, f32[64]{0:T(128)}, u32[]{:S(2)}) copy-start(f32[64]{0:T(128)} %param.13) | copy-start | bytes 772
  10.7 3.6 %copy-start.6 = (f32[64]{0:T(128)S(1)}, f32[64]{0:T(128)}, u32[]{:S(2)}) copy-start(f32[64]{0:T(128)} %param.14) | copy-start | bytes 772
  10.7 3.7 %copy-start.2 = (f32[729,256]{1,0:T(8,128)S(1)}, f32[729,256]{1,0:T(8,128)}, u32[]{:S(2)}) copy-start(f32[729,256]{1,0:T(8,128)} %constant.49.clone) | copy-start | bytes 2239492
  11.7 3.7 %copy-start.7 = (f32[64]{0:T(128)S(1)}, f32[64]{0:T(128)}, u32[]{:S(2)}) copy-start(f32[64]{0:T(128)} %param.16) | copy-start | bytes 772
  11.7 3.6 %copy-start.8 = (f32[64]{0:T(128)S(1)}, f32[64]{0:T(128)}, u32[]{:S(2)}) copy-start(f32[64]{0:T(128)} %param.17) | copy-start | bytes 772
  15.3 22.9 %copy-start.1 = (s32[7]{0:T(128)}, s32[7]{0:T(128)S(1)}, u32[]{:S(2)}) copy-start(s32[7]{0:T(128)S(1)} %stack.55.place_ref) | copy-start | bytes 88
  15.4 11.8 %copy-start = (f32[4,128]{1,0:T(4,128)}, f32[4,128]{1,0:T(4,128)S(1)}, u32[]{:S(2)}) copy-start(f32[4,128]{1,0:T(4,128)S(1)} %pad_maximum_fusion.1.par_ref) | copy-start | bytes 6148
  22.0 5.7 %collective-permute-start = (f16[32,40,128]{2,1,0:T(8,128)(2,1)S(1)}, f16[32,40,128]{2,1,0:T(8,128)(2,1)S(1)}, u32[]{:S(2)}, u32[]{:S(2)}) collective-permute-start(f16[32,40,128]{2,1,0:T(8,128)(2,1)S(1)} %all-to-all-done), channel_id=1, source_target_pairs={{0,8},{8,0},{16,24},{24,16},{1,9},{9,1},{17,25},{25,17},{2,10},{10... | collective-permute-start | bytes 983048 | tf_op jit(solution)/shard_map/ppermute | solution.py:694
  27.2 1.5 %collective-permute-start.1 = (f32[128,128]{1,0:T(8,128)S(1)}, f32[128,128]{1,0:T(8,128)S(1)}, u32[]{:S(2)}, u32[]{:S(2)}) collective-permute-start(f32[128,128]{1,0:T(8,128)S(1)} %moments.1.mine_ref), channel_id=1, source_target_pairs={{0,8},{8,0},{16,24},{24,16},{1,9},{9,1},{17,25},{25,17},{2,10},{10... | collective-permute-start | bytes 196616 | tf_op jit(solution)/shard_map/ppermute | solution.py:697
  35.6 12.2 %all-to-all-start.1 = ((f32[32,2,128]{2,1,0:T(2,128)}), f32[32,2,128]{2,1,0:T(2,128)S(1)}, u32[]{:S(2)}, u32[]{:S(2)}) async-start(f32[32,2,128]{2,1,0:T(2,128)} %get-tuple-element.12), calls=%async_computation.1 | async-start | bytes 65536 | tf_op jit(solution)/shard_map/all_to_all | solution.py:699
  47.9 0.6 copy-start.4

commit v5 on v4

--- a/solution.py
+++ b/solution.py
@@ -79,15 +79,15 @@
     lax.fori_loop(0, nd, gather, 0)
 
     def slide(i, _):
-        at = 4 * i
-        for u in range(4):
+        at = 8 * i
+        for u in range(8):
             v = img[2 + at + u, 8:8 + yn]
             for n, move in enumerate((-2, -1, 1, 2)):
                 kept = (side + move >= 0) & (side + move < 128)
                 slid[n, at + u, 8:8 + yn] = jnp.where(kept, pltpu.roll(v, (128 - move) % 128, 1), 0.0)
         return _
 
-    lax.fori_loop(0, zn // 4, slide, 0)
+    lax.fori_loop(0, zn // 8, slide, 0)
 
     def other(z, y, x):
         if x == 0:
@@ -129,7 +129,12 @@
     for y in range(-2, 3):
         lags = [(far, x) for far in range(3) for x in range(-2, 3) if (far, y, x) >= (0, 0, 0)]
         empty = ((nothing,) * len(lags),) * (1 if y else 3)
-        state = lax.fori_loop(0, zn, lambda z, state: products(z, y, lags, state, (0, 1, 2)), empty)
+        def several(i, state):
+            for u in range(4):
+                state = products(4 * i + u, y, lags, state, (0, 1, 2))
+            return state
+
+        state = lax.fori_loop(0, zn // 4, several, empty)
         record("a", y, lags, state, (0, 1, 2))
         if y >= 0:
             for d, z in (("f", 0), ("l", zn - 1)):

time: 64.6 us -> 63.9 us (0.989)
  Pallas kernels: 36.9 us -> 35.9 us
    pallas_call x1, Pallas kernels: 5.01 us -> 4.02 us  [moments(): pl.pallas_call(functools.partial(moments_kernel, nd, nh, slab, strip), ou...]
  transfers between devices with their start and end apart: 4 -> 4, of which waited for: 2 -> 2; matrix products, arithmetic and copies ran while one was open for 8% -> 8% of each run, Pallas kernels for 23% -> 22%
where the time goes in v5:
time: 63.9 us; the launch traced here: 63.2 us
  Pallas kernels  35.9 us (56%)
  starting transfers between devices  10.7 us (17%)
  waiting for transfers between devices  7.24 us (11%)
  local copies, waits for them, and re-layouts  4.32 us (7%)
  other arithmetic  3.05 us (5%)
  between operations  1.13 us (2%)
  matrix products  0.82 us (1%)
    pallas_call x1, Pallas kernels, match(): pl.pallas_call(functools.partial(match_kernel, slab, strip), out_shape=ja...  15.3 us
    pallas_call x1, Pallas kernels, rim(): pl.pallas_call(functools.partial(rim_kernel, nd, nh, slab, strip), out_sh...  9.59 us
    all_to_all x1, starting transfers between devices, gathered(): lax.all_to_all(sent.reshape((depth * height,) + sent.shape[3:]), AXES, 0, 0)  7.3 us
    pallas_call x1, Pallas kernels, encode(): pl.pallas_call(functools.partial(encode_kernel, nd, nh, slab, strip), out...  6.95 us
    all_to_all x1, waiting for transfers between devices, gathered(): lax.all_to_all(sent.reshape((depth * height,) + sent.shape[3:]), AXES, 0, 0)  6.44 us
    pallas_call x1, Pallas kernels, moments(): pl.pallas_call(functools.partial(moments_kernel, nd, nh, slab, strip), ou...  4.02 us
    all_to_all x1, starting transfers between devices, local(): sums = lax.all_to_all(sums, AXES, 0, 0)  2.77 us
    reshape x3, local copies, waits for them, and re-layouts, parameters(): conv_two.reshape(3, 3, 3, 64, 64).transpose(2, 4, 0, 1, 3).reshape(192, 576)  1.65 us
  transfers between devices with their start and end apart: 4, of which 2 were waited for; matrix products, arithmetic and copies ran while one was open for 8% of the time, Pallas kernels for 22%

profile of v5, /device:TPU:0, one launch (start us, length us, event | category | flops | bytes accessed | tf_op | source)
XLA Modules:
  0.0 63.2 jit_solution(8836713343521345497)
XLA Ops:
  0.0 0.0 copy-start.3
  0.0 0.9 %abs_reduce_fusion = f32[2]{0:T(128)S(1)} fusion(f32[1,32,128]{2,1,0:T(8,128)} %bitcast.37, f32[1,32,128]{2,1,0:T(8,128)} %bitcast.39), kind=kLoop, calls=%fused_computation.7 | loop fusion | flops 24574 | bytes 32776 | tf_op jit(solution)/shard_map/reduce_max | solution.py:678
  0.9 0.8 %fusion = f32[2,32,128]{2,1,0:T(8,128)S(1)} fusion(f32[1,32,128]{2,1,0:T(8,128)} %bitcast.38, f32[1,32,128]{2,1,0:T(8,128)} %bitcast.40, f32[2]{0:T(128)S(1)} %get-tuple-element.13), kind=kLoop, calls=%fused_computation.8 | loop fusion | flops 16384 | bytes 65544 | tf_op jit(solution)/shard_map/mul | solution.py:679
  1.7 0.1 select_convert_fusion
  1.8 0.8 %broadcast_in_dim.22 = f16[2,2,8,40,128]{4,3,2,1,0:T(8,128)(2,1)} broadcast(f16[2,40,128]{2,1,0:T(8,128)(2,1)S(1)} %select_convert_fusion), dimensions={1,3,4} | broadcast | bytes 348160 | tf_op jit(solution)/shard_map/broadcast_in_dim | solution.py:682
  2.6 7.3 %all-to-all-start = ((f16[32,40,128]{2,1,0:T(8,128)(2,1)}), f16[32,40,128]{2,1,0:T(8,128)(2,1)S(1)}, u32[]{:S(2)}, u32[]{:S(2)}) async-start(f16[32,40,128]{2,1,0:T(8,128)(2,1)} %bitcast.2), calls=%async_computation | async-start | bytes 655360 | tf_op jit(solution)/shard_map/all_to_all | solution.py:683
  9.9 0.8 %reduce = f32[64,3,3,3]{0,3,2,1:T(4,128)S(1)} reduce(f32[64,1,3,3,3]{0,1,4,3,2:T(1,128)} %param.12, f32[]{:T(128)} %constant.56), dimensions={1}, to_apply=%param.12.reduce_sub_computation | reduce | bytes 13828 | tf_op args[2]
  10.7 0.0 copy-start.5
  10.7 0.0 copy-start.6
  10.7 0.0 copy-start.2
  10.8 0.1 copy.14
  10.8 0.8 %copy.25 = f32[64,1,3,3,3]{0,3,4,2,1:T(4,128)S(1)} copy(f32[64,1,3,3,3]{0,1,4,3,2:T(1,128)} %param.12) | data formatting | bytes 13824 | tf_op jit(solution)/shard_map/transpose | solution.py:410
  11.7 0.0 copy-done.3
  11.7 0.0 copy-start.7
  11.7 0.0 copy-start.8
  11.7 0.4 reshape.51
  12.1 0.8 %copy.19 = bf16[3,3,3,64,64]{3,1,0,4,2:T(4,128)(2,1)S(1)} copy(bf16[3,3,3,64,64]{4,3,2,1,0:T(8,128)(2,1)S(1)} %reshape.51) | data formatting | bytes 442368 | tf_op jit(solution)/shard_map/reshape | solution.py:416
  13.0 0.4 reshape.52.two_ref
  13.4 0.1 copy.16
  13.5 0.1 pad.28.clone
  13.6 0.1 pad.13.clone
  14.3 0.0 copy-done.5
  14.3 0.0 copy-done.6
  14.3 0.1 maximum_bitcast_fusion
  14.4 0.0 copy-done.2
  14.4 0.8 %fusion.5 = f32[64,256]{1,0:T(8,128)S(1)} fusion(f32[64,729]{0,1:T(8,128)S(1)} %mul.65, f32[729,256]{1,0:T(8,128)S(1)} %copy-done.2), kind=kOutput, calls=%fused_computation.24 | convolution fusion | flops 143327232 | bytes 998656 | tf_op jit(solution)/shard_map/dot_general | solution.py:414
  15.2 0.1 stack.55.place_ref
  15.3 0.0 copy-done.7
  15.3 0.0 copy-done.8
  15.3 0.0 copy-start.1
  15.3 0.1 maximum_bitcast_fusion.2
  15.4 0.0 copy-start
  15.5 0.1 maximum_maximum_fusion.taps_ref
  15.6 6.4 %all-to-all-done = f16[32,40,128]{2,1,0:T(8,128)(2,1)S(1)} async-done(((f16[32,40,128]{2,1,0:T(8,128)(2,1)}), f16[32,40,128]{2,1,0:T(8,128)(2,1)S(1)}, u32[]{:S(2)}, u32[]{:S(2)}) %all-to-all-start) | async-done | bytes 327712 | tf_op jit(solution)/shard_map/all_to_all | solution.py:683
  22.0 0.1 collective-permute-start
  22.1 0.1 convert_multiply_fusion.1.own_ref
  22.2 4.0 %moments.1.mine_ref = f32[128,128]{1,0:T(8,128)S(1)} custom-call(f32[32,32,128]{2,1,0:T(8,128)S(1)} %convert_multiply_fusion.1.own_ref, f32[64,288]{1,0:T(8,128)S(1)} %maximum_maximum_fusion.1.pairs_ref, f32[4,128]{1,0:T(4,128)S(1)} %pad_maximum_fusion.1.par_ref), custom_call_target="tpu_custom_call" | custom-call | flops 1000000000 | bytes 1000000 | tf_op jit(solution)/shard_map/moments/pallas_call | solution.py:181
  26.2 0.0 copy-done
  26.2 0.6 collective-permute-start.1
  26.8 0.0 collective-permute-done
  26.8 0.1 convert_multiply_fusion.other_ref
  26.9 0.8 %collective-permute-done.1.theirs_ref = f32[128,128]{1,0:T(8,128)S(1)} collective-permute-done((f32[128,128]{1,0:T(8,128)S(1)}, f32[128,128]{1,0:T(8,128)S(1)}, u32[]{:S(2)}, u32[]{:S(2)}) %collective-permute-start.1) | collective-permute-done | bytes 65568 | tf_op jit(solution)/shard_map/ppermute | solution.py:702
  27.7 7.0 %encode.1 = (f32[8,2,64,512]{3,2,1,0:T(8,128)}, f32[32,2,128]{2,1,0:T(2,128)}) custom-call(f32[32,32,128]{2,1,0:T(8,128)S(1)} %convert_multiply_fusion.1.own_ref, f32[32,32,128]{2,1,0:T(8,128)S(1)} %convert_multiply_fusion.other_ref, f32[128,128]{1,0:T(8,128)S(1)} %moments.1.mine_ref, f32[128,128]{1,0:T(8,128)S(1)} %collective-permute-done.1.theirs_ref, ...), custom_call_target="tpu_custom_call" | custom-call | tf_op jit(solution)/shard_map/encode/pallas_call | solution.py:311
  34.7 2.8 %all-to-all-start.1 = ((f32[32,2,128]{2,1,0:T(2,128)}), f32[32,2,128]{2,1,0:T(2,128)S(1)}, u32[]{:S(2)}, u32[]{:S(2)}) async-start(f32[32,2,128]{2,1,0:T(2,128)} %get-tuple-element.12), calls=%async_computation.1 | async-start | bytes 65536 | tf_op jit(solution)/shard_map/all_to_all | solution.py:704
  37.4 0.0 copy-done.1
  37.4 9.6 %rim.1 = (f32[6,64,1280]{2,1,0:T(8,128)}, f32[8,64,768]{2,1,0:T(8,128)}) custom-call(f32[32,32,128]{2,1,0:T(8,128)S(1)} %convert_multiply_fusion.1.own_ref, f32[32,32,128]{2,1,0:T(8,128)S(1)} %convert_multiply_fusion.other_ref, f32[128,128]{1,0:T(8,128)S(1)} %moments.1.mine_ref, f32[128,128]{1,0:T(8,128)S(1)} %collective-permute-done.1.theirs_ref, ...), custom_call_target="tpu_custom_call" | custom-call | flops 6000000000 | bytes 10000000 | tf_op jit(solution)/shard_map/rim/pallas_call | solution.py:386
  47.0 0.0 all-to-all-done.1.sums_ref
  47.1 0.0 copy-start.4
  47.1 0.6 copy-done.4
  47.7 15.3 %match.1 = f32[3,8,4,128]{3,2,1,0:T(4,128)} custom-call(f32[6,64,1280]{2,1,0:T(8,128)} %get-tuple-element.9.edge_hbm, f32[8,64,768]{2,1,0:T(8,128)} %get-tuple-element.10.side_hbm, f32[8,2,64,512]{3,2,1,0:T(8,128)} %get-tuple-element.11.raw_hbm, f32[32,2,128]{2,1,0:T(2,128)} %copy-done.4, f32[4,128]{1,0:T(4,128)} %copy-done, s32[7]{0:T(128)} %copy-done.1, ...), custom_call_target="tpu_custom_call" | custom-call | tf_op jit(solution)/shard_map/match/pallas_call | solution.py:649
  (13 shorter events, 0.2 us)
Async XLA Ops:
  0.0 11.7 %copy-start.3 = (bf16[27,4096]{1,0:T(8,128)(2,1)S(1)}, bf16[27,4096]{1,0:T(8,128)(2,1)}, u32[]{:S(2)}) copy-start(bf16[27,4096]{1,0:T(8,128)(2,1)} %param.15) | copy-start | bytes 663556
  2.6 19.4 %all-to-all-start = ((f16[32,40,128]{2,1,0:T(8,128)(2,1)}), f16[32,40,128]{2,1,0:T(8,128)(2,1)S(1)}, u32[]{:S(2)}, u32[]{:S(2)}) async-start(f16[32,40,128]{2,1,0:T(8,128)(2,1)} %bitcast.2), calls=%async_computation | async-start | bytes 655360 | tf_op jit(solution)/shard_map/all_to_all | solution.py:683
  10.7 3.6 %copy-start.5 = (f32[64]{0:T(128)S(1)}, f32[64]{0:T(128)}, u32[]{:S(2)}) copy-start(f32[64]{0:T(128)} %param.13) | copy-start | bytes 772
  10.7 3.6 %copy-start.6 = (f32[64]{0:T(128)S(1)}, f32[64]{0:T(128)}, u32[]{:S(2)}) copy-start(f32[64]{0:T(128)} %param.14) | copy-start | bytes 772
  10.7 3.7 %copy-start.2 = (f32[729,256]{1,0:T(8,128)S(1)}, f32[729,256]{1,0:T(8,128)}, u32[]{:S(2)}) copy-start(f32[729,256]{1,0:T(8,128)} %constant.49.clone) | copy-start | bytes 2239492
  11.7 3.7 %copy-start.7 = (f32[64]{0:T(128)S(1)}, f32[64]{0:T(128)}, u32[]{:S(2)}) copy-start(f32[64]{0:T(128)} %param.16) | copy-start | bytes 772
  11.7 3.6 %copy-start.8 = (f32[64]{0:T(128)S(1)}, f32[64]{0:T(128)}, u32[]{:S(2)}) copy-start(f32[64]{0:T(128)} %param.17) | copy-start | bytes 772
  15.3 22.1 %copy-start.1 = (s32[7]{0:T(128)}, s32[7]{0:T(128)S(1)}, u32[]{:S(2)}) copy-start(s32[7]{0:T(128)S(1)} %stack.55.place_ref) | copy-start | bytes 88
  15.4 10.8 %copy-start = (f32[4,128]{1,0:T(4,128)}, f32[4,128]{1,0:T(4,128)S(1)}, u32[]{:S(2)}) copy-start(f32[4,128]{1,0:T(4,128)S(1)} %pad_maximum_fusion.1.par_ref) | copy-start | bytes 6148
  22.0 4.8 %collective-permute-start = (f16[32,40,128]{2,1,0:T(8,128)(2,1)S(1)}, f16[32,40,128]{2,1,0:T(8,128)(2,1)S(1)}, u32[]{:S(2)}, u32[]{:S(2)}) collective-permute-start(f16[32,40,128]{2,1,0:T(8,128)(2,1)S(1)} %all-to-all-done), channel_id=1, source_target_pairs={{0,8},{8,0},{16,24},{24,16},{1,9},{9,1},{17,25},{25,17},{2,10},{10... | collective-permute-start | bytes 983048 | tf_op jit(solution)/shard_map/ppermute | solution.py:699
  26.2 1.5 %collective-permute-start.1 = (f32[128,128]{1,0:T(8,128)S(1)}, f32[128,128]{1,0:T(8,128)S(1)}, u32[]{:S(2)}, u32[]{:S(2)}) collective-permute-start(f32[128,128]{1,0:T(8,128)S(1)} %moments.1.mine_ref), channel_id=1, source_target_pairs={{0,8},{8,0},{16,24},{24,16},{1,9},{9,1},{17,25},{25,17},{2,10},{10... | collective-permute-start | bytes 196616 | tf_op jit(solution)/shard_map/ppermute | solution.py:702
  34.7 12.4 %all-to-all-start.1 = ((f32[32,2,128]{2,1,0:T(2,128)}), f32[32,2,128]{2,1,0:T(2,128)S(1)}, u32[]{:S(2)}, u32[]{:S(2)}) async-start(f32[32,2,128]{2,1,0:T(2,128)} %get-tuple-element.12), calls=%async_computation.1 | async-start | bytes 65536 | tf_op jit(solution)/shard_map/all_to_all | solution.py:704
  47.1 0.6 copy-start.4
